TPU v7x, 32 devices: a whole 2x2x4 slice. The times are simulated.
32 devices in a mesh: groups: 2 (over y), dp: 8 (over z, x), sub: 2 (over core).
Axes of the slice: x: 2, y: 2, z: 4, core: 2. Of those that a mesh axis runs over, the one named last changes fastest.
Arguments:
- queries: bfloat16 [32, 128, 576], P(('groups', 'dp', 'sub')), parts along dimension 0, may hold values from -100 to 100
- new_latent: bfloat16 [32, 576], P(('groups', 'dp', 'sub')), parts along dimension 0, may hold values from -4 to 4
- cache: bfloat16 [32, 384, 576], P(('groups', 'dp', 'sub')), parts along dimension 0, may hold values from -4 to 4
- lengths: int32 [32], P('groups'), parts along dimension 0, may hold values from 2 to 383
- moves: int32 [4, 3], P('groups'), parts along dimension 0, may hold values from 0 to 15, as said below
- resid: bfloat16 [32, 7168], P(('groups', 'dp', 'sub')), parts along dimension 0, may hold values from -6 to 6
- w_uv: bfloat16 [128, 512, 128], P('dp'), may hold values from -0.25 to 0.25
- w_out: bfloat16 [16384, 7168], P('dp'), may hold values from -0.1875 to 0.1875
- norm_gain: bfloat16 [7168], replicated, may hold values from 0.099609375 to 1.8984375
- w_gate: bfloat16 [7168, 9216], P(None, ('dp', 'sub')), may hold values from -0.0625 to 0.0625
- w_up: bfloat16 [7168, 9216], P(None, ('dp', 'sub')), may hold values from -0.0625 to 0.0625
- w_down: bfloat16 [9216, 7168], P(None, ('dp', 'sub')), may hold values from -0.0625 to 0.0625
Outputs:
- cache_out: bfloat16 [32, 384, 576], P(('groups', 'dp', 'sub')), parts along dimension 0
- spare_out: bfloat16 [32, 192, 576], P(('groups', 'dp', 'sub')), parts along dimension 0
- mixed: bfloat16 [32, 7168], P('groups', ('dp', 'sub')), parts along dimension 0
There are 2 independent parts, one for each index of `groups`. A program takes and returns all parts, laid end to end along the dimension named above; an argument that names none is the same for every part. Nothing has to cross between parts.
Inputs may be any that keep to these rules, and one draw needn't show every extreme that they name: `moves`: each row is (request, source rank, destination rank) with request = source rank * 2 + the request's sub index; rows s * (1) to (s + 1) * 1 - 1 are those of sub index s; a request slot is the source of at most one row and the destination of at most one, never both; every migrated request is longer than 192.
All inputs are finite; a program needn't handle non-finite values.
Results may differ from a plain program's by a relative error of at most 0.0067.
Values may be sent and summed in bfloat16 or wider, within the bound.
No kernel may reach another device: no remote copies, remote signals or barrier semaphores. Data moves between devices by JAX's collectives and lax.ppermute only.
A program may use at most 128 MiB of HBM per device.

v0:
```python
import jax
import jax.numpy as jnp
from jax import lax
from jax.sharding import PartitionSpec as P


def partial_attend(query, keys, live, scale, latent):
    scores = jnp.einsum("hw,pw->hp", query, keys, preferred_element_type=jnp.float32) * scale
    scores = jnp.where(live[None, :], scores, -1e30)
    top = jnp.max(scores, axis=1)
    weights = jnp.where(live[None, :], jnp.exp(scores - top[:, None]), 0.0)
    total = jnp.sum(weights, axis=1)
    acc = jnp.dot(
        weights.astype(jnp.bfloat16), keys[:, :latent], preferred_element_type=jnp.float32
    )
    return (top, total, acc)


def route(spread, partner, present):
    shape = (spread.shape[0],) + (1,) * (spread.ndim - 1)
    picked = jnp.take(spread, partner, axis=0)
    return jnp.where(present.reshape(shape), picked, jnp.zeros((), spread.dtype))


def per_device(
    queries, new_latent, cache, lengths, moves, resid, w_uv, w_out, norm_gain, w_gate, w_up, w_down
):
    n_dp = lax.axis_size("dp")
    n_sub = lax.axis_size("sub")
    rank = lax.axis_index("dp")
    core = lax.axis_index("sub")
    device = rank * n_sub + core
    cap = cache.shape[1]
    half = cap // 2
    width = cache.shape[2]
    heads = queries.shape[1]
    latent = w_uv.shape[1]
    scale = (w_uv.shape[2] + width - latent) ** (-0.5)
    length = lax.dynamic_index_in_dim(lengths, device, 0, keepdims=False)
    positions = jnp.arange(cap, dtype=jnp.int32)
    appended = jnp.where((positions == length)[:, None], new_latent[0][None, :], cache[0])
    moved_req = moves[:, 0]
    sources = moves[:, 1]
    targets = moves[:, 2]
    same_core = moved_req % n_sub == core
    sending = jnp.any(moved_req == device)
    peers = jnp.arange(n_dp, dtype=jnp.int32)
    to_match = same_core[None, :] & (peers[:, None] == targets[None, :])
    from_of = jnp.sum(jnp.where(to_match, sources[None, :], 0), axis=1)
    to_has = jnp.any(to_match, axis=1)
    zero_bf = jnp.zeros((), jnp.bfloat16)
    upper = jnp.where(sending, appended[half:], zero_bf).reshape(n_dp, -1)
    spread = lax.all_to_all(upper, "dp", split_axis=0, concat_axis=0, tiled=True)
    landed = lax.all_to_all(
        route(spread, from_of, to_has), "dp", split_axis=0, concat_axis=0, tiled=True
    )
    spare = landed.reshape(half, width)
    kept = jnp.where(sending & (positions >= half)[:, None], zero_bf, appended)
    top, total, acc = partial_attend(queries[0], appended, positions <= length, scale, latent)
    o_lat = (acc / total[:, None]).astype(jnp.bfloat16)
    owners = lax.all_to_all(
        o_lat.reshape(n_dp, heads // n_dp, latent), "dp", split_axis=0, concat_axis=0, tiled=True
    )
    values = jnp.einsum("rhl,hlv->rhv", owners, w_uv, preferred_element_type=jnp.float32).astype(
        jnp.bfloat16
    )
    values = values.reshape(n_dp, -1)
    cols = w_down.shape[1]
    units = w_gate.shape[1]
    col_start = device * cols
    gain = norm_gain.astype(jnp.float32)
    summed = lax.psum_scatter(
        jnp.dot(values, w_out, preferred_element_type=jnp.float32),
        "dp",
        scatter_dimension=0,
        tiled=True,
    )
    x_rows = (resid.astype(jnp.float32) + summed).astype(jnp.bfloat16)
    piece = lax.all_gather(x_rows, ("dp", "sub"), axis=0, tiled=True)
    xf = piece.astype(jnp.float32)
    normed = (xf * lax.rsqrt(jnp.mean(xf * xf, axis=1, keepdims=True) + 1e-06) * gain).astype(
        jnp.bfloat16
    )
    gate = jnp.dot(normed, w_gate, preferred_element_type=jnp.float32)
    up_part = jnp.dot(normed, w_up, preferred_element_type=jnp.float32)
    hidden_part = (jax.nn.silu(gate) * up_part).astype(jnp.bfloat16)
    own_cols = lax.dynamic_slice_in_dim(piece, col_start, cols, 1)
    joined = jnp.concatenate([hidden_part, own_cols], axis=1)
    hidden = joined[:, :units]
    base = joined[:, units:]
    down = jnp.dot(
        lax.all_gather(hidden, ("dp", "sub"), axis=1, tiled=True),
        w_down,
        preferred_element_type=jnp.float32,
    )
    mixed = (base.astype(jnp.float32) + down).astype(jnp.bfloat16)
    return (kept[None], spare[None], mixed)


def solution(mesh):
    return jax.shard_map(
        per_device,
        mesh=mesh,
        in_specs=(
            P(("groups", "dp", "sub"), None, None),
            P(("groups", "dp", "sub"), None),
            P(("groups", "dp", "sub"), None, None),
            P("groups"),
            P("groups", None),
            P(("groups", "dp", "sub"), None),
            P("dp", None, None),
            P("dp", None),
            P(),
            P(None, ("dp", "sub")),
            P(None, ("dp", "sub")),
            P(None, ("dp", "sub")),
        ),
        out_specs=(
            P(("groups", "dp", "sub"), None, None),
            P(("groups", "dp", "sub"), None, None),
            P("groups", ("dp", "sub")),
        ),
        check_vma=False,
    )
```

profile of v0, /device:TPU:0, one launch (start us, length us, event | category | flops | bytes accessed | tf_op | source)
XLA Modules:
  0.0 191.6 jit_solution(15338085588012755496)
XLA Ops:
  7.2 0.0 copy-start
  7.2 1.4 dynamic_slice.7
  8.6 0.6 iota_compare_fusion
  9.2 0.7 reduce.3
  9.9 1.2 bitcast_select_fusion
  11.1 1.5 fusion.34
  12.6 0.1 fusion.14
  12.8 1.0 fusion
  13.8 7.2 %all-to-all-start.2 = ((bf16[8,16,512]{2,1,0:T(8,128)(2,1)}), bf16[8,16,512]{2,1,0:T(8,128)(2,1)S(1)}, u32[]{:S(2)}, u32[]{:S(2)}) async-start(bf16[8,16,512]{2,1,0:T(8,128)(2,1)} %bitcast.7), calls=%async_computation.2 | async-start | bytes 262144 | tf_op jit(solution)/shard_map/all_to_all | solution.py:61
  21.0 1.0 slice_reduce_fusion.1
  22.0 0.6 fusion.27
  22.7 0.8 slice_select_fusion
  23.5 0.7 fusion.25
  24.1 0.1 fusion.26
  24.2 0.1 select_reduce_fusion
  24.3 1.9 %broadcast_select_fusion.1 = bf16[1,384,576]{1,2,0:T(8,128)(2,1)} fusion(pred[384]{0:T(512)(128)(4,1)S(1)} %fusion.25, bf16[1,384,576]{1,2,0:T(8,128)(2,1)} %param.14, pred[384]{0:T(512)(128)(4,1)S(1)} %get-tuple-element.11, bf16[576]{0:T(1024)(128)(2,1)S(1)} %reduce.3), kind=kLoop, calls=%fused_computation.20 | loop fusion | flops 442368 | bytes 886656 | tf_op jit(solution)/shard_map/jit(_where)/select_n | solution.py:58
  26.3 0.7 convert_element_type.44
  27.0 0.2 copy.31
  27.2 0.3 all_to_all.20
  27.5 0.5 broadcast.197
  28.0 1.9 %reduce.10 = bf16[8,13824]{1,0:T(8,128)(2,1)S(1)} reduce(bf16[8,1,13824]{2,1,0:T(2,128)(2,1)S(1)} %all_to_all.20, bf16[]{:T(256)} %broadcast.197), dimensions={1}, to_apply=%all_to_all.20.reduce_sub_computation | reduce | bytes 442370 | tf_op jit(solution)/shard_map/all_to_all | solution.py:53
  29.9 0.8 reshape.188
  30.7 1.3 dynamic-slice.1
  32.0 6.0 %all-to-all-start = ((bf16[8,2,6912]{2,1,0:T(2,128)(2,1)}), bf16[8,2,6912]{2,1,0:T(2,128)(2,1)S(1)}, u32[]{:S(2)}, u32[]{:S(2)}) async-start(bf16[8,2,6912]{2,1,0:T(2,128)(2,1)} %reshape.188), calls=%async_computation | async-start | bytes 442368 | tf_op jit(solution)/shard_map/all_to_all | solution.py:53
  38.0 0.0 all-reduce.3.cloned.1.call-start
  38.1 12.2 %fusion.10 = f32[8,7168]{1,0:T(8,128)} fusion(bf16[2048,7168]{1,0:T(8,128)(2,1)} %param.19, bf16[16,512,128]{2,1,0:T(8,128)(2,1)S(1)} %copy-done, bf16[8,16,512]{2,1,0:T(8,128)(2,1)S(1)} %all-to-all-done.2), kind=kOutput, calls=%fused_computation.21 | convolution fusion | flops 251674624 | bytes 31817728 | tf_op jit(solution)/shard_map/dot_general | solution.py:73
  50.3 0.0 all-reduce.3.cloned.1.call-update
  50.3 0.2 reshape.189
  50.6 0.7 gather_fusion
  51.2 0.1 fusion.12
  51.3 0.8 reduce.11
  52.1 0.8 reshape.190
  52.9 5.9 %all-to-all-start.1 = ((bf16[8,2,6912]{2,1,0:T(2,128)(2,1)}), bf16[8,2,6912]{2,1,0:T(2,128)(2,1)S(1)}, u32[]{:S(2)}, u32[]{:S(2)}) async-start(bf16[8,2,6912]{2,1,0:T(2,128)(2,1)} %reshape.190), calls=%async_computation.1 | async-start | bytes 442368 | tf_op jit(solution)/shard_map/all_to_all | solution.py:54
  58.8 64.0 %all-reduce.3.cloned.1.call-done = f32[8,7168]{1,0:T(8,128)} async-done(((f32[8,7168]{1,0:T(8,128)}), f32[8,7168]{1,0:T(8,128)}) %all-reduce.3.cloned.1.call-update) | async-done | bytes 229392
  122.8 1.7 fusion.24
  124.5 20.8 %all-gather = bf16[16,1,7168]{2,1,0:T(2,128)(2,1)S(1)} all-gather(bf16[1,1,7168]{2,1,0:T(2,128)(2,1)S(1)} %fusion.24), channel_id=1, replica_groups=mesh['groups'=2,'dp'=8,'sub'=2] {'dp','sub'}, dimensions={0}, use_global_device_ids=true | all-gather | bytes 243712 | tf_op jit(solution)/shard_map/all_gather | solution.py:79
  145.3 0.5 convert_element_type.50
  145.8 0.2 fusion.6
  146.0 5.6 %fusion.32 = f32[16,576]{1,0:T(8,128)S(1)} fusion(bf16[7168,576]{0,1:T(8,128)(2,1)} %param.21, f32[16,1,7168]{2,1,0:T(1,128)S(1)} %convert_element_type.50, f32[7168]{0:T(1024)S(1)} %convert_element_type.44, f32[16]{0:T(128)S(1)} %add_rsqrt_fusion), kind=kOutput, calls=%fused_computation.64 | convolution fusion | flops 132464640 | bytes 8781888 | tf_op jit(solution)/shard_map/dot_general | solution.py:84
  151.5 5.6 %fusion.5 = bf16[1,576,16]{1,2,0:T(8,128)(2,1)S(1)} fusion(bf16[7168,576]{0,1:T(8,128)(2,1)} %param.22, f32[16,576]{1,0:T(8,128)S(1)} %fusion.32, f32[16,1,7168]{2,1,0:T(1,128)S(1)} %convert_element_type.50, f32[7168]{0:T(1024)S(1)} %convert_element_type.44, f32[16]{0:T(128)S(1)} %add_rsqrt_fusion), kind=kOutput, calls=%fused_computation.11 | convolution fusion | flops 132519936 | bytes 8800320 | tf_op jit(solution)/shard_map/dot_general | solution.py:85
  157.1 18.5 %all-gather.1 = bf16[16,576,16]{1,2,0:T(8,128)(2,1)S(1)} all-gather(bf16[1,576,16]{1,2,0:T(8,128)(2,1)S(1)} %fusion.5), channel_id=1, replica_groups=mesh['groups'=2,'dp'=8,'sub'=2] {'dp','sub'}, dimensions={0}, use_global_device_ids=true | all-gather | bytes 313344 | tf_op jit(solution)/shard_map/all_gather | solution.py:92
  175.7 0.1 copy.36
  175.7 0.3 reshape.178
  176.0 0.1 constant_dynamic-slice_fusion
  176.1 6.2 %fusion.4 = bf16[16,448]{1,0:T(8,128)(2,1)} fusion(bf16[9216,16]{0,1:T(8,128)(2,1)S(1)} %reshape.178, bf16[9216,448]{0,1:T(8,128)(2,1)} %param.23, bf16[16,1,448]{2,1,0:T(2,128)(2,1)S(1)} %constant_dynamic-slice_fusion), kind=kOutput, calls=%fused_computation.10 | convolution fusion | flops 132142080 | bytes 8581120 | tf_op jit(solution)/shard_map/dot_general | solution.py:91
  182.3 0.2 reshape.191
  182.5 1.3 reduce.6
  183.8 0.9 broadcast_in_dim_reshape.3
  (11 shorter events, 0.1 us)
Async XLA Ops:
  7.2 30.9 %copy-start = (bf16[16,512,128]{2,1,0:T(8,128)(2,1)S(1)}, bf16[16,512,128]{2,1,0:T(8,128)(2,1)}, u32[]{:S(2)}) copy-start(bf16[16,512,128]{2,1,0:T(8,128)(2,1)} %param.18) | copy-start | bytes 6291460
  13.8 18.2 %all-to-all-start.2 = ((bf16[8,16,512]{2,1,0:T(8,128)(2,1)}), bf16[8,16,512]{2,1,0:T(8,128)(2,1)S(1)}, u32[]{:S(2)}, u32[]{:S(2)}) async-start(bf16[8,16,512]{2,1,0:T(8,128)(2,1)} %bitcast.7), calls=%async_computation.2 | async-start | bytes 262144 | tf_op jit(solution)/shard_map/all_to_all | solution.py:61
  32.0 18.3 %all-to-all-start = ((bf16[8,2,6912]{2,1,0:T(2,128)(2,1)}), bf16[8,2,6912]{2,1,0:T(2,128)(2,1)S(1)}, u32[]{:S(2)}, u32[]{:S(2)}) async-start(bf16[8,2,6912]{2,1,0:T(2,128)(2,1)} %reshape.188), calls=%async_computation | async-start | bytes 442368 | tf_op jit(solution)/shard_map/all_to_all | solution.py:53
  38.0 84.8 %copy-start.1 = (bf16[1,7168]{1,0:T(2,128)(2,1)S(1)}, bf16[1,7168]{1,0:T(2,128)(2,1)}, u32[]{:S(2)}) copy-start(bf16[1,7168]{1,0:T(2,128)(2,1)} %param.17) | copy-start | bytes 43012
  38.0 84.8 %all-reduce.3.cloned.1.call-start = ((), (), s32[]{:S(2)}) async-start(), calls=%async_computation.3 | async-start | bytes 458752
  52.9 129.5 %all-to-all-start.1 = ((bf16[8,2,6912]{2,1,0:T(2,128)(2,1)}), bf16[8,2,6912]{2,1,0:T(2,128)(2,1)S(1)}, u32[]{:S(2)}, u32[]{:S(2)}) async-start(bf16[8,2,6912]{2,1,0:T(2,128)(2,1)} %reshape.190), calls=%async_computation.1 | async-start | bytes 442368 | tf_op jit(solution)/shard_map/all_to_all | solution.py:54
Sparse Core Ops, SparseCore 0:
  50.5 72.2 all-reduce.2
where the time goes:
time: 192 us
  waiting for transfers between devices  64 us (33%)
  blocking collectives  39.3 us (20%)
  matrix products  32.2 us (17%)
  starting transfers between devices  19.2 us (10%)
  between operations  14.2 us (7%)
  other arithmetic  14 us (7%)
  local copies, waits for them, and re-layouts  8.61 us (4%)
    unnamed x2, waiting for transfers between devices  64 us
    all_gather x1, blocking collectives, per_device(): piece = lax.all_gather(x_rows, ('dp', 'sub'), axis=0, tiled=True)  20.8 us
    all_gather x1, blocking collectives, per_device(): lax.all_gather(hidden, ('dp', 'sub'), axis=1, tiled=True)  18.5 us
    dot_general x1, matrix products, per_device(): jnp.dot(values, w_out, preferred_element_type=jnp.float32)  12.2 us
    all_to_all x1, starting transfers between devices, per_device(): lax.all_to_all(o_lat.reshape(n_dp, heads // n_dp, latent), 'dp', split_ax...  7.25 us
    dot_general x1, matrix products, per_device(): jnp.dot(lax.all_gather(hidden, ('dp', 'sub'), axis=1, tiled=True), w_down...  6.23 us
    all_to_all x1, starting transfers between devices, per_device(): lax.all_to_all(upper, 'dp', split_axis=0, concat_axis=0, tiled=True)  6.01 us
    all_to_all x1, starting transfers between devices, per_device(): lax.all_to_all(route(spread, from_of, to_has), 'dp', split_axis=0, concat...  5.94 us
  transfers between devices with their start and end apart: 4, of which 1 were waited for; matrix products, arithmetic and copies ran while one was open for 24% of the time, Pallas kernels for 0%

commit v1 on v0

--- a/solution.py
+++ b/solution.py
@@ -1,6 +1,10 @@
+import functools
+
 import jax
 import jax.numpy as jnp
 from jax import lax
+from jax.experimental import pallas as pl
+from jax.experimental.pallas import tpu as pltpu
 from jax.sharding import PartitionSpec as P
 
 
@@ -22,7 +26,7 @@
     return jnp.where(present.reshape(shape), picked, jnp.zeros((), spread.dtype))
 
 
-def per_device(
+def per_device_any(
     queries, new_latent, cache, lengths, moves, resid, w_uv, w_out, norm_gain, w_gate, w_up, w_down
 ):
     n_dp = lax.axis_size("dp")
@@ -97,6 +101,339 @@
     return (kept[None], spare[None], mixed)
 
 
+VMEM = pl.BlockSpec(memory_space=pltpu.VMEM)
+SMEM = pl.BlockSpec(memory_space=pltpu.SMEM)
+HBM = pl.BlockSpec(memory_space=pl.ANY)
+NT = (((1,), (1,)), ((), ()))
+TN = (((0,), (0,)), ((), ()))
+
+
+def params(mib):
+    return pltpu.CompilerParams(vmem_limit_bytes=mib << 20)
+
+
+def place(n_sub):
+    rank = lax.axis_index("dp")
+    core = lax.axis_index("sub")
+    return jnp.stack([rank, core, rank * n_sub + core]).astype(jnp.int32)
+
+
+def attend_kernel(
+    scale, n_dp, n_sub, at, lengths, moves, q_ref, fresh_ref, cache_ref, kept_ref, out_ref
+):
+    width, cap = cache_ref.shape
+    half = cap // 2
+    latent = 512
+    heads = q_ref.shape[1]
+    device = at[2]
+    length = lengths[device]
+    sending = moves[0, 0] == device
+    for row in range(1, moves.shape[0]):
+        sending = sending | (moves[row, 0] == device)
+    fresh = jnp.broadcast_to(fresh_ref[...].astype(jnp.float32), (128, width)).T
+    fresh = jnp.concatenate([fresh] * (cap // 128), axis=1)
+    positions = lax.broadcasted_iota(jnp.int32, (width, cap), 1)
+    appended = jnp.where(positions == length, fresh, cache_ref[...].astype(jnp.float32))
+    drop = jnp.where(sending, half, cap)
+    kept_ref[...] = jnp.where(positions >= drop, 0.0, appended).astype(jnp.bfloat16)
+    keys = appended.astype(jnp.bfloat16)
+    scores = lax.dot_general(q_ref[...], keys, TN, preferred_element_type=jnp.float32) * scale
+    live = lax.broadcasted_iota(jnp.int32, (heads, cap), 1) <= length
+    scores = jnp.where(live, scores, -1e30)
+    top = jnp.max(scores, axis=1, keepdims=True)
+    weights = jnp.where(live, jnp.exp(scores - top), 0.0)
+    total = jnp.sum(weights, axis=1, keepdims=True)
+    acc = lax.dot_general(
+        weights.astype(jnp.bfloat16), keys[:latent], NT, preferred_element_type=jnp.float32
+    )
+    o_lat = (acc / total).astype(jnp.bfloat16)
+    share = heads // n_dp
+    rows = half // n_dp
+    upper = jnp.where(sending, appended.T[half:], 0.0)
+    for peer in range(n_dp):
+        out_ref[peer, 0:share, 0:latent] = o_lat[peer * share : (peer + 1) * share]
+        out_ref[peer, 0:share, latent:width] = jnp.zeros((share, width - latent), jnp.bfloat16)
+        out_ref[peer, share : share + rows, :] = upper[peer * rows : (peer + 1) * rows].astype(
+            jnp.bfloat16
+        )
+
+
+def values_kernel(got_ref, uv_ref, out_ref, wide):
+    n_dp = got_ref.shape[0]
+    share, latent, vh = uv_ref.shape
+    for src in range(n_dp):
+        for k in range(latent // 128):
+            wide[k, src * share : (src + 1) * share, :] = got_ref[
+                src, 0:share, 128 * k : 128 * (k + 1)
+            ].astype(jnp.float32)
+    for head in range(share):
+        rows = jnp.concatenate(
+            [wide[k, pl.ds(head, n_dp, stride=share), :] for k in range(latent // 128)], axis=1
+        ).astype(jnp.bfloat16)
+        out_ref[:, head * vh : (head + 1) * vh] = jnp.dot(
+            rows, uv_ref[head], preferred_element_type=jnp.float32
+        ).astype(jnp.bfloat16)
+
+
+def interleave(first, second):
+    n = first.shape[0]
+    row = lax.broadcasted_iota(jnp.int32, (2 * n, 2 * n), 0)
+    col = lax.broadcasted_iota(jnp.int32, (2 * n, 2 * n), 1)
+    pick = (col == (row % 2) * n + row // 2).astype(jnp.bfloat16)
+    both = jnp.concatenate([first, second], axis=0)
+    return jnp.dot(pick, both, preferred_element_type=jnp.float32).astype(jnp.bfloat16)
+
+
+def project_kernel(at, own_ref, peer_ref, w_ref, out_ref, weights, sems):
+    chunks = sems.shape[0]
+    n_dp = out_ref.shape[0]
+    per = out_ref.shape[1]
+    half = out_ref.shape[2]
+    wide = half // chunks
+    core = at[1]
+
+    def fetch(i):
+        start = pl.multiple_of(core * half + i * wide, 128)
+        return pltpu.make_async_copy(
+            w_ref.at[:, pl.ds(start, wide)], weights.at[i], sems.at[i]
+        )
+
+    for i in range(chunks):
+        fetch(i).start()
+    own = own_ref[...].astype(jnp.float32)
+    peer = peer_ref[...].astype(jnp.float32)
+    first = jnp.where(core == 0, own, peer).astype(jnp.bfloat16)
+    second = jnp.where(core == 0, peer, own).astype(jnp.bfloat16)
+    values = interleave(first, second)
+    for i in range(chunks):
+        fetch(i).wait()
+        part = jnp.dot(values, weights[i], preferred_element_type=jnp.float32)
+        for dst in range(n_dp):
+            out_ref[dst, :, i * wide : (i + 1) * wide] = part[dst * per : (dst + 1) * per]
+
+
+def sum_kernel(n_sub, at, moves, part_ref, resid_ref, got_ref, out_ref):
+    n_dp, per, half = part_ref.shape
+    rows_at = 16
+    rows = out_ref.shape[1] - rows_at
+    total = resid_ref[...].astype(jnp.float32)
+    for src in range(n_dp):
+        total = total + part_ref[src]
+    x = total.astype(jnp.bfloat16)
+    core = at[1]
+    for dst in range(n_dp):
+        for k in range(half // 512):
+            out_ref[dst, per * k : per * (k + 1), 0:512] = x[:, 512 * k : 512 * (k + 1)]
+        source = jnp.int32(0)
+        found = jnp.int32(0)
+        for row in range(moves.shape[0]):
+            hit = (moves[row, 2] == dst) & (moves[row, 0] % n_sub == core)
+            source = jnp.where(hit, moves[row, 1], source)
+            found = jnp.where(hit, 1, found)
+
+        @pl.when(found == 1)
+        def _():
+            out_ref[dst, rows_at : rows_at + rows, :] = got_ref[source, rows_at : rows_at + rows, :]
+
+        @pl.when(found == 0)
+        def _():
+            out_ref[dst, rows_at : rows_at + rows, :] = jnp.zeros(
+                (rows, out_ref.shape[2]), jnp.bfloat16
+            )
+
+
+def gate_up_kernel(x_ref, gain_ref, gate_ref, up_ref, out_ref, weights, sems):
+    chunks = sems.shape[0] // 2
+    tall = weights.shape[1]
+
+    def fetch(i):
+        ref = gate_ref if i % 2 == 0 else up_ref
+        return pltpu.make_async_copy(
+            ref.at[pl.ds((i // 2) * tall, tall), :], weights.at[i], sems.at[i]
+        )
+
+    for i in range(2 * chunks):
+        fetch(i).start()
+    xf = x_ref[...].astype(jnp.float32)
+    inverse = lax.rsqrt(jnp.mean(xf * xf, axis=1, keepdims=True) + 1e-06)
+    normed = (xf * inverse * gain_ref[...].astype(jnp.float32)).astype(jnp.bfloat16)
+    for i in range(chunks):
+        fetch(2 * i).wait()
+        gate = lax.dot_general(weights[2 * i], normed, NT, preferred_element_type=jnp.float32)
+        fetch(2 * i + 1).wait()
+        up = lax.dot_general(weights[2 * i + 1], normed, NT, preferred_element_type=jnp.float32)
+        out_ref[i * tall : (i + 1) * tall, :] = (gate * jax.nn.sigmoid(gate) * up).astype(
+            jnp.bfloat16
+        )
+
+
+def down_kernel(hidden_ref, down_ref, out_ref, weights, sems):
+    chunks = sems.shape[0]
+    tall = weights.shape[1]
+
+    def fetch(i):
+        return pltpu.make_async_copy(
+            down_ref.at[pl.ds(i * tall, tall), :], weights.at[i], sems.at[i]
+        )
+
+    for i in range(chunks):
+        fetch(i).start()
+    hidden = hidden_ref[...]
+    for i in range(chunks):
+        fetch(i).wait()
+        out_ref[i * tall : (i + 1) * tall, :] = lax.dot_general(
+            weights[i], hidden, NT, preferred_element_type=jnp.float32
+        )
+
+
+def swap(x, n_sub):
+    return lax.ppermute(x, "sub", [(i, (i + 1) % n_sub) for i in range(n_sub)])
+
+
+def exchange(x):
+    return lax.all_to_all(x, "dp", split_axis=0, concat_axis=0, tiled=True)
+
+
+def per_device_fast(
+    queries, new_latent, cache, lengths, moves, resid, w_uv, w_out, norm_gain, w_gate, w_up, w_down
+):
+    n_dp = lax.axis_size("dp")
+    n_sub = lax.axis_size("sub")
+    cap, width = cache.shape[1:]
+    heads = queries.shape[1]
+    share, latent, vh = w_uv.shape
+    half = cap // 2
+    rows = half // n_dp
+    dim = w_out.shape[1]
+    requests = n_dp * n_sub
+    units = w_gate.shape[1]
+    cols = w_down.shape[1]
+    scale = (vh + width - latent) ** (-0.5)
+    bf16, f32 = jnp.bfloat16, jnp.float32
+    at = place(n_sub)
+    core = lax.axis_index("sub")
+
+    kept, sent = pl.pallas_call(
+        functools.partial(attend_kernel, scale, n_dp, n_sub),
+        out_shape=(
+            jax.ShapeDtypeStruct((width, cap), bf16),
+            jax.ShapeDtypeStruct((n_dp, share + rows, width), bf16),
+        ),
+        in_specs=[SMEM] * 3 + [VMEM] * 3,
+        out_specs=(VMEM, VMEM),
+        compiler_params=params(16),
+        name="attend",
+    )(at, lengths, moves, queries[0].T, new_latent, cache[0].T)
+    got = exchange(sent)
+    wide_half = dim // n_sub
+    mine = lax.dynamic_slice_in_dim(resid, core * wide_half, wide_half, 1)
+    other = lax.dynamic_slice_in_dim(resid, (1 - core) * wide_half, wide_half, 1)
+    theirs = swap(other, n_sub)
+    resid_pair = jnp.where(
+        core == 0, jnp.concatenate([mine, theirs]), jnp.concatenate([theirs, mine])
+    )
+    values = pl.pallas_call(
+        values_kernel,
+        out_shape=jax.ShapeDtypeStruct((n_dp, share * vh), bf16),
+        in_specs=[VMEM] * 2,
+        out_specs=VMEM,
+        scratch_shapes=[pltpu.VMEM((latent // 128, n_dp * share, 128), f32)],
+        compiler_params=params(16),
+        name="values",
+    )(got, w_uv)
+    chunks = 4
+    partial = pl.pallas_call(
+        project_kernel,
+        out_shape=jax.ShapeDtypeStruct((n_dp, n_sub, wide_half), f32),
+        in_specs=[SMEM, VMEM, VMEM, HBM],
+        out_specs=VMEM,
+        scratch_shapes=[
+            pltpu.VMEM((chunks, share * vh, wide_half // chunks), bf16),
+            pltpu.SemaphoreType.DMA((chunks,)),
+        ],
+        compiler_params=params(32),
+        name="project",
+    )(at, values, swap(values, n_sub), w_out)
+    summed = exchange(partial)
+    routed = pl.pallas_call(
+        functools.partial(sum_kernel, n_sub),
+        out_shape=jax.ShapeDtypeStruct((n_dp, 16 + rows, width), bf16),
+        in_specs=[SMEM] * 2 + [VMEM] * 3,
+        out_specs=VMEM,
+        compiler_params=params(16),
+        name="sum",
+    )(at, moves, summed, resid_pair, got)
+    landed = exchange(routed)
+    spare = landed[:, 16:, :].reshape(half, width)
+    x_half = (
+        landed[:, : wide_half // 512 * n_sub, :latent]
+        .reshape(n_dp, wide_half // 512, n_sub, 512)
+        .transpose(0, 2, 1, 3)
+        .reshape(requests, wide_half)
+    )
+    x_peer = swap(x_half, n_sub)
+    x = jnp.where(
+        core == 0,
+        jnp.concatenate([x_half, x_peer], axis=1),
+        jnp.concatenate([x_peer, x_half], axis=1),
+    )
+    chunks = 6
+    hidden = pl.pallas_call(
+        gate_up_kernel,
+        out_shape=jax.ShapeDtypeStruct((units, requests), bf16),
+        in_specs=[VMEM, VMEM, HBM, HBM],
+        out_specs=VMEM,
+        scratch_shapes=[
+            pltpu.VMEM((2 * chunks, units // chunks, dim), bf16),
+            pltpu.SemaphoreType.DMA((2 * chunks,)),
+        ],
+        compiler_params=params(40),
+        name="gate_up",
+    )(x, norm_gain[None], w_gate.T, w_up.T)
+    every = exchange(jnp.broadcast_to(hidden.T[None], (n_dp, requests, units)))
+    every_peer = swap(every, n_sub)
+    pair = jnp.where(
+        core == 0,
+        jnp.concatenate([every, every_peer], axis=2),
+        jnp.concatenate([every_peer, every], axis=2),
+    )
+    all_hidden = pair.transpose(1, 0, 2).reshape(requests, n_dp * n_sub * units)
+    chunks = 4
+    down = pl.pallas_call(
+        down_kernel,
+        out_shape=jax.ShapeDtypeStruct((cols, requests), f32),
+        in_specs=[VMEM, HBM],
+        out_specs=VMEM,
+        scratch_shapes=[
+            pltpu.VMEM((chunks, cols // chunks, w_down.shape[0]), bf16),
+            pltpu.SemaphoreType.DMA((chunks,)),
+        ],
+        compiler_params=params(24),
+        name="down",
+    )(all_hidden, w_down.T)
+    base = lax.dynamic_slice_in_dim(x, at[2] * cols, cols, 1)
+    mixed = (base.astype(f32) + down.T).astype(bf16)
+    return (kept.T[None], spare[None], mixed)
+
+
+def per_device(*args):
+    queries, cache, w_uv, w_out = args[0], args[2], args[6], args[7]
+    w_gate, w_down = args[9], args[11]
+    n_dp = lax.axis_size("dp")
+    n_sub = lax.axis_size("sub")
+    fits = (
+        n_sub == 2
+        and n_dp == 8
+        and cache.shape[1] % (2 * 8 * n_dp) == 0
+        and queries.shape[1] // n_dp == 16
+        and w_uv.shape[1] == 512
+        and w_out.shape[1] % (n_sub * 4 * 128) == 0
+        and w_gate.shape[1] % 96 == 0
+        and w_down.shape[1] % 64 == 0
+    )
+    return per_device_fast(*args) if fits else per_device_any(*args)
+
+
 def solution(mesh):
     return jax.shard_map(
         per_device,

time: 192 us -> 111 us (0.58)
  waiting for transfers between devices: 64 us -> 23.3 us
  matrix products: 32.2 us -> 0 us
  Pallas kernels: 0 us -> 28.1 us
  between operations: 14.2 us -> 0.83 us
  blocking collectives: 39.3 us -> 26.1 us
  other arithmetic: 14 us -> 2.11 us
  local copies, waits for them, and re-layouts: 8.61 us -> 18 us
  starting transfers between devices: 19.2 us -> 11.7 us
    unnamed x2 -> x0, waiting for transfers between devices: 64 us -> none
    all_gather x2 -> x0, blocking collectives: 39.3 us -> none  [the longest x1 20.8 us: per_device(): piece = lax.all_gather(x_rows, ('dp', 'sub'), axis=0, tiled=True)]
    dot_general x6 -> x0, matrix products: 32.2 us -> none  [the longest x1 12.2 us: per_device(): jnp.dot(values, w_out, preferred_element_type=jnp.float32)]
    pallas_call x0 -> x6, Pallas kernels: none -> 28.1 us  [the longest x1 11.3 us: per_device_fast(): pl.pallas_call(gate_up_kernel, out_shape=jax.ShapeDtypeStruct((units, req...]
    all_to_all x0 -> x2, blocking collectives: none -> 26.1 us  [exchange(): return lax.all_to_all(x, 'dp', split_axis=0, concat_axis=0, tiled=True)]
    all_to_all x3 -> x2, waiting for transfers between devices: 0.01 us -> 20.7 us  [exchange(): return lax.all_to_all(x, 'dp', split_axis=0, concat_axis=0, tiled=True)]
    unnamed x11 -> x24, local copies, waits for them, and re-layouts: 3.45 us -> 13 us
    all_to_all x3 -> x2, starting transfers between devices: 19.2 us -> 11 us  [exchange(): return lax.all_to_all(x, 'dp', split_axis=0, concat_axis=0, tiled=True)]
  transfers between devices with their start and end apart: 4 -> 6, of which waited for: 1 -> 5; matrix products, arithmetic and copies ran while one was open for 24% -> 1% of each run, Pallas kernels for 0% -> 7%
where the time goes in v1:
time: 111 us; the launch traced here: 110 us
  Pallas kernels  28.1 us (25%)
  blocking collectives  26.1 us (24%)
  waiting for transfers between devices  23.3 us (21%)
  local copies, waits for them, and re-layouts  18 us (16%)
  starting transfers between devices  11.7 us (11%)
  other arithmetic  2.11 us (2%)
    all_to_all x2, blocking collectives, exchange(): return lax.all_to_all(x, 'dp', split_axis=0, concat_axis=0, tiled=True)  26.1 us
    all_to_all x2, waiting for transfers between devices, exchange(): return lax.all_to_all(x, 'dp', split_axis=0, concat_axis=0, tiled=True)  20.7 us
    unnamed x24, local copies, waits for them, and re-layouts  13 us
    pallas_call x1, Pallas kernels, per_device_fast(): pl.pallas_call(gate_up_kernel, out_shape=jax.ShapeDtypeStruct((units, req...  11.3 us
    all_to_all x2, starting transfers between devices, exchange(): return lax.all_to_all(x, 'dp', split_axis=0, concat_axis=0, tiled=True)  11 us
    pallas_call x1, Pallas kernels, per_device_fast(): pl.pallas_call(project_kernel, out_shape=jax.ShapeDtypeStruct((n_dp, n_su...  7.23 us
    pallas_call x1, Pallas kernels, per_device_fast(): pl.pallas_call(down_kernel, out_shape=jax.ShapeDtypeStruct((cols, request...  6.44 us
    ppermute x4, waiting for transfers between devices, swap(): return lax.ppermute(x, 'sub', [(i, (i + 1) % n_sub) for i in range(n_sub)])  2.55 us
  transfers between devices with their start and end apart: 6, of which 5 were waited for; matrix products, arithmetic and copies ran while one was open for 1% of the time, Pallas kernels for 7%

profile of v1, /device:TPU:0, one launch (start us, length us, event | category | flops | bytes accessed | tf_op | source)
XLA Modules:
  0.0 110.1 jit_solution(5362982432712559598)
XLA Ops:
  0.6 0.1 pad_add_fusion.at
  0.7 0.0 copy-start.3
  0.7 1.0 copy-done.3
  1.7 0.0 copy-start.4
  1.7 0.9 copy-done.4
  2.6 0.7 copy-done.5
  3.3 0.7 copy-done.7
  4.0 0.7 copy-done.8
  4.7 2.0 %attend.1 = (bf16[576,384]{1,0:T(8,128)(2,1)}, bf16[8,40,576]{2,1,0:T(8,128)(2,1)}) custom-call(s32[3]{0:T(128)S(1)} %pad_add_fusion.at, s32[16]{0:T(128)S(1)} %copy-done.8, s32[2,3]{1,0:T(2,128)S(1)} %copy-done.5, bf16[576,128]{1,0:T(8,128)(2,1)S(1)} %bitcast.36, bf16[1,576]{1,0:T(2,128)(2,1)S(1)} %copy-done.7, bf16[576,384]{1,0:T(8,128)(2,1)S(1)} %bitcast.35), custom_call_target="tpu_custom_call" | custom-call | tf_op jit(solution)/shard_map/attend/pallas_call | solution.py:316
  6.7 7.4 %all-to-all-start = ((bf16[8,40,576]{2,1,0:T(8,128)(2,1)}), bf16[8,40,576]{2,1,0:T(8,128)(2,1)S(1)}, u32[]{:S(2)}, u32[]{:S(2)}) async-start(bf16[8,40,576]{2,1,0:T(8,128)(2,1)} %get-tuple-element.6), calls=%async_computation | async-start | bytes 819200 | tf_op jit(solution)/shard_map/all_to_all | solution.py:294
  14.0 12.0 %all-to-all-done.got_ref = bf16[8,40,576]{2,1,0:T(8,128)(2,1)S(1)} async-done(((bf16[8,40,576]{2,1,0:T(8,128)(2,1)}), bf16[8,40,576]{2,1,0:T(8,128)(2,1)S(1)}, u32[]{:S(2)}, u32[]{:S(2)}) %all-to-all-start) | async-done | bytes 368672 | tf_op jit(solution)/shard_map/all_to_all | solution.py:294
  26.1 1.6 %copy-done.2 = bf16[16,512,128]{2,1,0:T(8,128)(2,1)S(1)} copy-done((bf16[16,512,128]{2,1,0:T(8,128)(2,1)S(1)}, bf16[16,512,128]{2,1,0:T(8,128)(2,1)}, u32[]{:S(2)}) %copy-start.2) | copy-done | bytes 2097176
  27.7 0.4 values.1.own_ref
  28.1 0.1 collective-permute-start
  28.2 0.0 copy-done.9
  28.2 0.5 collective-permute-start.1
  28.8 0.6 collective-permute-done.peer_ref
  29.3 7.2 %project.1 = f32[8,2,3584]{2,1,0:T(2,128)} custom-call(s32[3]{0:T(128)S(1)} %pad_add_fusion.at, bf16[8,2048]{1,0:T(8,128)(2,1)S(1)} %values.1.own_ref, bf16[8,2048]{1,0:T(8,128)(2,1)S(1)} %collective-permute-done.peer_ref, bf16[2048,7168]{1,0:T(8,128)(2,1)} %w_ref.1), custom_call_target="tpu_custom_call" | custom-call | tf_op jit(solution)/shard_map/project/pallas_call | solution.py:345
  36.6 0.0 copy-start.10
  36.6 3.6 %all-to-all-start.1 = ((f32[8,2,3584]{2,1,0:T(2,128)}), f32[8,2,3584]{2,1,0:T(2,128)S(1)}, u32[]{:S(2)}, u32[]{:S(2)}) async-start(f32[8,2,3584]{2,1,0:T(2,128)} %project.1), calls=%async_computation.1 | async-start | bytes 458752 | tf_op jit(solution)/shard_map/all_to_all | solution.py:294
  40.2 0.0 collective-permute-done.1
  40.3 0.1 broadcast_select_fusion.1.resid_ref
  40.3 8.7 %all-to-all-done.1.part_ref = f32[8,2,3584]{2,1,0:T(2,128)S(1)} async-done(((f32[8,2,3584]{2,1,0:T(2,128)}), f32[8,2,3584]{2,1,0:T(2,128)S(1)}, u32[]{:S(2)}, u32[]{:S(2)}) %all-to-all-start.1) | async-done | bytes 229408 | tf_op jit(solution)/shard_map/all_to_all | solution.py:294
  49.0 0.0 copy-done.6
  49.0 0.7 sum.1
  49.8 15.2 %all_to_all.20 = bf16[8,40,576]{2,1,0:T(8,128)(2,1)S(1)} all-to-all(bf16[8,40,576]{2,1,0:T(8,128)(2,1)S(1)} %sum.1), channel_id=1, replica_groups=mesh['groups'=2,'dp'=8,'sub'=2] {'dp'}, dimensions={0} | all-to-all | bytes 737280 | tf_op jit(solution)/shard_map/all_to_all | solution.py:294
  65.0 0.1 copy.27
  65.1 0.1 copy.28
  65.2 0.1 collective-permute-start.2
  65.3 0.0 copy-done.10
  65.3 1.3 %collective-permute-done.2 = bf16[16,3584]{1,0:T(8,128)(2,1)S(1)} collective-permute-done((bf16[16,3584]{1,0:T(8,128)(2,1)S(1)}, bf16[16,3584]{1,0:T(8,128)(2,1)S(1)}, u32[]{:S(2)}, u32[]{:S(2)}) %collective-permute-start.2) | collective-permute-done | bytes 114720 | tf_op jit(solution)/shard_map/ppermute | solution.py:290
  66.6 1.7 %copy.29 = bf16[16,7168]{0,1:T(8,128)(2,1)} copy(bf16[16,7168]{1,0:T(8,128)(2,1)S(1)} %get-tuple-element.17) | data formatting | bytes 458752 | tf_op jit(solution)/shard_map/concatenate | solution.py:377
  68.3 1.6 %copy.30 = bf16[16,7168]{0,1:T(8,128)(2,1)} copy(bf16[16,7168]{1,0:T(8,128)(2,1)S(1)} %get-tuple-element.16) | data formatting | bytes 458752 | tf_op jit(solution)/shard_map/concatenate | solution.py:378
  69.9 1.7 %broadcast_select_fusion = bf16[16,7168]{0,1:T(8,128)(2,1)S(1)} fusion(bf16[16,7168]{0,1:T(8,128)(2,1)} %copy.29, bf16[16,7168]{0,1:T(8,128)(2,1)} %copy.30, pred[]{:T(512)S(6)} %eq.2), kind=kLoop, calls=%fused_computation | loop fusion | flops 114688 | bytes 688129 | tf_op jit(solution)/shard_map/jit(_where)/select_n | solution.py:375
  71.6 0.7 copy.31.x_ref
  72.3 0.0 copy-start.1
  72.3 3.3 %copy-done.1 = bf16[7168,576]{0,1:T(8,128)(2,1)S(1)} copy-done((bf16[7168,576]{0,1:T(8,128)(2,1)S(1)}, bf16[7168,576]{0,1:T(8,128)(2,1)}, u32[]{:S(2)}) %copy-start.1) | copy-done | bytes 8257560
  75.6 11.3 %gate_up.1 = bf16[576,16]{1,0:T(8,128)(2,1)S(1)} custom-call(bf16[16,7168]{1,0:T(8,128)(2,1)S(1)} %copy.31.x_ref, bf16[1,7168]{1,0:T(2,128)(2,1)S(1)} %broadcast_in_dim.13.gain_ref, bf16[576,7168]{1,0:T(8,128)(2,1)S(1)} %bitcast.32, bf16[576,7168]{1,0:T(8,128)(2,1)} %bitcast.37), custom_call_target="tpu_custom_call" | custom-call | tf_op jit(solution)/shard_map/gate_up/pallas_call | solution.py:381
  86.9 0.1 copy.32
  87.1 10.9 %all_to_all.21 = bf16[8,16,576]{2,1,0:T(8,128)(2,1)S(1)} all-to-all(bf16[8,16,576]{2,1,0:T(8,128)(2,1)S(1)} %broadcast_in_dim.14), channel_id=1, replica_groups=mesh['groups'=2,'dp'=8,'sub'=2] {'dp'}, dimensions={0} | all-to-all | bytes 294912 | tf_op jit(solution)/shard_map/all_to_all | solution.py:294
  97.9 0.0 collective-permute-start.3
  97.9 0.7 slice.8
  98.6 0.7 collective-permute-done.3
  99.3 0.2 fusion
  99.6 0.0 copy-start
  99.6 3.3 %copy-done = bf16[9216,448]{0,1:T(8,128)(2,1)S(1)} copy-done((bf16[9216,448]{0,1:T(8,128)(2,1)S(1)}, bf16[9216,448]{0,1:T(8,128)(2,1)}, u32[]{:S(2)}) %copy-start) | copy-done | bytes 8257560
  102.9 6.4 %down.1 = f32[448,16]{1,0:T(8,128)S(1)} custom-call(bf16[16,9216]{1,0:T(8,128)(2,1)S(1)} %bitcast.33, bf16[448,9216]{1,0:T(8,128)(2,1)S(1)} %bitcast.31), custom_call_target="tpu_custom_call" | custom-call | tf_op jit(solution)/shard_map/down/pallas_call | solution.py:402
  109.4 0.7 copy.34
  (14 shorter events, 0.2 us)
Async XLA Ops:
  0.7 1.0 copy-start.3
  1.7 0.9 copy-start.4
  2.6 0.7 copy-start.5
  3.3 0.7 copy-start.7
  4.0 0.7 copy-start.8
  6.7 21.5 %copy-start.9 = (bf16[1,7168]{1,0:T(2,128)(2,1)S(1)}, bf16[1,7168]{1,0:T(2,128)(2,1)}, u32[]{:S(2)}) copy-start(bf16[1,7168]{1,0:T(2,128)(2,1)} %param.17) | copy-start | bytes 43012
  6.7 19.4 %all-to-all-start = ((bf16[8,40,576]{2,1,0:T(8,128)(2,1)}), bf16[8,40,576]{2,1,0:T(8,128)(2,1)S(1)}, u32[]{:S(2)}, u32[]{:S(2)}) async-start(bf16[8,40,576]{2,1,0:T(8,128)(2,1)} %get-tuple-element.6), calls=%async_computation | async-start | bytes 819200 | tf_op jit(solution)/shard_map/all_to_all | solution.py:294
  26.1 1.6 %copy-start.2 = (bf16[16,512,128]{2,1,0:T(8,128)(2,1)S(1)}, bf16[16,512,128]{2,1,0:T(8,128)(2,1)}, u32[]{:S(2)}) copy-start(bf16[16,512,128]{2,1,0:T(8,128)(2,1)} %uv_ref.1) | copy-start | bytes 6291460
  28.1 1.3 %collective-permute-start = (bf16[8,2048]{1,0:T(8,128)(2,1)S(1)}, bf16[8,2048]{1,0:T(8,128)(2,1)S(1)}, u32[]{:S(2)}, u32[]{:S(2)}) collective-permute-start(bf16[8,2048]{1,0:T(8,128)(2,1)S(1)} %values.1.own_ref), channel_id=1, source_target_pairs={{0,1},{1,0},{2,3},{3,2},{4,5},{5,4},{6,7},{7,6},{8,9},{9,8},{10,11... | collective-permute-start | bytes 98312 | tf_op jit(solution)/shard_map/ppermute | solution.py:290
  28.2 12.0 %collective-permute-start.1 = (bf16[1,3584]{1,0:T(2,128)(2,1)S(1)}, bf16[1,3584]{1,0:T(2,128)(2,1)S(1)}, u32[]{:S(2)}, u32[]{:S(2)}) collective-permute-start(bf16[1,3584]{1,0:T(2,128)(2,1)S(1)} %get-tuple-element.19), channel_id=1, source_target_pairs={{0,1},{1,0},{2,3},{3,2},{4,5},{5,4},{6,7},{7,6},{8,9},{9,8},{10,11... | collective-permute-start | bytes 21512 | tf_op jit(solution)/shard_map/ppermute | solution.py:290
  28.8 20.3 %copy-start.6 = (s32[2,3]{1,0:T(2,128)S(1)}, s32[2,3]{1,0:T(2,128)}, u32[]{:S(2)}) copy-start(s32[2,3]{1,0:T(2,128)} %moves.3) | copy-start | bytes 76
  36.6 28.7 %copy-start.10 = (bf16[7168]{0:T(1024)(128)(2,1)S(1)}, bf16[7168]{0:T(1024)(128)(2,1)}, u32[]{:S(2)}) copy-start(bf16[7168]{0:T(1024)(128)(2,1)} %param.20) | copy-start | bytes 43012
  36.6 12.4 %all-to-all-start.1 = ((f32[8,2,3584]{2,1,0:T(2,128)}), f32[8,2,3584]{2,1,0:T(2,128)S(1)}, u32[]{:S(2)}, u32[]{:S(2)}) async-start(f32[8,2,3584]{2,1,0:T(2,128)} %project.1), calls=%async_computation.1 | async-start | bytes 458752 | tf_op jit(solution)/shard_map/all_to_all | solution.py:294
  65.2 1.4 %collective-permute-start.2 = (bf16[16,3584]{1,0:T(8,128)(2,1)S(1)}, bf16[16,3584]{1,0:T(8,128)(2,1)S(1)}, u32[]{:S(2)}, u32[]{:S(2)}) collective-permute-start(bf16[16,3584]{1,0:T(8,128)(2,1)S(1)} %bitcast.40), channel_id=1, source_target_pairs={{0,1},{1,0},{2,3},{3,2},{4,5},{5,4},{6,7},{7,6},{8,9},{9,8},{10,11... | collective-permute-start | bytes 344072 | tf_op jit(solution)/shard_map/ppermute | solution.py:290
  72.3 3.3 %copy-start.1 = (bf16[7168,576]{0,1:T(8,128)(2,1)S(1)}, bf16[7168,576]{0,1:T(8,128)(2,1)}, u32[]{:S(2)}) copy-start(bf16[7168,576]{0,1:T(8,128)(2,1)} %param.21) | copy-start | bytes 24772612
  97.9 1.4 %collective-permute-start.3 = (bf16[8,16,576]{2,1,0:T(8,128)(2,1)S(1)}, bf16[8,16,576]{2,1,0:T(8,128)(2,1)S(1)}, u32[]{:S(2)}, u32[]{:S(2)}) collective-permute-start(bf16[8,16,576]{2,1,0:T(8,128)(2,1)S(1)} %all_to_all.21), channel_id=1, source_target_pairs={{0,1},{1,0},{2,3},{3,2},{4,5},{5,4},{6,7},{7,6},{8,9},{9,8},{10,11... | collective-permute-start | bytes 442376 | tf_op jit(solution)/shard_map/ppermute | solution.py:290
  99.6 3.3 %copy-start = (bf16[9216,448]{0,1:T(8,128)(2,1)S(1)}, bf16[9216,448]{0,1:T(8,128)(2,1)}, u32[]{:S(2)}) copy-start(bf16[9216,448]{0,1:T(8,128)(2,1)} %param.23) | copy-start | bytes 24772612

commit v2 on v1

--- a/solution.py
+++ b/solution.py
@@ -115,17 +115,16 @@
 def place(n_sub):
     rank = lax.axis_index("dp")
     core = lax.axis_index("sub")
-    return jnp.stack([rank, core, rank * n_sub + core]).astype(jnp.int32)
+    return rank, core, rank * n_sub + core
 
 
 def attend_kernel(
-    scale, n_dp, n_sub, at, lengths, moves, q_ref, fresh_ref, cache_ref, kept_ref, out_ref
+    scale, n_dp, n_sub, latent, lengths, moves, q_ref, fresh_ref, cache_ref, kept_ref, out_ref
 ):
     width, cap = cache_ref.shape
     half = cap // 2
-    latent = 512
     heads = q_ref.shape[1]
-    device = at[2]
+    _, _, device = place(n_sub)
     length = lengths[device]
     sending = moves[0, 0] == device
     for row in range(1, moves.shape[0]):
@@ -184,13 +183,13 @@
     return jnp.dot(pick, both, preferred_element_type=jnp.float32).astype(jnp.bfloat16)
 
 
-def project_kernel(at, own_ref, peer_ref, w_ref, out_ref, weights, sems):
+def project_kernel(n_sub, own_ref, peer_ref, w_ref, out_ref, weights, sems):
     chunks = sems.shape[0]
     n_dp = out_ref.shape[0]
     per = out_ref.shape[1]
     half = out_ref.shape[2]
     wide = half // chunks
-    core = at[1]
+    _, core, _ = place(n_sub)
 
     def fetch(i):
         start = pl.multiple_of(core * half + i * wide, 128)
@@ -212,15 +211,20 @@
             out_ref[dst, :, i * wide : (i + 1) * wide] = part[dst * per : (dst + 1) * per]
 
 
-def sum_kernel(n_sub, at, moves, part_ref, resid_ref, got_ref, out_ref):
+def sum_kernel(n_sub, moves, part_ref, resid_ref, theirs_ref, got_ref, out_ref):
     n_dp, per, half = part_ref.shape
     rows_at = 16
     rows = out_ref.shape[1] - rows_at
-    total = resid_ref[...].astype(jnp.float32)
+    _, core, _ = place(n_sub)
+    mine = resid_ref[...].astype(jnp.float32)
+    theirs = theirs_ref[...].astype(jnp.float32)
+    mine = jnp.where(core == 0, mine[:, :half], mine[:, half:])
+    theirs = jnp.where(core == 0, theirs[:, :half], theirs[:, half:])
+    row = lax.broadcasted_iota(jnp.int32, (per, half), 0)
+    total = jnp.where(row == core, mine, theirs)
     for src in range(n_dp):
         total = total + part_ref[src]
     x = total.astype(jnp.bfloat16)
-    core = at[1]
     for dst in range(n_dp):
         for k in range(half // 512):
             out_ref[dst, per * k : per * (k + 1), 0:512] = x[:, 512 * k : 512 * (k + 1)]
@@ -242,9 +246,30 @@
             )
 
 
-def gate_up_kernel(x_ref, gain_ref, gate_ref, up_ref, out_ref, weights, sems):
+def unpack_kernel(n_sub, got_ref, x_ref, spare_ref):
+    n_dp = got_ref.shape[0]
+    rows = spare_ref.shape[0] // n_dp
+    half = x_ref.shape[1]
+    for k in range(half // 512):
+        x_ref[:, 512 * k : 512 * (k + 1)] = jnp.concatenate(
+            [
+                got_ref[src, n_sub * k : n_sub * (k + 1), 0:512].astype(jnp.float32)
+                for src in range(n_dp)
+            ],
+            axis=0,
+        ).astype(jnp.bfloat16)
+    for src in range(n_dp):
+        spare_ref[src * rows : (src + 1) * rows, :] = got_ref[src, 16 : 16 + rows, :]
+
+
+def gate_up_kernel(
+    n_sub, own_ref, peer_ref, gain_ref, gate_ref, up_ref, out_ref, base_ref, whole, weights, sems
+):
     chunks = sems.shape[0] // 2
     tall = weights.shape[1]
+    half = own_ref.shape[1]
+    cols = base_ref.shape[1]
+    rank, core, _ = place(n_sub)
 
     def fetch(i):
         ref = gate_ref if i % 2 == 0 else up_ref
@@ -254,22 +279,33 @@
 
     for i in range(2 * chunks):
         fetch(i).start()
-    xf = x_ref[...].astype(jnp.float32)
+    own = own_ref[...].astype(jnp.float32)
+    peer = peer_ref[...].astype(jnp.float32)
+    whole[:, :half] = jnp.where(core == 0, own, peer)
+    whole[:, half:] = jnp.where(core == 0, peer, own)
+    xf = whole[...]
     inverse = lax.rsqrt(jnp.mean(xf * xf, axis=1, keepdims=True) + 1e-06)
     normed = (xf * inverse * gain_ref[...].astype(jnp.float32)).astype(jnp.bfloat16)
+    start = pl.multiple_of(rank * n_sub * cols + core * (cols // 128 * 128), 128)
+    near = whole[:, pl.ds(start, cols + 64)]
+    base_ref[...] = jnp.where(core == 0, near[:, :cols], near[:, 64:]).astype(jnp.bfloat16)
+    parts = []
     for i in range(chunks):
         fetch(2 * i).wait()
         gate = lax.dot_general(weights[2 * i], normed, NT, preferred_element_type=jnp.float32)
         fetch(2 * i + 1).wait()
         up = lax.dot_general(weights[2 * i + 1], normed, NT, preferred_element_type=jnp.float32)
-        out_ref[i * tall : (i + 1) * tall, :] = (gate * jax.nn.sigmoid(gate) * up).astype(
-            jnp.bfloat16
-        )
-
-
-def down_kernel(hidden_ref, down_ref, out_ref, weights, sems):
+        parts.append(gate * jax.nn.sigmoid(gate) * up)
+    hidden = jnp.concatenate(parts, axis=0).T.astype(jnp.bfloat16)
+    for dst in range(out_ref.shape[0]):
+        out_ref[dst] = hidden
+
+
+def down_kernel(n_sub, own_ref, peer_ref, base_ref, down_ref, out_ref, hidden, weights, sems):
     chunks = sems.shape[0]
     tall = weights.shape[1]
+    units = own_ref.shape[2]
+    _, core, _ = place(n_sub)
 
     def fetch(i):
         return pltpu.make_async_copy(
@@ -278,12 +314,23 @@
 
     for i in range(chunks):
         fetch(i).start()
-    hidden = hidden_ref[...]
+    for src in range(own_ref.shape[0]):
+        own = own_ref[src].astype(jnp.float32)
+        peer = peer_ref[src].astype(jnp.float32)
+        first = jnp.where(core == 0, own, peer)
+        second = jnp.where(core == 0, peer, own)
+        hidden[:, src * n_sub * units : (src + 1) * n_sub * units] = jnp.concatenate(
+            [first, second], axis=1
+        ).astype(jnp.bfloat16)
+    every = hidden[...]
+    parts = []
     for i in range(chunks):
         fetch(i).wait()
-        out_ref[i * tall : (i + 1) * tall, :] = lax.dot_general(
-            weights[i], hidden, NT, preferred_element_type=jnp.float32
+        parts.append(
+            lax.dot_general(weights[i], every, NT, preferred_element_type=jnp.float32)
         )
+    down = jnp.concatenate(parts, axis=0).T
+    out_ref[...] = (base_ref[...].astype(jnp.float32) + down).astype(jnp.bfloat16)
 
 
 def swap(x, n_sub):
@@ -310,109 +357,96 @@
     cols = w_down.shape[1]
     scale = (vh + width - latent) ** (-0.5)
     bf16, f32 = jnp.bfloat16, jnp.float32
-    at = place(n_sub)
-    core = lax.axis_index("sub")
 
     kept, sent = pl.pallas_call(
-        functools.partial(attend_kernel, scale, n_dp, n_sub),
+        functools.partial(attend_kernel, scale, n_dp, n_sub, latent),
         out_shape=(
             jax.ShapeDtypeStruct((width, cap), bf16),
             jax.ShapeDtypeStruct((n_dp, share + rows, width), bf16),
         ),
-        in_specs=[SMEM] * 3 + [VMEM] * 3,
+        in_specs=[SMEM] * 2 + [VMEM] * 3,
         out_specs=(VMEM, VMEM),
-        compiler_params=params(16),
+        compiler_params=params(60),
         name="attend",
-    )(at, lengths, moves, queries[0].T, new_latent, cache[0].T)
+    )(lengths, moves, queries[0].T, new_latent, cache[0].T)
     got = exchange(sent)
     wide_half = dim // n_sub
-    mine = lax.dynamic_slice_in_dim(resid, core * wide_half, wide_half, 1)
-    other = lax.dynamic_slice_in_dim(resid, (1 - core) * wide_half, wide_half, 1)
-    theirs = swap(other, n_sub)
-    resid_pair = jnp.where(
-        core == 0, jnp.concatenate([mine, theirs]), jnp.concatenate([theirs, mine])
-    )
+    theirs = swap(resid, n_sub)
     values = pl.pallas_call(
         values_kernel,
         out_shape=jax.ShapeDtypeStruct((n_dp, share * vh), bf16),
         in_specs=[VMEM] * 2,
         out_specs=VMEM,
         scratch_shapes=[pltpu.VMEM((latent // 128, n_dp * share, 128), f32)],
-        compiler_params=params(16),
+        compiler_params=params(60),
         name="values",
     )(got, w_uv)
     chunks = 4
     partial = pl.pallas_call(
-        project_kernel,
+        functools.partial(project_kernel, n_sub),
         out_shape=jax.ShapeDtypeStruct((n_dp, n_sub, wide_half), f32),
-        in_specs=[SMEM, VMEM, VMEM, HBM],
+        in_specs=[VMEM, VMEM, HBM],
         out_specs=VMEM,
         scratch_shapes=[
             pltpu.VMEM((chunks, share * vh, wide_half // chunks), bf16),
             pltpu.SemaphoreType.DMA((chunks,)),
         ],
-        compiler_params=params(32),
+        compiler_params=params(60),
         name="project",
-    )(at, values, swap(values, n_sub), w_out)
+    )(values, swap(values, n_sub), w_out)
     summed = exchange(partial)
     routed = pl.pallas_call(
         functools.partial(sum_kernel, n_sub),
         out_shape=jax.ShapeDtypeStruct((n_dp, 16 + rows, width), bf16),
-        in_specs=[SMEM] * 2 + [VMEM] * 3,
+        in_specs=[SMEM] + [VMEM] * 4,
         out_specs=VMEM,
-        compiler_params=params(16),
+        compiler_params=params(60),
         name="sum",
-    )(at, moves, summed, resid_pair, got)
+    )(moves, summed, resid, theirs, got)
     landed = exchange(routed)
-    spare = landed[:, 16:, :].reshape(half, width)
-    x_half = (
-        landed[:, : wide_half // 512 * n_sub, :latent]
-        .reshape(n_dp, wide_half // 512, n_sub, 512)
-        .transpose(0, 2, 1, 3)
-        .reshape(requests, wide_half)
-    )
-    x_peer = swap(x_half, n_sub)
-    x = jnp.where(
-        core == 0,
-        jnp.concatenate([x_half, x_peer], axis=1),
-        jnp.concatenate([x_peer, x_half], axis=1),
-    )
-    chunks = 6
-    hidden = pl.pallas_call(
-        gate_up_kernel,
-        out_shape=jax.ShapeDtypeStruct((units, requests), bf16),
-        in_specs=[VMEM, VMEM, HBM, HBM],
-        out_specs=VMEM,
+    x_half, spare = pl.pallas_call(
+        functools.partial(unpack_kernel, n_sub),
+        out_shape=(
+            jax.ShapeDtypeStruct((requests, wide_half), bf16),
+            jax.ShapeDtypeStruct((half, width), bf16),
+        ),
+        in_specs=[VMEM],
+        out_specs=(VMEM, VMEM),
+        compiler_params=params(60),
+        name="unpack",
+    )(landed)
+    chunks = 3
+    hidden, base = pl.pallas_call(
+        functools.partial(gate_up_kernel, n_sub),
+        out_shape=(
+            jax.ShapeDtypeStruct((n_dp, requests, units), bf16),
+            jax.ShapeDtypeStruct((requests, cols), bf16),
+        ),
+        in_specs=[VMEM] * 3 + [HBM] * 2,
+        out_specs=(VMEM, VMEM),
         scratch_shapes=[
+            pltpu.VMEM((requests, dim), f32),
             pltpu.VMEM((2 * chunks, units // chunks, dim), bf16),
             pltpu.SemaphoreType.DMA((2 * chunks,)),
         ],
-        compiler_params=params(40),
+        compiler_params=params(60),
         name="gate_up",
-    )(x, norm_gain[None], w_gate.T, w_up.T)
-    every = exchange(jnp.broadcast_to(hidden.T[None], (n_dp, requests, units)))
-    every_peer = swap(every, n_sub)
-    pair = jnp.where(
-        core == 0,
-        jnp.concatenate([every, every_peer], axis=2),
-        jnp.concatenate([every_peer, every], axis=2),
-    )
-    all_hidden = pair.transpose(1, 0, 2).reshape(requests, n_dp * n_sub * units)
+    )(x_half, swap(x_half, n_sub), norm_gain[None], w_gate.T, w_up.T)
+    every = exchange(hidden)
     chunks = 4
-    down = pl.pallas_call(
-        down_kernel,
-        out_shape=jax.ShapeDtypeStruct((cols, requests), f32),
-        in_specs=[VMEM, HBM],
+    mixed = pl.pallas_call(
+        functools.partial(down_kernel, n_sub),
+        out_shape=jax.ShapeDtypeStruct((requests, cols), bf16),
+        in_specs=[VMEM] * 3 + [HBM],
         out_specs=VMEM,
         scratch_shapes=[
+            pltpu.VMEM((requests, n_dp * n_sub * units), bf16),
             pltpu.VMEM((chunks, cols // chunks, w_down.shape[0]), bf16),
             pltpu.SemaphoreType.DMA((chunks,)),
         ],
-        compiler_params=params(24),
+        compiler_params=params(60),
         name="down",
-    )(all_hidden, w_down.T)
-    base = lax.dynamic_slice_in_dim(x, at[2] * cols, cols, 1)
-    mixed = (base.astype(f32) + down.T).astype(bf16)
+    )(every, swap(every, n_sub), base, w_down.T)
     return (kept.T[None], spare[None], mixed)
 
 

time: 111 us -> 105 us (0.946)
  blocking collectives: 26.1 us -> 47 us
  local copies, waits for them, and re-layouts: 18 us -> 3.23 us
  waiting for transfers between devices: 23.3 us -> 12.4 us
  Pallas kernels: 28.1 us -> 37.5 us
  starting transfers between devices: 11.7 us -> 3.65 us
  other arithmetic: 2.11 us -> 0 us
    all_to_all x2 -> x3, blocking collectives: 26.1 us -> 47 us  [exchange(): return lax.all_to_all(x, 'dp', split_axis=0, concat_axis=0, tiled=True)]
    all_to_all x2 -> x1, waiting for transfers between devices: 20.7 us -> 7.7 us  [exchange(): return lax.all_to_all(x, 'dp', split_axis=0, concat_axis=0, tiled=True)]
    unnamed x24 -> x16, local copies, waits for them, and re-layouts: 13 us -> 2.6 us
    all_to_all x2 -> x1, starting transfers between devices: 11 us -> 3.41 us  [exchange(): return lax.all_to_all(x, 'dp', split_axis=0, concat_axis=0, tiled=True)]
    pallas_call x4 -> x5, Pallas kernels: 26.9 us -> 32.5 us  [the longest x1 12.7 us: per_device_fast(): pl.pallas_call(functools.partial(gate_up_kernel, n_sub), out_shape=(jax.S...]
    concatenate x2 -> x0, local copies, waits for them, and re-layouts: 3.24 us -> none  [the longest x1 1.65 us: per_device_fast(): jnp.concatenate([x_half, x_peer], axis=1)]
    pallas_call x1, Pallas kernels: 0.42 us -> 2.77 us  [per_device_fast(): pl.pallas_call(values_kernel, out_shape=jax.ShapeDtypeStruct((n_dp, share...]
    ppermute x4, waiting for transfers between devices: 2.55 us -> 4.75 us  [swap(): return lax.ppermute(x, 'sub', [(i, (i + 1) % n_sub) for i in range(n_sub)])]
  transfers between devices with their start and end apart: 6 -> 5, of which waited for: 5 -> 5; matrix products, arithmetic and copies ran while one was open for 1% -> 1% of each run, Pallas kernels for 7% -> 0%
where the time goes in v2:
time: 105 us; the launch traced here: 104 us
  blocking collectives  47 us (45%)
  Pallas kernels  37.5 us (36%)
  waiting for transfers between devices  12.4 us (12%)
  starting transfers between devices  3.65 us (3%)
  local copies, waits for them, and re-layouts  3.23 us (3%)
    all_to_all x3, blocking collectives, exchange(): return lax.all_to_all(x, 'dp', split_axis=0, concat_axis=0, tiled=True)  47 us
    pallas_call x1, Pallas kernels, per_device_fast(): pl.pallas_call(functools.partial(gate_up_kernel, n_sub), out_shape=(jax.S...  12.7 us
    pallas_call x1, Pallas kernels, per_device_fast(): pl.pallas_call(functools.partial(down_kernel, n_sub), out_shape=jax.Shape...  7.99 us
    all_to_all x1, waiting for transfers between devices, exchange(): return lax.all_to_all(x, 'dp', split_axis=0, concat_axis=0, tiled=True)  7.7 us
    pallas_call x1, Pallas kernels, per_device_fast(): pl.pallas_call(functools.partial(project_kernel, n_sub), out_shape=jax.Sh...  7.46 us
    ppermute x4, waiting for transfers between devices, swap(): return lax.ppermute(x, 'sub', [(i, (i + 1) % n_sub) for i in range(n_sub)])  4.75 us
    all_to_all x1, starting transfers between devices, exchange(): return lax.all_to_all(x, 'dp', split_axis=0, concat_axis=0, tiled=True)  3.41 us
    pallas_call x1, Pallas kernels, per_device_fast(): pl.pallas_call(values_kernel, out_shape=jax.ShapeDtypeStruct((n_dp, share...  2.77 us
  transfers between devices with their start and end apart: 5, of which 5 were waited for; matrix products, arithmetic and copies ran while one was open for 1% of the time, Pallas kernels for 0%

profile of v2, /device:TPU:0, one launch (start us, length us, event | category | flops | bytes accessed | tf_op | source)
XLA Modules:
  0.0 104.5 jit_solution(10176192425796016437)
XLA Ops:
  0.6 2.5 %attend.1 = (bf16[576,384]{1,0:T(8,128)(2,1)}, bf16[8,40,576]{2,1,0:T(8,128)(2,1)}) custom-call(s32[16]{0:T(128)} %lengths.1, s32[2,3]{1,0:T(2,128)} %moves.3, bf16[576,128]{1,0:T(8,128)(2,1)} %bitcast.17, bf16[1,576]{1,0:T(2,128)(2,1)} %fresh_ref.1, bf16[576,384]{1,0:T(8,128)(2,1)} %bitcast.16), custom_call_target="tpu_custom_call" | custom-call | tf_op jit(solution)/shard_map/attend/pallas_call | solution.py:361
  3.2 19.7 %all_to_all.20.got_ref = bf16[8,40,576]{2,1,0:T(8,128)(2,1)} all-to-all(bf16[8,40,576]{2,1,0:T(8,128)(2,1)} %get-tuple-element.10), channel_id=1, replica_groups=mesh['groups'=2,'dp'=8,'sub'=2] {'dp'}, dimensions={0} | all-to-all | bytes 737280 | tf_op jit(solution)/shard_map/all_to_all | solution.py:341
  22.9 2.8 %values.1.own_ref = bf16[8,2048]{1,0:T(8,128)(2,1)} custom-call(bf16[8,40,576]{2,1,0:T(8,128)(2,1)} %all_to_all.20.got_ref, bf16[16,512,128]{2,1,0:T(8,128)(2,1)} %uv_ref.1), custom_call_target="tpu_custom_call" | custom-call | tf_op jit(solution)/shard_map/values/pallas_call | solution.py:375
  25.7 0.0 copy-start.5
  25.7 0.0 copy-start.7
  25.7 0.0 collective-permute-start
  25.7 1.4 %collective-permute-done.peer_ref = bf16[8,2048]{1,0:T(8,128)(2,1)S(1)} collective-permute-done((bf16[8,2048]{1,0:T(8,128)(2,1)}, bf16[8,2048]{1,0:T(8,128)(2,1)S(1)}, u32[]{:S(2)}, u32[]{:S(2)}) %collective-permute-start) | collective-permute-done | bytes 32800 | tf_op jit(solution)/shard_map/ppermute | solution.py:337
  27.1 0.0 copy-start.4
  27.1 0.6 copy-done.4
  27.7 7.5 %project.1 = f32[8,2,3584]{2,1,0:T(2,128)} custom-call(bf16[8,2048]{1,0:T(8,128)(2,1)} %values.1.own_ref, bf16[8,2048]{1,0:T(8,128)(2,1)} %copy-done.4, bf16[2048,7168]{1,0:T(8,128)(2,1)} %w_ref.1), custom_call_target="tpu_custom_call" | custom-call | tf_op jit(solution)/shard_map/project/pallas_call | solution.py:385
  35.2 3.4 %all-to-all-start.1 = ((f32[8,2,3584]{2,1,0:T(2,128)}), f32[8,2,3584]{2,1,0:T(2,128)S(1)}, u32[]{:S(2)}, u32[]{:S(2)}) async-start(f32[8,2,3584]{2,1,0:T(2,128)} %project.1), calls=%async_computation.1 | async-start | bytes 458752 | tf_op jit(solution)/shard_map/all_to_all | solution.py:341
  38.6 0.0 copy-done.5
  38.6 0.2 collective-permute-start.1
  38.8 1.0 collective-permute-done.1.theirs_ref
  39.9 0.0 copy-start.6
  39.9 7.7 %all-to-all-done.1.part_ref = f32[8,2,3584]{2,1,0:T(2,128)S(1)} async-done(((f32[8,2,3584]{2,1,0:T(2,128)}), f32[8,2,3584]{2,1,0:T(2,128)S(1)}, u32[]{:S(2)}, u32[]{:S(2)}) %all-to-all-start.1) | async-done | bytes 229408 | tf_op jit(solution)/shard_map/all_to_all | solution.py:341
  47.6 0.0 copy-done.6
  47.6 0.0 copy-start
  47.6 0.7 copy-done
  48.3 2.2 %sum.1 = bf16[8,40,576]{2,1,0:T(8,128)(2,1)} custom-call(s32[2,3]{1,0:T(2,128)} %moves.3, f32[8,2,3584]{2,1,0:T(2,128)} %copy-done, bf16[1,7168]{1,0:T(2,128)(2,1)} %resid_ref.1, bf16[1,7168]{1,0:T(2,128)(2,1)} %copy-done.6, bf16[8,40,576]{2,1,0:T(8,128)(2,1)} %all_to_all.20.got_ref), custom_call_target="tpu_custom_call" | custom-call | tf_op jit(solution)/shard_map/sum/pallas_call | solution.py:398
  50.4 15.9 %all_to_all.21.got_ref = bf16[8,40,576]{2,1,0:T(8,128)(2,1)} all-to-all(bf16[8,40,576]{2,1,0:T(8,128)(2,1)} %sum.1), channel_id=1, replica_groups=mesh['groups'=2,'dp'=8,'sub'=2] {'dp'}, dimensions={0} | all-to-all | bytes 737280 | tf_op jit(solution)/shard_map/all_to_all | solution.py:341
  66.3 1.8 %unpack.1 = (bf16[16,3584]{1,0:T(8,128)(2,1)}, bf16[192,576]{1,0:T(8,128)(2,1)}) custom-call(bf16[8,40,576]{2,1,0:T(8,128)(2,1)} %all_to_all.21.got_ref), custom_call_target="tpu_custom_call" | custom-call | tf_op jit(solution)/shard_map/unpack/pallas_call | solution.py:407
  68.1 0.0 collective-permute-start.2
  68.1 0.0 copy-done.7
  68.1 0.6 broadcast_in_dim.11.gain_ref
  68.8 0.9 collective-permute-done.2.peer_ref
  69.7 0.0 copy-start.3
  69.7 0.6 copy-done.3
  70.3 12.7 %gate_up.1 = (bf16[8,16,576]{2,1,0:T(8,128)(2,1)}, bf16[16,448]{1,0:T(8,128)(2,1)}) custom-call(bf16[16,3584]{1,0:T(8,128)(2,1)} %get-tuple-element.12.own_ref, bf16[16,3584]{1,0:T(8,128)(2,1)} %copy-done.3, bf16[1,7168]{1,0:T(2,128)(2,1)} %broadcast_in_dim.11.gain_ref, bf16[576,7168]{1,0:T(8,128)(2,1)} %bitcast.13, bf16[576,7168]{1,0:T(8,128)(2,1)} %bitcast.14), custom_call_target="tpu_custom_call" | custom-call | tf_op jit(solution)/shard_map/gate_up/pallas_call | solution.py:419
  83.0 11.4 %all_to_all.22.own_ref = bf16[8,16,576]{2,1,0:T(8,128)(2,1)S(1)} all-to-all(bf16[8,16,576]{2,1,0:T(8,128)(2,1)} %get-tuple-element.13), channel_id=1, replica_groups=mesh['groups'=2,'dp'=8,'sub'=2] {'dp'}, dimensions={0} | all-to-all | bytes 294912 | tf_op jit(solution)/shard_map/all_to_all | solution.py:341
  94.4 0.0 copy-start.1
  94.4 0.0 collective-permute-start.3
  94.4 1.4 %collective-permute-done.3.peer_ref = bf16[8,16,576]{2,1,0:T(8,128)(2,1)S(1)} collective-permute-done((bf16[8,16,576]{2,1,0:T(8,128)(2,1)S(1)}, bf16[8,16,576]{2,1,0:T(8,128)(2,1)S(1)}, u32[]{:S(2)}, u32[]{:S(2)}) %collective-permute-start.3) | collective-permute-done | bytes 147488 | tf_op jit(solution)/shard_map/ppermute | solution.py:337
  95.8 0.0 copy-start.2
  95.8 0.0 copy-done.1
  95.8 0.7 copy-done.2
  96.5 8.0 %down.1 = bf16[16,448]{1,0:T(8,128)(2,1)} custom-call(bf16[8,16,576]{2,1,0:T(8,128)(2,1)} %copy-done.1, bf16[8,16,576]{2,1,0:T(8,128)(2,1)} %copy-done.2, bf16[16,448]{1,0:T(8,128)(2,1)} %get-tuple-element.14.base_ref, bf16[448,9216]{1,0:T(8,128)(2,1)} %bitcast.15), custom_call_target="tpu_custom_call" | custom-call | tf_op jit(solution)/shard_map/down/pallas_call | solution.py:437
Async XLA Ops:
  25.7 12.9 %copy-start.5 = (bf16[1,7168]{1,0:T(2,128)(2,1)S(1)}, bf16[1,7168]{1,0:T(2,128)(2,1)}, u32[]{:S(2)}) copy-start(bf16[1,7168]{1,0:T(2,128)(2,1)} %resid_ref.1) | copy-start | bytes 43012
  25.7 42.5 %copy-start.7 = (bf16[7168]{0:T(1024)(128)(2,1)S(1)}, bf16[7168]{0:T(1024)(128)(2,1)}, u32[]{:S(2)}) copy-start(bf16[7168]{0:T(1024)(128)(2,1)} %param.20) | copy-start | bytes 43012
  25.7 1.4 %collective-permute-start = (bf16[8,2048]{1,0:T(8,128)(2,1)}, bf16[8,2048]{1,0:T(8,128)(2,1)S(1)}, u32[]{:S(2)}, u32[]{:S(2)}) collective-permute-start(bf16[8,2048]{1,0:T(8,128)(2,1)} %values.1.own_ref), channel_id=1, source_target_pairs={{0,1},{1,0},{2,3},{3,2},{4,5},{5,4},{6,7},{7,6},{8,9},{9,8},{10,11... | collective-permute-start | bytes 98312 | tf_op jit(solution)/shard_map/ppermute | solution.py:337
  27.1 0.6 copy-start.4
  35.2 12.4 %all-to-all-start.1 = ((f32[8,2,3584]{2,1,0:T(2,128)}), f32[8,2,3584]{2,1,0:T(2,128)S(1)}, u32[]{:S(2)}, u32[]{:S(2)}) async-start(f32[8,2,3584]{2,1,0:T(2,128)} %project.1), calls=%async_computation.1 | async-start | bytes 458752 | tf_op jit(solution)/shard_map/all_to_all | solution.py:341
  38.6 1.3 %collective-permute-start.1 = (bf16[1,7168]{1,0:T(2,128)(2,1)S(1)}, bf16[1,7168]{1,0:T(2,128)(2,1)S(1)}, u32[]{:S(2)}, u32[]{:S(2)}) collective-permute-start(bf16[1,7168]{1,0:T(2,128)(2,1)S(1)} %copy-done.5), channel_id=1, source_target_pairs={{0,1},{1,0},{2,3},{3,2},{4,5},{5,4},{6,7},{7,6},{8,9},{9,8},{10,11... | collective-permute-start | bytes 43016 | tf_op jit(solution)/shard_map/ppermute | solution.py:337
  39.9 7.7 %copy-start.6 = (bf16[1,7168]{1,0:T(2,128)(2,1)}, bf16[1,7168]{1,0:T(2,128)(2,1)S(1)}, u32[]{:S(2)}) copy-start(bf16[1,7168]{1,0:T(2,128)(2,1)S(1)} %collective-permute-done.1.theirs_ref) | copy-start | bytes 43012
  47.6 0.7 copy-start
  68.1 1.5 %collective-permute-start.2 = (bf16[16,3584]{1,0:T(8,128)(2,1)}, bf16[16,3584]{1,0:T(8,128)(2,1)S(1)}, u32[]{:S(2)}, u32[]{:S(2)}) collective-permute-start(bf16[16,3584]{1,0:T(8,128)(2,1)} %get-tuple-element.12.own_ref), channel_id=1, source_target_pairs={{0,1},{1,0},{2,3},{3,2},{4,5},{5,4},{6,7},{7,6},{8,9},{9,8},{10,11... | collective-permute-start | bytes 344072 | tf_op jit(solution)/shard_map/ppermute | solution.py:337
  69.7 0.6 copy-start.3
  94.4 1.4 %copy-start.1 = (bf16[8,16,576]{2,1,0:T(8,128)(2,1)}, bf16[8,16,576]{2,1,0:T(8,128)(2,1)S(1)}, u32[]{:S(2)}) copy-start(bf16[8,16,576]{2,1,0:T(8,128)(2,1)S(1)} %all_to_all.22.own_ref) | copy-start | bytes 442372
  94.4 1.4 %collective-permute-start.3 = (bf16[8,16,576]{2,1,0:T(8,128)(2,1)S(1)}, bf16[8,16,576]{2,1,0:T(8,128)(2,1)S(1)}, u32[]{:S(2)}, u32[]{:S(2)}) collective-permute-start(bf16[8,16,576]{2,1,0:T(8,128)(2,1)S(1)} %all_to_all.22.own_ref), channel_id=1, source_target_pairs={{0,1},{1,0},{2,3},{3,2},{4,5},{5,4},{6,7},{7,6},{8,9},{9,8},{10,11... | collective-permute-start | bytes 442376 | tf_op jit(solution)/shard_map/ppermute | solution.py:337
  95.8 0.7 copy-start.2

commit v3 on v2

--- a/solution.py
+++ b/solution.py
@@ -108,6 +108,10 @@
 TN = (((0,), (0,)), ((), ()))
 
 
+def cost(mib):
+    return pl.CostEstimate(flops=300 * (mib << 20), bytes_accessed=mib << 20, transcendentals=0)
+
+
 def params(mib):
     return pltpu.CompilerParams(vmem_limit_bytes=mib << 20)
 
@@ -118,8 +122,12 @@
     return rank, core, rank * n_sub + core
 
 
+def position_kernel(out_ref):
+    out_ref[...] = lax.broadcasted_iota(jnp.int32, out_ref.shape, 1)
+
+
 def attend_kernel(
-    scale, n_dp, n_sub, latent, lengths, moves, q_ref, fresh_ref, cache_ref, kept_ref, out_ref
+    scale, n_dp, n_sub, latent, lengths, moves, at_ref, q_ref, fresh_ref, cache_ref, kept_ref, out_ref
 ):
     width, cap = cache_ref.shape
     half = cap // 2
@@ -131,13 +139,14 @@
         sending = sending | (moves[row, 0] == device)
     fresh = jnp.broadcast_to(fresh_ref[...].astype(jnp.float32), (128, width)).T
     fresh = jnp.concatenate([fresh] * (cap // 128), axis=1)
-    positions = lax.broadcasted_iota(jnp.int32, (width, cap), 1)
+    positions = at_ref[...]
+    positions = jnp.concatenate([positions] * (width // positions.shape[0]), axis=0)
     appended = jnp.where(positions == length, fresh, cache_ref[...].astype(jnp.float32))
     drop = jnp.where(sending, half, cap)
     kept_ref[...] = jnp.where(positions >= drop, 0.0, appended).astype(jnp.bfloat16)
     keys = appended.astype(jnp.bfloat16)
     scores = lax.dot_general(q_ref[...], keys, TN, preferred_element_type=jnp.float32) * scale
-    live = lax.broadcasted_iota(jnp.int32, (heads, cap), 1) <= length
+    live = positions[:heads] <= length
     scores = jnp.where(live, scores, -1e30)
     top = jnp.max(scores, axis=1, keepdims=True)
     weights = jnp.where(live, jnp.exp(scores - top), 0.0)
@@ -157,7 +166,7 @@
         )
 
 
-def values_kernel(got_ref, uv_ref, out_ref, wide):
+def values_kernel(got_ref, uv_ref, resid_ref, out_ref, wide):
     n_dp = got_ref.shape[0]
     share, latent, vh = uv_ref.shape
     for src in range(n_dp):
@@ -165,6 +174,9 @@
             wide[k, src * share : (src + 1) * share, :] = got_ref[
                 src, 0:share, 128 * k : 128 * (k + 1)
             ].astype(jnp.float32)
+    piece = resid_ref.shape[1] // n_dp
+    for src in range(n_dp):
+        out_ref[src : src + 1, share * vh :] = resid_ref[:, src * piece : (src + 1) * piece]
     for head in range(share):
         rows = jnp.concatenate(
             [wide[k, pl.ds(head, n_dp, stride=share), :] for k in range(latent // 128)], axis=1
@@ -184,10 +196,9 @@
 
 
 def project_kernel(n_sub, own_ref, peer_ref, w_ref, out_ref, weights, sems):
+    n_dp, per, half = out_ref.shape
+    depth = w_ref.shape[0]
     chunks = sems.shape[0]
-    n_dp = out_ref.shape[0]
-    per = out_ref.shape[1]
-    half = out_ref.shape[2]
     wide = half // chunks
     _, core, _ = place(n_sub)
 
@@ -199,8 +210,8 @@
 
     for i in range(chunks):
         fetch(i).start()
-    own = own_ref[...].astype(jnp.float32)
-    peer = peer_ref[...].astype(jnp.float32)
+    own = own_ref[:, :depth].astype(jnp.float32)
+    peer = peer_ref[:, :depth].astype(jnp.float32)
     first = jnp.where(core == 0, own, peer).astype(jnp.bfloat16)
     second = jnp.where(core == 0, peer, own).astype(jnp.bfloat16)
     values = interleave(first, second)
@@ -211,15 +222,21 @@
             out_ref[dst, :, i * wide : (i + 1) * wide] = part[dst * per : (dst + 1) * per]
 
 
-def sum_kernel(n_sub, moves, part_ref, resid_ref, theirs_ref, got_ref, out_ref):
+def sum_kernel(n_sub, moves, part_ref, own_ref, peer_ref, got_ref, out_ref):
     n_dp, per, half = part_ref.shape
     rows_at = 16
     rows = out_ref.shape[1] - rows_at
     _, core, _ = place(n_sub)
-    mine = resid_ref[...].astype(jnp.float32)
-    theirs = theirs_ref[...].astype(jnp.float32)
-    mine = jnp.where(core == 0, mine[:, :half], mine[:, half:])
-    theirs = jnp.where(core == 0, theirs[:, :half], theirs[:, half:])
+    piece = n_sub * half // n_dp
+    at = own_ref.shape[1] - piece
+
+    def row_of(ref):
+        every = ref[:, at:].astype(jnp.float32)
+        near = jnp.where(core == 0, every[: n_dp // 2], every[n_dp // 2 :])
+        return jnp.concatenate([near[i : i + 1] for i in range(n_dp // 2)], axis=1)
+
+    mine = row_of(own_ref)
+    theirs = row_of(peer_ref)
     row = lax.broadcasted_iota(jnp.int32, (per, half), 0)
     total = jnp.where(row == core, mine, theirs)
     for src in range(n_dp):
@@ -263,57 +280,33 @@
 
 
 def gate_up_kernel(
-    n_sub, own_ref, peer_ref, gain_ref, gate_ref, up_ref, out_ref, base_ref, whole, weights, sems
+    n_sub, own_ref, peer_ref, gain_ref, gate_ref, up_ref, out_ref, base_ref, whole
 ):
-    chunks = sems.shape[0] // 2
-    tall = weights.shape[1]
     half = own_ref.shape[1]
     cols = base_ref.shape[1]
     rank, core, _ = place(n_sub)
 
-    def fetch(i):
-        ref = gate_ref if i % 2 == 0 else up_ref
-        return pltpu.make_async_copy(
-            ref.at[pl.ds((i // 2) * tall, tall), :], weights.at[i], sems.at[i]
-        )
-
-    for i in range(2 * chunks):
-        fetch(i).start()
     own = own_ref[...].astype(jnp.float32)
     peer = peer_ref[...].astype(jnp.float32)
     whole[:, :half] = jnp.where(core == 0, own, peer)
     whole[:, half:] = jnp.where(core == 0, peer, own)
     xf = whole[...]
     inverse = lax.rsqrt(jnp.mean(xf * xf, axis=1, keepdims=True) + 1e-06)
-    normed = (xf * inverse * gain_ref[...].astype(jnp.float32)).astype(jnp.bfloat16)
+    normed = (xf * inverse * gain_ref[...].astype(jnp.float32).reshape(1, -1)).astype(jnp.bfloat16)
     start = pl.multiple_of(rank * n_sub * cols + core * (cols // 128 * 128), 128)
     near = whole[:, pl.ds(start, cols + 64)]
     base_ref[...] = jnp.where(core == 0, near[:, :cols], near[:, 64:]).astype(jnp.bfloat16)
-    parts = []
-    for i in range(chunks):
-        fetch(2 * i).wait()
-        gate = lax.dot_general(weights[2 * i], normed, NT, preferred_element_type=jnp.float32)
-        fetch(2 * i + 1).wait()
-        up = lax.dot_general(weights[2 * i + 1], normed, NT, preferred_element_type=jnp.float32)
-        parts.append(gate * jax.nn.sigmoid(gate) * up)
-    hidden = jnp.concatenate(parts, axis=0).T.astype(jnp.bfloat16)
+    gate = lax.dot_general(gate_ref[...], normed, NT, preferred_element_type=jnp.float32)
+    up = lax.dot_general(up_ref[...], normed, NT, preferred_element_type=jnp.float32)
+    hidden = (gate * jax.nn.sigmoid(gate) * up).T.astype(jnp.bfloat16)
     for dst in range(out_ref.shape[0]):
         out_ref[dst] = hidden
 
 
-def down_kernel(n_sub, own_ref, peer_ref, base_ref, down_ref, out_ref, hidden, weights, sems):
-    chunks = sems.shape[0]
-    tall = weights.shape[1]
+def down_kernel(n_sub, own_ref, peer_ref, base_ref, down_ref, out_ref, hidden):
     units = own_ref.shape[2]
     _, core, _ = place(n_sub)
 
-    def fetch(i):
-        return pltpu.make_async_copy(
-            down_ref.at[pl.ds(i * tall, tall), :], weights.at[i], sems.at[i]
-        )
-
-    for i in range(chunks):
-        fetch(i).start()
     for src in range(own_ref.shape[0]):
         own = own_ref[src].astype(jnp.float32)
         peer = peer_ref[src].astype(jnp.float32)
@@ -322,14 +315,9 @@
         hidden[:, src * n_sub * units : (src + 1) * n_sub * units] = jnp.concatenate(
             [first, second], axis=1
         ).astype(jnp.bfloat16)
-    every = hidden[...]
-    parts = []
-    for i in range(chunks):
-        fetch(i).wait()
-        parts.append(
-            lax.dot_general(weights[i], every, NT, preferred_element_type=jnp.float32)
-        )
-    down = jnp.concatenate(parts, axis=0).T
+    down = lax.dot_general(
+        down_ref[...], hidden[...], NT, preferred_element_type=jnp.float32
+    ).T
     out_ref[...] = (base_ref[...].astype(jnp.float32) + down).astype(jnp.bfloat16)
 
 
@@ -358,51 +346,62 @@
     scale = (vh + width - latent) ** (-0.5)
     bf16, f32 = jnp.bfloat16, jnp.float32
 
+    positions = pl.pallas_call(
+        position_kernel,
+        out_shape=jax.ShapeDtypeStruct((8, cap), jnp.int32),
+        out_specs=VMEM,
+        compiler_params=params(8),
+        cost_estimate=cost(40),
+        name="positions",
+    )()
     kept, sent = pl.pallas_call(
         functools.partial(attend_kernel, scale, n_dp, n_sub, latent),
         out_shape=(
             jax.ShapeDtypeStruct((width, cap), bf16),
             jax.ShapeDtypeStruct((n_dp, share + rows, width), bf16),
         ),
-        in_specs=[SMEM] * 2 + [VMEM] * 3,
+        in_specs=[SMEM] * 2 + [VMEM] * 4,
         out_specs=(VMEM, VMEM),
-        compiler_params=params(60),
+        compiler_params=params(8),
+        cost_estimate=cost(24),
         name="attend",
-    )(lengths, moves, queries[0].T, new_latent, cache[0].T)
+    )(lengths, moves, positions, queries[0].T, new_latent, cache[0].T)
     got = exchange(sent)
     wide_half = dim // n_sub
-    theirs = swap(resid, n_sub)
     values = pl.pallas_call(
         values_kernel,
-        out_shape=jax.ShapeDtypeStruct((n_dp, share * vh), bf16),
-        in_specs=[VMEM] * 2,
+        out_shape=jax.ShapeDtypeStruct((n_dp, share * vh + dim // n_dp), bf16),
+        in_specs=[VMEM] * 3,
         out_specs=VMEM,
         scratch_shapes=[pltpu.VMEM((latent // 128, n_dp * share, 128), f32)],
-        compiler_params=params(60),
+        compiler_params=params(8),
+        cost_estimate=cost(1),
         name="values",
-    )(got, w_uv)
-    chunks = 4
+    )(got, w_uv, resid)
+    peer_values = swap(values, n_sub)
     partial = pl.pallas_call(
         functools.partial(project_kernel, n_sub),
         out_shape=jax.ShapeDtypeStruct((n_dp, n_sub, wide_half), f32),
         in_specs=[VMEM, VMEM, HBM],
         out_specs=VMEM,
         scratch_shapes=[
-            pltpu.VMEM((chunks, share * vh, wide_half // chunks), bf16),
-            pltpu.SemaphoreType.DMA((chunks,)),
+            pltpu.VMEM((4, share * vh, wide_half // 4), bf16),
+            pltpu.SemaphoreType.DMA((4,)),
         ],
-        compiler_params=params(60),
+        compiler_params=params(38),
+        cost_estimate=cost(24),
         name="project",
-    )(values, swap(values, n_sub), w_out)
+    )(values, peer_values, w_out)
     summed = exchange(partial)
     routed = pl.pallas_call(
         functools.partial(sum_kernel, n_sub),
         out_shape=jax.ShapeDtypeStruct((n_dp, 16 + rows, width), bf16),
         in_specs=[SMEM] + [VMEM] * 4,
         out_specs=VMEM,
-        compiler_params=params(60),
+        compiler_params=params(8),
+        cost_estimate=cost(64),
         name="sum",
-    )(moves, summed, resid, theirs, got)
+    )(moves, summed, values, peer_values, got)
     landed = exchange(routed)
     x_half, spare = pl.pallas_call(
         functools.partial(unpack_kernel, n_sub),
@@ -412,39 +411,36 @@
         ),
         in_specs=[VMEM],
         out_specs=(VMEM, VMEM),
-        compiler_params=params(60),
+        compiler_params=params(8),
+        cost_estimate=cost(1),
         name="unpack",
     )(landed)
-    chunks = 3
     hidden, base = pl.pallas_call(
         functools.partial(gate_up_kernel, n_sub),
         out_shape=(
             jax.ShapeDtypeStruct((n_dp, requests, units), bf16),
             jax.ShapeDtypeStruct((requests, cols), bf16),
         ),
-        in_specs=[VMEM] * 3 + [HBM] * 2,
+        in_specs=[VMEM] * 5,
         out_specs=(VMEM, VMEM),
         scratch_shapes=[
             pltpu.VMEM((requests, dim), f32),
-            pltpu.VMEM((2 * chunks, units // chunks, dim), bf16),
-            pltpu.SemaphoreType.DMA((2 * chunks,)),
         ],
-        compiler_params=params(60),
+        compiler_params=params(24),
+        cost_estimate=cost(1),
         name="gate_up",
-    )(x_half, swap(x_half, n_sub), norm_gain[None], w_gate.T, w_up.T)
+    )(x_half, swap(x_half, n_sub), norm_gain, w_gate.T, w_up.T)
     every = exchange(hidden)
-    chunks = 4
     mixed = pl.pallas_call(
         functools.partial(down_kernel, n_sub),
         out_shape=jax.ShapeDtypeStruct((requests, cols), bf16),
-        in_specs=[VMEM] * 3 + [HBM],
+        in_specs=[VMEM] * 4,
         out_specs=VMEM,
         scratch_shapes=[
             pltpu.VMEM((requests, n_dp * n_sub * units), bf16),
-            pltpu.VMEM((chunks, cols // chunks, w_down.shape[0]), bf16),
-            pltpu.SemaphoreType.DMA((chunks,)),
         ],
-        compiler_params=params(60),
+        compiler_params=params(16),
+        cost_estimate=cost(1),
         name="down",
     )(every, swap(every, n_sub), base, w_down.T)
     return (kept.T[None], spare[None], mixed)

time: 105 us -> 81.3 us (0.77)
  Pallas kernels: 37.5 us -> 17.3 us
  blocking collectives: 47 us -> 57.9 us
  waiting for transfers between devices: 12.4 us -> 3.93 us
  starting transfers between devices: 3.65 us -> 0.08 us
  local copies, waits for them, and re-layouts: 3.23 us -> 1.07 us
    all_to_all x3 -> x4, blocking collectives: 47 us -> 57.9 us  [exchange(): return lax.all_to_all(x, 'dp', split_axis=0, concat_axis=0, tiled=True)]
    pallas_call x1, Pallas kernels: 12.7 us -> 4.67 us  [per_device_fast(): pl.pallas_call(functools.partial(gate_up_kernel, n_sub), out_shape=(jax.S...]
    all_to_all x1 -> x0, waiting for transfers between devices: 7.7 us -> none  [exchange(): return lax.all_to_all(x, 'dp', split_axis=0, concat_axis=0, tiled=True)]
    pallas_call x1, Pallas kernels: 7.99 us -> 2.95 us  [per_device_fast(): pl.pallas_call(functools.partial(down_kernel, n_sub), out_shape=jax.Shape...]
    all_to_all x1 -> x0, starting transfers between devices: 3.41 us -> none  [exchange(): return lax.all_to_all(x, 'dp', split_axis=0, concat_axis=0, tiled=True)]
    pallas_call x1, Pallas kernels: 2.77 us -> 0.47 us  [per_device_fast(): pl.pallas_call(values_kernel, out_shape=jax.ShapeDtypeStruct((n_dp, share...]
    unnamed x16 -> x28, local copies, waits for them, and re-layouts: 2.6 us -> 1.07 us
    pallas_call x1, Pallas kernels: 2.17 us -> 0.81 us  [per_device_fast(): pl.pallas_call(functools.partial(sum_kernel, n_sub), out_shape=jax.ShapeD...]
  transfers between devices with their start and end apart: 5 -> 3, of which waited for: 5 -> 3; matrix products, arithmetic and copies ran while one was open for 1% -> 0% of each run, Pallas kernels for 0% -> 0%
where the time goes in v3:
time: 81.3 us; the launch traced here: 81 us
  blocking collectives  57.9 us (71%)
  Pallas kernels  17.3 us (21%)
  waiting for transfers between devices  3.93 us (5%)
  local copies, waits for them, and re-layouts  1.07 us (1%)
    all_to_all x4, blocking collectives, exchange(): return lax.all_to_all(x, 'dp', split_axis=0, concat_axis=0, tiled=True)  57.9 us
    pallas_call x1, Pallas kernels, per_device_fast(): pl.pallas_call(functools.partial(project_kernel, n_sub), out_shape=jax.Sh...  6.14 us
    pallas_call x1, Pallas kernels, per_device_fast(): pl.pallas_call(functools.partial(gate_up_kernel, n_sub), out_shape=(jax.S...  4.67 us
    ppermute x3, waiting for transfers between devices, swap(): return lax.ppermute(x, 'sub', [(i, (i + 1) % n_sub) for i in range(n_sub)])  3.93 us
    pallas_call x1, Pallas kernels, per_device_fast(): pl.pallas_call(functools.partial(down_kernel, n_sub), out_shape=jax.Shape...  2.95 us
  transfers between devices with their start and end apart: 3, of which 3 were waited for; matrix products, arithmetic and copies ran while one was open for 0% of the time, Pallas kernels for 0%

profile of v3, /device:TPU:0, one launch (start us, length us, event | category | flops | bytes accessed | tf_op | source)
XLA Modules:
  0.0 81.0 jit_solution(15857190955157569486)
XLA Ops:
  0.6 0.0 copy-start.6
  0.6 0.0 copy-start.7
  0.7 0.0 copy-start.3
  0.7 0.0 copy-start.5
  0.7 0.0 copy-start.4
  0.7 0.6 copy-done.6
  1.3 0.0 copy-done.7
  1.3 0.4 copy-done.3
  1.7 0.0 copy-done.5
  1.7 0.0 copy-done.4
  1.7 0.0 copy-start
  1.7 0.0 copy-start.1
  1.7 1.5 %attend.1 = (bf16[576,384]{1,0:T(8,128)(2,1)}, bf16[8,40,576]{2,1,0:T(8,128)(2,1)S(1)}) custom-call(s32[16]{0:T(128)S(1)} %copy-done.7, s32[2,3]{1,0:T(2,128)S(1)} %copy-done.6, s32[8,384]{1,0:T(8,128)S(1)} %positions.1.at_ref, bf16[576,128]{1,0:T(8,128)(2,1)S(1)} %bitcast.23, bf16[1,576]{1,0:T(2,128)(2,1)S(1)} %copy-done.5, bf16[576,384]{1,0:T(8,128)(2,1)S(1)} %bitcast.22), custom_call_target="tpu_custom_call" | custom-call | flops 7549747200 | bytes 25165824 | tf_op jit(solution)/shard_map/attend/pallas_call | solution.py:357
  3.3 19.4 %all_to_all.20.got_ref = bf16[8,40,576]{2,1,0:T(8,128)(2,1)S(1)} all-to-all(bf16[8,40,576]{2,1,0:T(8,128)(2,1)S(1)} %get-tuple-element.10), channel_id=1, replica_groups=mesh['groups'=2,'dp'=8,'sub'=2] {'dp'}, dimensions={0} | all-to-all | bytes 737280 | tf_op jit(solution)/shard_map/all_to_all | solution.py:329
  22.7 0.0 copy-done
  22.7 0.0 copy-done.1
  22.7 0.5 values.1.own_ref
  23.2 0.1 collective-permute-start
  23.2 1.2 %collective-permute-done.peer_ref = bf16[8,2944]{1,0:T(8,128)(2,1)S(1)} collective-permute-done((bf16[8,2944]{1,0:T(8,128)(2,1)S(1)}, bf16[8,2944]{1,0:T(8,128)(2,1)S(1)}, u32[]{:S(2)}, u32[]{:S(2)}) %collective-permute-start) | collective-permute-done | bytes 47136 | tf_op jit(solution)/shard_map/ppermute | solution.py:325
  24.5 0.0 slice-start
  24.5 0.0 slice-start.2
  24.5 0.0 slice-start.4
  24.5 6.1 %project.1 = f32[8,2,3584]{2,1,0:T(2,128)S(1)} custom-call(bf16[8,2944]{1,0:T(8,128)(2,1)S(1)} %values.1.own_ref, bf16[8,2944]{1,0:T(8,128)(2,1)S(1)} %collective-permute-done.peer_ref, bf16[2048,7168]{1,0:T(8,128)(2,1)} %w_ref.1), custom_call_target="tpu_custom_call" | custom-call | flops 7549747200 | bytes 25165824 | tf_op jit(solution)/shard_map/project/pallas_call | solution.py:382
  30.6 12.1 %all_to_all.21.part_ref = f32[8,2,3584]{2,1,0:T(2,128)S(1)} all-to-all(f32[8,2,3584]{2,1,0:T(2,128)S(1)} %project.1), channel_id=1, replica_groups=mesh['groups'=2,'dp'=8,'sub'=2] {'dp'}, dimensions={0} | all-to-all | bytes 458752 | tf_op jit(solution)/shard_map/all_to_all | solution.py:329
  42.7 0.0 slice-start.1
  42.7 0.0 slice-start.3
  42.7 0.0 copy-start.2
  42.7 0.0 slice-start.5
  42.7 0.8 sum.1
  43.5 15.5 %all_to_all.22.got_ref = bf16[8,40,576]{2,1,0:T(8,128)(2,1)S(1)} all-to-all(bf16[8,40,576]{2,1,0:T(8,128)(2,1)S(1)} %sum.1), channel_id=1, replica_groups=mesh['groups'=2,'dp'=8,'sub'=2] {'dp'}, dimensions={0} | all-to-all | bytes 737280 | tf_op jit(solution)/shard_map/all_to_all | solution.py:329
  59.0 0.7 unpack.1
  59.8 0.0 collective-permute-start.1
  59.8 1.3 %collective-permute-done.1.peer_ref = bf16[16,3584]{1,0:T(8,128)(2,1)S(1)} collective-permute-done((bf16[16,3584]{1,0:T(8,128)(2,1)S(1)}, bf16[16,3584]{1,0:T(8,128)(2,1)S(1)}, u32[]{:S(2)}, u32[]{:S(2)}) %collective-permute-start.1) | collective-permute-done | bytes 114720 | tf_op jit(solution)/shard_map/ppermute | solution.py:325
  61.1 0.0 slice-done
  61.1 0.0 slice-done.2
  61.1 0.0 slice-done.1
  61.1 0.0 slice-done.3
  61.1 0.0 copy-done.2
  61.2 4.7 %gate_up.1 = (bf16[8,16,576]{2,1,0:T(8,128)(2,1)S(1)}, bf16[16,448]{1,0:T(8,128)(2,1)S(1)}) custom-call(bf16[16,3584]{1,0:T(8,128)(2,1)S(1)} %get-tuple-element.12.own_ref, bf16[16,3584]{1,0:T(8,128)(2,1)S(1)} %collective-permute-done.1.peer_ref, bf16[7168]{0:T(1024)(128)(2,1)S(1)} %copy-done.2, bf16[576,7168]{1,0:T(8,128)(2,1)S(1)} %bitcast.15, ...), custom_call_target="tpu_custom_call" | custom-call | flops 314572800 | bytes 1048576 | tf_op jit(solution)/shard_map/gate_up/pallas_call | solution.py:418
  65.8 10.8 %all_to_all.23.own_ref = bf16[8,16,576]{2,1,0:T(8,128)(2,1)S(1)} all-to-all(bf16[8,16,576]{2,1,0:T(8,128)(2,1)S(1)} %get-tuple-element.13), channel_id=1, replica_groups=mesh['groups'=2,'dp'=8,'sub'=2] {'dp'}, dimensions={0} | all-to-all | bytes 294912 | tf_op jit(solution)/shard_map/all_to_all | solution.py:329
  76.7 0.0 collective-permute-start.2
  76.7 1.4 %collective-permute-done.2.peer_ref = bf16[8,16,576]{2,1,0:T(8,128)(2,1)S(1)} collective-permute-done((bf16[8,16,576]{2,1,0:T(8,128)(2,1)S(1)}, bf16[8,16,576]{2,1,0:T(8,128)(2,1)S(1)}, u32[]{:S(2)}, u32[]{:S(2)}) %collective-permute-start.2) | collective-permute-done | bytes 147488 | tf_op jit(solution)/shard_map/ppermute | solution.py:325
  78.1 0.0 slice-done.4
  78.1 0.0 slice-done.5
  78.1 2.9 %down.1 = bf16[16,448]{1,0:T(8,128)(2,1)} custom-call(bf16[8,16,576]{2,1,0:T(8,128)(2,1)S(1)} %all_to_all.23.own_ref, bf16[8,16,576]{2,1,0:T(8,128)(2,1)S(1)} %collective-permute-done.2.peer_ref, bf16[16,448]{1,0:T(8,128)(2,1)S(1)} %get-tuple-element.14.base_ref, bf16[448,9216]{1,0:T(8,128)(2,1)S(1)} %bitcast.21), custom_call_target="tpu_custom_call" | custom-call | flops 314572800 | bytes 1048576 | tf_op jit(solution)/shard_map/down/pallas_call | solution.py:434
  (4 shorter events, 0.0 us)
Async XLA Ops:
  0.6 0.7 copy-start.6
  0.6 0.7 copy-start.7
  0.7 1.0 %copy-start.3 = (bf16[1,384,576]{1,2,0:T(8,128)(2,1)S(1)}, bf16[1,384,576]{1,2,0:T(8,128)(2,1)}, u32[]{:S(2)}) copy-start(bf16[1,384,576]{1,2,0:T(8,128)(2,1)} %param.14) | copy-start | bytes 1327108
  0.7 1.0 %copy-start.5 = (bf16[1,576]{1,0:T(2,128)(2,1)S(1)}, bf16[1,576]{1,0:T(2,128)(2,1)}, u32[]{:S(2)}) copy-start(bf16[1,576]{1,0:T(2,128)(2,1)} %fresh_ref.1) | copy-start | bytes 3460
  0.7 1.1 %copy-start.4 = (bf16[1,128,576]{1,2,0:T(8,128)(2,1)S(1)}, bf16[1,128,576]{1,2,0:T(8,128)(2,1)}, u32[]{:S(2)}) copy-start(bf16[1,128,576]{1,2,0:T(8,128)(2,1)} %param.12) | copy-start | bytes 442372
  1.7 21.0 %copy-start = (bf16[16,512,128]{2,1,0:T(8,128)(2,1)S(1)}, bf16[16,512,128]{2,1,0:T(8,128)(2,1)}, u32[]{:S(2)}) copy-start(bf16[16,512,128]{2,1,0:T(8,128)(2,1)} %uv_ref.1) | copy-start | bytes 6291460
  1.7 21.0 %copy-start.1 = (bf16[1,7168]{1,0:T(2,128)(2,1)S(1)}, bf16[1,7168]{1,0:T(2,128)(2,1)}, u32[]{:S(2)}) copy-start(bf16[1,7168]{1,0:T(2,128)(2,1)} %resid_ref.1) | copy-start | bytes 43012
  23.2 1.3 %collective-permute-start = (bf16[8,2944]{1,0:T(8,128)(2,1)S(1)}, bf16[8,2944]{1,0:T(8,128)(2,1)S(1)}, u32[]{:S(2)}, u32[]{:S(2)}) collective-permute-start(bf16[8,2944]{1,0:T(8,128)(2,1)S(1)} %values.1.own_ref), channel_id=1, source_target_pairs={{0,1},{1,0},{2,3},{3,2},{4,5},{5,4},{6,7},{7,6},{8,9},{9,8},{10,11... | collective-permute-start | bytes 141320 | tf_op jit(solution)/shard_map/ppermute | solution.py:325
  24.5 36.7 %slice-start = ((s8[8257536]{0:T(1024)(128)(4,1)}), s8[4194304]{0:T(1024)(128)(4,1)S(1)}, s32[]{:S(2)}) async-start(s8[8257536]{0:T(1024)(128)(4,1)} %bitcast.13), calls=%async_computation.4 | async-start | bytes 8388608
  24.5 36.7 %slice-start.2 = ((s8[8257536]{0:T(1024)(128)(4,1)}), s8[4194304]{0:T(1024)(128)(4,1)S(1)}, s32[]{:S(2)}) async-start(s8[8257536]{0:T(1024)(128)(4,1)} %bitcast.16), calls=%async_computation.6 | async-start | bytes 8388608
  24.5 53.6 %slice-start.4 = ((s8[8257536]{0:T(1024)(128)(4,1)}), s8[4194304]{0:T(1024)(128)(4,1)S(1)}, s32[]{:S(2)}) async-start(s8[8257536]{0:T(1024)(128)(4,1)} %bitcast.19), calls=%async_computation.8 | async-start | bytes 8388608
  42.7 18.4 %slice-start.1 = ((s8[8257536]{0:T(1024)(128)(4,1)}), s8[4063232]{0:T(1024)(128)(4,1)S(1)}, s32[]{:S(2)}) async-start(s8[8257536]{0:T(1024)(128)(4,1)} %bitcast.13), calls=%async_computation.5 | async-start | bytes 8126464
  42.7 18.4 %slice-start.3 = ((s8[8257536]{0:T(1024)(128)(4,1)}), s8[4063232]{0:T(1024)(128)(4,1)S(1)}, s32[]{:S(2)}) async-start(s8[8257536]{0:T(1024)(128)(4,1)} %bitcast.16), calls=%async_computation.7 | async-start | bytes 8126464
  42.7 18.4 %copy-start.2 = (bf16[7168]{0:T(1024)(128)(2,1)S(1)}, bf16[7168]{0:T(1024)(128)(2,1)}, u32[]{:S(2)}) copy-start(bf16[7168]{0:T(1024)(128)(2,1)} %gain_ref.1) | copy-start | bytes 43012
  42.7 35.4 %slice-start.5 = ((s8[8257536]{0:T(1024)(128)(4,1)}), s8[4063232]{0:T(1024)(128)(4,1)S(1)}, s32[]{:S(2)}) async-start(s8[8257536]{0:T(1024)(128)(4,1)} %bitcast.19), calls=%async_computation.9 | async-start | bytes 8126464
  59.8 1.3 %collective-permute-start.1 = (bf16[16,3584]{1,0:T(8,128)(2,1)S(1)}, bf16[16,3584]{1,0:T(8,128)(2,1)S(1)}, u32[]{:S(2)}, u32[]{:S(2)}) collective-permute-start(bf16[16,3584]{1,0:T(8,128)(2,1)S(1)} %get-tuple-element.12.own_ref), channel_id=1, source_target_pairs={{0,1},{1,0},{2,3},{3,2},{4,5},{5,4},{6,7},{7,6},{8,9},{9,8},{10,11... | collective-permute-start | bytes 344072 | tf_op jit(solution)/shard_map/ppermute | solution.py:325
  76.7 1.4 %collective-permute-start.2 = (bf16[8,16,576]{2,1,0:T(8,128)(2,1)S(1)}, bf16[8,16,576]{2,1,0:T(8,128)(2,1)S(1)}, u32[]{:S(2)}, u32[]{:S(2)}) collective-permute-start(bf16[8,16,576]{2,1,0:T(8,128)(2,1)S(1)} %all_to_all.23.own_ref), channel_id=1, source_target_pairs={{0,1},{1,0},{2,3},{3,2},{4,5},{5,4},{6,7},{7,6},{8,9},{9,8},{10,11... | collective-permute-start | bytes 442376 | tf_op jit(solution)/shard_map/ppermute | solution.py:325

commit v4 on v3

--- a/solution.py
+++ b/solution.py
@@ -196,11 +196,12 @@
 
 
 def project_kernel(n_sub, own_ref, peer_ref, w_ref, out_ref, weights, sems):
-    n_dp, per, half = out_ref.shape
+    requests, half = out_ref.shape
+    n_dp = requests // n_sub
     depth = w_ref.shape[0]
     chunks = sems.shape[0]
     wide = half // chunks
-    _, core, _ = place(n_sub)
+    rank, core, _ = place(n_sub)
 
     def fetch(i):
         start = pl.multiple_of(core * half + i * wide, 128)
@@ -215,72 +216,40 @@
     first = jnp.where(core == 0, own, peer).astype(jnp.bfloat16)
     second = jnp.where(core == 0, peer, own).astype(jnp.bfloat16)
     values = interleave(first, second)
+
+    def resid_of(ref):
+        every = ref[:, depth:].astype(jnp.float32)
+        near = jnp.where(core == 0, every[: n_dp // 2], every[n_dp // 2 :])
+        return jnp.concatenate([near[i : i + 1] for i in range(n_dp // 2)], axis=1)
+
+    mine = resid_of(own_ref)
+    theirs = resid_of(peer_ref)
+    row = lax.broadcasted_iota(jnp.int32, (requests, wide), 0)
     for i in range(chunks):
         fetch(i).wait()
+        span = slice(i * wide, (i + 1) * wide)
         part = jnp.dot(values, weights[i], preferred_element_type=jnp.float32)
-        for dst in range(n_dp):
-            out_ref[dst, :, i * wide : (i + 1) * wide] = part[dst * per : (dst + 1) * per]
-
-
-def sum_kernel(n_sub, moves, part_ref, own_ref, peer_ref, got_ref, out_ref):
-    n_dp, per, half = part_ref.shape
-    rows_at = 16
-    rows = out_ref.shape[1] - rows_at
-    _, core, _ = place(n_sub)
-    piece = n_sub * half // n_dp
-    at = own_ref.shape[1] - piece
-
-    def row_of(ref):
-        every = ref[:, at:].astype(jnp.float32)
-        near = jnp.where(core == 0, every[: n_dp // 2], every[n_dp // 2 :])
-        return jnp.concatenate([near[i : i + 1] for i in range(n_dp // 2)], axis=1)
-
-    mine = row_of(own_ref)
-    theirs = row_of(peer_ref)
-    row = lax.broadcasted_iota(jnp.int32, (per, half), 0)
-    total = jnp.where(row == core, mine, theirs)
+        near = jnp.where(row % n_sub == core, mine[:, span], theirs[:, span])
+        part = part + jnp.where(row // n_sub == rank, near, 0.0)
+        out_ref[:, span] = part.astype(jnp.bfloat16)
+
+
+def add_kernel(a_ref, b_ref, out_ref):
+    out_ref[...] = (a_ref[...].astype(jnp.float32) + b_ref[...].astype(jnp.float32)).astype(
+        jnp.bfloat16
+    )
+
+
+def unpack_kernel(got_ref, hidden_ref, spare_ref):
+    n_dp, share, _ = hidden_ref.shape
+    rows = spare_ref.shape[0] // n_dp
     for src in range(n_dp):
-        total = total + part_ref[src]
-    x = total.astype(jnp.bfloat16)
-    for dst in range(n_dp):
-        for k in range(half // 512):
-            out_ref[dst, per * k : per * (k + 1), 0:512] = x[:, 512 * k : 512 * (k + 1)]
-        source = jnp.int32(0)
-        found = jnp.int32(0)
-        for row in range(moves.shape[0]):
-            hit = (moves[row, 2] == dst) & (moves[row, 0] % n_sub == core)
-            source = jnp.where(hit, moves[row, 1], source)
-            found = jnp.where(hit, 1, found)
-
-        @pl.when(found == 1)
-        def _():
-            out_ref[dst, rows_at : rows_at + rows, :] = got_ref[source, rows_at : rows_at + rows, :]
-
-        @pl.when(found == 0)
-        def _():
-            out_ref[dst, rows_at : rows_at + rows, :] = jnp.zeros(
-                (rows, out_ref.shape[2]), jnp.bfloat16
-            )
-
-
-def unpack_kernel(n_sub, got_ref, x_ref, spare_ref):
-    n_dp = got_ref.shape[0]
-    rows = spare_ref.shape[0] // n_dp
-    half = x_ref.shape[1]
-    for k in range(half // 512):
-        x_ref[:, 512 * k : 512 * (k + 1)] = jnp.concatenate(
-            [
-                got_ref[src, n_sub * k : n_sub * (k + 1), 0:512].astype(jnp.float32)
-                for src in range(n_dp)
-            ],
-            axis=0,
-        ).astype(jnp.bfloat16)
-    for src in range(n_dp):
-        spare_ref[src * rows : (src + 1) * rows, :] = got_ref[src, 16 : 16 + rows, :]
+        hidden_ref[src] = got_ref[src, 0:share, :]
+        spare_ref[src * rows : (src + 1) * rows, :] = got_ref[src, share : share + rows, :]
 
 
 def gate_up_kernel(
-    n_sub, own_ref, peer_ref, gain_ref, gate_ref, up_ref, out_ref, base_ref, whole
+    n_sub, moves, own_ref, peer_ref, gain_ref, got_ref, gate_ref, up_ref, out_ref, base_ref, whole
 ):
     half = own_ref.shape[1]
     cols = base_ref.shape[1]
@@ -299,8 +268,25 @@
     gate = lax.dot_general(gate_ref[...], normed, NT, preferred_element_type=jnp.float32)
     up = lax.dot_general(up_ref[...], normed, NT, preferred_element_type=jnp.float32)
     hidden = (gate * jax.nn.sigmoid(gate) * up).T.astype(jnp.bfloat16)
+    requests = hidden.shape[0]
+    rows = out_ref.shape[1] - requests
+    from_row = got_ref.shape[1] - rows
     for dst in range(out_ref.shape[0]):
-        out_ref[dst] = hidden
+        out_ref[dst, 0:requests, :] = hidden
+        source = jnp.int32(0)
+        found = jnp.int32(0)
+        for row in range(moves.shape[0]):
+            hit = (moves[row, 2] == dst) & (moves[row, 0] % n_sub == core)
+            source = jnp.where(hit, moves[row, 1], source)
+            found = jnp.where(hit, 1, found)
+
+        @pl.when(found == 1)
+        def _():
+            out_ref[dst, requests:, :] = got_ref[source, from_row:, :]
+
+        @pl.when(found == 0)
+        def _():
+            out_ref[dst, requests:, :] = jnp.zeros((rows, out_ref.shape[2]), jnp.bfloat16)
 
 
 def down_kernel(n_sub, own_ref, peer_ref, base_ref, down_ref, out_ref, hidden):
@@ -379,9 +365,9 @@
         name="values",
     )(got, w_uv, resid)
     peer_values = swap(values, n_sub)
-    partial = pl.pallas_call(
+    x_half = pl.pallas_call(
         functools.partial(project_kernel, n_sub),
-        out_shape=jax.ShapeDtypeStruct((n_dp, n_sub, wide_half), f32),
+        out_shape=jax.ShapeDtypeStruct((requests, wide_half), bf16),
         in_specs=[VMEM, VMEM, HBM],
         out_specs=VMEM,
         scratch_shapes=[
@@ -392,21 +378,36 @@
         cost_estimate=cost(24),
         name="project",
     )(values, peer_values, w_out)
-    summed = exchange(partial)
-    routed = pl.pallas_call(
-        functools.partial(sum_kernel, n_sub),
-        out_shape=jax.ShapeDtypeStruct((n_dp, 16 + rows, width), bf16),
-        in_specs=[SMEM] + [VMEM] * 4,
-        out_specs=VMEM,
-        compiler_params=params(8),
-        cost_estimate=cost(64),
-        name="sum",
-    )(moves, summed, values, peer_values, got)
-    landed = exchange(routed)
-    x_half, spare = pl.pallas_call(
-        functools.partial(unpack_kernel, n_sub),
+    step = 1
+    while step < n_dp:
+        other = lax.ppermute(x_half, "dp", [(i, i ^ step) for i in range(n_dp)])
+        x_half = pl.pallas_call(
+            add_kernel,
+            out_shape=jax.ShapeDtypeStruct((requests, wide_half), bf16),
+            in_specs=[VMEM] * 2,
+            out_specs=VMEM,
+            compiler_params=params(8),
+            cost_estimate=cost(24),
+            name="add",
+        )(x_half, other)
+        step *= 2
+    sent, base = pl.pallas_call(
+        functools.partial(gate_up_kernel, n_sub),
         out_shape=(
-            jax.ShapeDtypeStruct((requests, wide_half), bf16),
+            jax.ShapeDtypeStruct((n_dp, requests + rows, units), bf16),
+            jax.ShapeDtypeStruct((requests, cols), bf16),
+        ),
+        in_specs=[SMEM] + [VMEM] * 6,
+        out_specs=(VMEM, VMEM),
+        scratch_shapes=[pltpu.VMEM((requests, dim), f32)],
+        compiler_params=params(24),
+        cost_estimate=cost(24),
+        name="gate_up",
+    )(moves, x_half, swap(x_half, n_sub), norm_gain, got, w_gate.T, w_up.T)
+    every, spare = pl.pallas_call(
+        unpack_kernel,
+        out_shape=(
+            jax.ShapeDtypeStruct((n_dp, requests, units), bf16),
             jax.ShapeDtypeStruct((half, width), bf16),
         ),
         in_specs=[VMEM],
@@ -414,31 +415,13 @@
         compiler_params=params(8),
         cost_estimate=cost(1),
         name="unpack",
-    )(landed)
-    hidden, base = pl.pallas_call(
-        functools.partial(gate_up_kernel, n_sub),
-        out_shape=(
-            jax.ShapeDtypeStruct((n_dp, requests, units), bf16),
-            jax.ShapeDtypeStruct((requests, cols), bf16),
-        ),
-        in_specs=[VMEM] * 5,
-        out_specs=(VMEM, VMEM),
-        scratch_shapes=[
-            pltpu.VMEM((requests, dim), f32),
-        ],
-        compiler_params=params(24),
-        cost_estimate=cost(1),
-        name="gate_up",
-    )(x_half, swap(x_half, n_sub), norm_gain, w_gate.T, w_up.T)
-    every = exchange(hidden)
+    )(exchange(sent))
     mixed = pl.pallas_call(
         functools.partial(down_kernel, n_sub),
         out_shape=jax.ShapeDtypeStruct((requests, cols), bf16),
         in_specs=[VMEM] * 4,
         out_specs=VMEM,
-        scratch_shapes=[
-            pltpu.VMEM((requests, n_dp * n_sub * units), bf16),
-        ],
+        scratch_shapes=[pltpu.VMEM((requests, n_dp * n_sub * units), bf16)],
         compiler_params=params(16),
         cost_estimate=cost(1),
         name="down",
@@ -458,7 +441,7 @@
         and queries.shape[1] // n_dp == 16
         and w_uv.shape[1] == 512
         and w_out.shape[1] % (n_sub * 4 * 128) == 0
-        and w_gate.shape[1] % 96 == 0
+        and w_gate.shape[1] == cache.shape[2]
         and w_down.shape[1] % 64 == 0
     )
     return per_device_fast(*args) if fits else per_device_any(*args)

time: 81.3 us -> 75.2 us (0.925)
  blocking collectives: 57.9 us -> 34.7 us
  waiting for transfers between devices: 3.93 us -> 17.8 us
  starting transfers between devices: 0.08 us -> 3.37 us
    all_to_all x4 -> x2, blocking collectives: 57.9 us -> 34.7 us  [exchange(): return lax.all_to_all(x, 'dp', split_axis=0, concat_axis=0, tiled=True)]
    ppermute x0 -> x3, waiting for transfers between devices: none -> 13.9 us  [per_device_fast(): other = lax.ppermute(x_half, 'dp', [(i, i ^ step) for i in range(n_dp)])]
    ppermute x0 -> x3, starting transfers between devices: none -> 3.22 us  [per_device_fast(): other = lax.ppermute(x_half, 'dp', [(i, i ^ step) for i in range(n_dp)])]
  transfers between devices with their start and end apart: 3 -> 6, of which waited for: 3 -> 6; matrix products, arithmetic and copies ran while one was open for 0% -> 0% of each run, Pallas kernels for 0% -> 0%
where the time goes in v4:
time: 75.2 us; the launch traced here: 75 us
  blocking collectives  34.7 us (46%)
  waiting for transfers between devices  17.8 us (24%)
  Pallas kernels  17.1 us (23%)
  starting transfers between devices  3.37 us (4%)
  local copies, waits for them, and re-layouts  1.09 us (1%)
  between operations  0.81 us (1%)
    all_to_all x2, blocking collectives, exchange(): return lax.all_to_all(x, 'dp', split_axis=0, concat_axis=0, tiled=True)  34.7 us
    ppermute x3, waiting for transfers between devices, per_device_fast(): other = lax.ppermute(x_half, 'dp', [(i, i ^ step) for i in range(n_dp)])  13.9 us
    pallas_call x1, Pallas kernels, per_device_fast(): pl.pallas_call(functools.partial(project_kernel, n_sub), out_shape=jax.Sh...  6 us
    pallas_call x1, Pallas kernels, per_device_fast(): pl.pallas_call(functools.partial(gate_up_kernel, n_sub), out_shape=(jax.S...  5.35 us
    ppermute x3, waiting for transfers between devices, swap(): return lax.ppermute(x, 'sub', [(i, (i + 1) % n_sub) for i in range(n_sub)])  3.92 us
    ppermute x3, starting transfers between devices, per_device_fast(): other = lax.ppermute(x_half, 'dp', [(i, i ^ step) for i in range(n_dp)])  3.22 us
    pallas_call x1, Pallas kernels, per_device_fast(): pl.pallas_call(functools.partial(down_kernel, n_sub), out_shape=jax.Shape...  2.96 us
    pallas_call x1, Pallas kernels, per_device_fast(): pl.pallas_call(functools.partial(attend_kernel, scale, n_dp, n_sub, laten...  1.54 us
  transfers between devices with their start and end apart: 6, of which 6 were waited for; matrix products, arithmetic and copies ran while one was open for 0% of the time, Pallas kernels for 0%

profile of v4, /device:TPU:0, one launch (start us, length us, event | category | flops | bytes accessed | tf_op | source)
XLA Modules:
  0.0 75.0 jit_solution(14466633055394153197)
XLA Ops:
  0.6 0.0 copy-start.6
  0.6 0.0 copy-start.7
  0.7 0.0 copy-start.2
  0.7 0.0 copy-start.5
  0.7 0.0 copy-start.3
  0.7 0.6 copy-done.6
  1.3 0.0 copy-done.7
  1.3 0.4 copy-done.2
  1.7 0.0 copy-done.5
  1.7 0.0 copy-done.3
  1.7 0.0 copy-start
  1.7 0.0 copy-start.1
  1.7 1.5 %attend.1 = (bf16[576,384]{1,0:T(8,128)(2,1)}, bf16[8,40,576]{2,1,0:T(8,128)(2,1)S(1)}) custom-call(s32[16]{0:T(128)S(1)} %copy-done.7, s32[2,3]{1,0:T(2,128)S(1)} %copy-done.6, s32[8,384]{1,0:T(8,128)S(1)} %positions.1.at_ref, bf16[576,128]{1,0:T(8,128)(2,1)S(1)} %bitcast.23, bf16[1,576]{1,0:T(2,128)(2,1)S(1)} %copy-done.5, bf16[576,384]{1,0:T(8,128)(2,1)S(1)} %bitcast.22), custom_call_target="tpu_custom_call" | custom-call | flops 7549747200 | bytes 25165824 | tf_op jit(solution)/shard_map/attend/pallas_call | solution.py:343
  3.3 19.4 %all_to_all.10.got_ref = bf16[8,40,576]{2,1,0:T(8,128)(2,1)S(1)} all-to-all(bf16[8,40,576]{2,1,0:T(8,128)(2,1)S(1)} %get-tuple-element.10), channel_id=1, replica_groups=mesh['groups'=2,'dp'=8,'sub'=2] {'dp'}, dimensions={0} | all-to-all | bytes 737280 | tf_op jit(solution)/shard_map/all_to_all | solution.py:315
  22.7 0.0 copy-done
  22.7 0.0 copy-done.1
  22.7 0.5 values.1.own_ref
  23.2 0.1 collective-permute-start
  23.2 1.2 %collective-permute-done.peer_ref = bf16[8,2944]{1,0:T(8,128)(2,1)S(1)} collective-permute-done((bf16[8,2944]{1,0:T(8,128)(2,1)S(1)}, bf16[8,2944]{1,0:T(8,128)(2,1)S(1)}, u32[]{:S(2)}, u32[]{:S(2)}) %collective-permute-start) | collective-permute-done | bytes 47136 | tf_op jit(solution)/shard_map/ppermute | solution.py:311
  24.5 6.0 %project.1.a_ref = bf16[16,3584]{1,0:T(8,128)(2,1)S(1)} custom-call(bf16[8,2944]{1,0:T(8,128)(2,1)S(1)} %values.1.own_ref, bf16[8,2944]{1,0:T(8,128)(2,1)S(1)} %collective-permute-done.peer_ref, bf16[2048,7168]{1,0:T(8,128)(2,1)} %w_ref.1), custom_call_target="tpu_custom_call" | custom-call | flops 7549747200 | bytes 25165824 | tf_op jit(solution)/shard_map/project/pallas_call | solution.py:368
  30.5 1.2 %collective-permute-start.1 = (bf16[16,3584]{1,0:T(8,128)(2,1)S(1)}, bf16[16,3584]{1,0:T(8,128)(2,1)S(1)}, u32[]{:S(2)}, u32[]{:S(2)}) collective-permute-start(bf16[16,3584]{1,0:T(8,128)(2,1)S(1)} %project.1.a_ref), channel_id=1, source_target_pairs={{0,2},{2,0},{4,6},{6,4},{8,10},{10,8},{12,14},{14,12},{1,3},{3,1},... | collective-permute-start | bytes 344072 | tf_op jit(solution)/shard_map/ppermute | solution.py:383
  31.7 4.1 %collective-permute-done.1.b_ref = bf16[16,3584]{1,0:T(8,128)(2,1)S(1)} collective-permute-done((bf16[16,3584]{1,0:T(8,128)(2,1)S(1)}, bf16[16,3584]{1,0:T(8,128)(2,1)S(1)}, u32[]{:S(2)}, u32[]{:S(2)}) %collective-permute-start.1) | collective-permute-done | bytes 114720 | tf_op jit(solution)/shard_map/ppermute | solution.py:383
  35.8 1.0 %collective-permute-start.2 = (bf16[16,3584]{1,0:T(8,128)(2,1)S(1)}, bf16[16,3584]{1,0:T(8,128)(2,1)S(1)}, u32[]{:S(2)}, u32[]{:S(2)}) collective-permute-start(bf16[16,3584]{1,0:T(8,128)(2,1)S(1)} %add.3.a_ref), channel_id=1, source_target_pairs={{0,4},{2,6},{4,0},{6,2},{8,12},{10,14},{12,8},{14,10},{1,5},{3,7},... | collective-permute-start | bytes 344072 | tf_op jit(solution)/shard_map/ppermute | solution.py:383
  36.8 3.8 %collective-permute-done.2.b_ref = bf16[16,3584]{1,0:T(8,128)(2,1)S(1)} collective-permute-done((bf16[16,3584]{1,0:T(8,128)(2,1)S(1)}, bf16[16,3584]{1,0:T(8,128)(2,1)S(1)}, u32[]{:S(2)}, u32[]{:S(2)}) %collective-permute-start.2) | collective-permute-done | bytes 114720 | tf_op jit(solution)/shard_map/ppermute | solution.py:383
  40.6 0.0 slice-start.2
  40.6 0.0 slice-start.4
  40.7 0.0 slice-start.3
  40.7 0.0 slice-start.5
  40.7 0.0 copy-start.4
  40.7 1.0 %collective-permute-start.3 = (bf16[16,3584]{1,0:T(8,128)(2,1)S(1)}, bf16[16,3584]{1,0:T(8,128)(2,1)S(1)}, u32[]{:S(2)}, u32[]{:S(2)}) collective-permute-start(bf16[16,3584]{1,0:T(8,128)(2,1)S(1)} %add.4.a_ref), channel_id=1, source_target_pairs={{0,8},{2,10},{4,12},{6,14},{8,0},{10,2},{12,4},{14,6},{1,9},{3,11}... | collective-permute-start | bytes 344072 | tf_op jit(solution)/shard_map/ppermute | solution.py:383
  41.7 6.0 %collective-permute-done.3.b_ref = bf16[16,3584]{1,0:T(8,128)(2,1)S(1)} collective-permute-done((bf16[16,3584]{1,0:T(8,128)(2,1)S(1)}, bf16[16,3584]{1,0:T(8,128)(2,1)S(1)}, u32[]{:S(2)}, u32[]{:S(2)}) %collective-permute-start.3) | collective-permute-done | bytes 114720 | tf_op jit(solution)/shard_map/ppermute | solution.py:383
  47.7 0.0 slice-start
  47.7 0.1 collective-permute-start.4
  47.8 1.3 %collective-permute-done.4.peer_ref = bf16[16,3584]{1,0:T(8,128)(2,1)S(1)} collective-permute-done((bf16[16,3584]{1,0:T(8,128)(2,1)S(1)}, bf16[16,3584]{1,0:T(8,128)(2,1)S(1)}, u32[]{:S(2)}, u32[]{:S(2)}) %collective-permute-start.4) | collective-permute-done | bytes 114720 | tf_op jit(solution)/shard_map/ppermute | solution.py:311
  49.1 0.0 slice-done.2
  49.1 0.0 slice-done.4
  49.1 0.0 slice-done.3
  49.1 0.0 slice-done.5
  49.1 0.0 copy-done.4
  49.2 0.0 slice-start.1
  49.2 5.3 %gate_up.1 = (bf16[8,40,576]{2,1,0:T(8,128)(2,1)S(1)}, bf16[16,448]{1,0:T(8,128)(2,1)S(1)}) custom-call(s32[2,3]{1,0:T(2,128)S(1)} %copy-done.6, bf16[16,3584]{1,0:T(8,128)(2,1)S(1)} %add.5.own_ref, bf16[16,3584]{1,0:T(8,128)(2,1)S(1)} %collective-permute-done.4.peer_ref, bf16[7168]{0:T(1024)(128)(2,1)S(1)} %copy-done.4, ...), custom_call_target="tpu_custom_call" | custom-call | flops 7549747200 | bytes 25165824 | tf_op jit(solution)/shard_map/gate_up/pallas_call | solution.py:394
  54.5 15.3 %all_to_all.11.got_ref = bf16[8,40,576]{2,1,0:T(8,128)(2,1)S(1)} all-to-all(bf16[8,40,576]{2,1,0:T(8,128)(2,1)S(1)} %get-tuple-element.11), channel_id=1, replica_groups=mesh['groups'=2,'dp'=8,'sub'=2] {'dp'}, dimensions={0} | all-to-all | bytes 737280 | tf_op jit(solution)/shard_map/all_to_all | solution.py:315
  69.9 0.7 unpack.1
  70.6 0.0 collective-permute-start.5
  70.6 1.4 %collective-permute-done.5.peer_ref = bf16[8,16,576]{2,1,0:T(8,128)(2,1)S(1)} collective-permute-done((bf16[8,16,576]{2,1,0:T(8,128)(2,1)S(1)}, bf16[8,16,576]{2,1,0:T(8,128)(2,1)S(1)}, u32[]{:S(2)}, u32[]{:S(2)}) %collective-permute-start.5) | collective-permute-done | bytes 147488 | tf_op jit(solution)/shard_map/ppermute | solution.py:311
  72.0 0.0 slice-done
  72.0 0.0 slice-done.1
  72.0 3.0 %down.1 = bf16[16,448]{1,0:T(8,128)(2,1)} custom-call(bf16[8,16,576]{2,1,0:T(8,128)(2,1)S(1)} %get-tuple-element.13.own_ref, bf16[8,16,576]{2,1,0:T(8,128)(2,1)S(1)} %collective-permute-done.5.peer_ref, bf16[16,448]{1,0:T(8,128)(2,1)S(1)} %get-tuple-element.14.base_ref, bf16[448,9216]{1,0:T(8,128)(2,1)S(1)} %bitcast.15), custom_call_target="tpu_custom_call" | custom-call | flops 314572800 | bytes 1048576 | tf_op jit(solution)/shard_map/down/pallas_call | solution.py:419
  (7 shorter events, 0.1 us)
Async XLA Ops:
  0.6 0.7 copy-start.6
  0.6 0.7 copy-start.7
  0.7 1.0 %copy-start.2 = (bf16[1,384,576]{1,2,0:T(8,128)(2,1)S(1)}, bf16[1,384,576]{1,2,0:T(8,128)(2,1)}, u32[]{:S(2)}) copy-start(bf16[1,384,576]{1,2,0:T(8,128)(2,1)} %param.14) | copy-start | bytes 1327108
  0.7 1.0 %copy-start.5 = (bf16[1,576]{1,0:T(2,128)(2,1)S(1)}, bf16[1,576]{1,0:T(2,128)(2,1)}, u32[]{:S(2)}) copy-start(bf16[1,576]{1,0:T(2,128)(2,1)} %fresh_ref.1) | copy-start | bytes 3460
  0.7 1.1 %copy-start.3 = (bf16[1,128,576]{1,2,0:T(8,128)(2,1)S(1)}, bf16[1,128,576]{1,2,0:T(8,128)(2,1)}, u32[]{:S(2)}) copy-start(bf16[1,128,576]{1,2,0:T(8,128)(2,1)} %param.12) | copy-start | bytes 442372
  1.7 21.0 %copy-start = (bf16[16,512,128]{2,1,0:T(8,128)(2,1)S(1)}, bf16[16,512,128]{2,1,0:T(8,128)(2,1)}, u32[]{:S(2)}) copy-start(bf16[16,512,128]{2,1,0:T(8,128)(2,1)} %uv_ref.1) | copy-start | bytes 6291460
  1.7 21.0 %copy-start.1 = (bf16[1,7168]{1,0:T(2,128)(2,1)S(1)}, bf16[1,7168]{1,0:T(2,128)(2,1)}, u32[]{:S(2)}) copy-start(bf16[1,7168]{1,0:T(2,128)(2,1)} %resid_ref.1) | copy-start | bytes 43012
  23.2 1.3 %collective-permute-start = (bf16[8,2944]{1,0:T(8,128)(2,1)S(1)}, bf16[8,2944]{1,0:T(8,128)(2,1)S(1)}, u32[]{:S(2)}, u32[]{:S(2)}) collective-permute-start(bf16[8,2944]{1,0:T(8,128)(2,1)S(1)} %values.1.own_ref), channel_id=1, source_target_pairs={{0,1},{1,0},{2,3},{3,2},{4,5},{5,4},{6,7},{7,6},{8,9},{9,8},{10,11... | collective-permute-start | bytes 141320 | tf_op jit(solution)/shard_map/ppermute | solution.py:311
  30.5 5.3 %collective-permute-start.1 = (bf16[16,3584]{1,0:T(8,128)(2,1)S(1)}, bf16[16,3584]{1,0:T(8,128)(2,1)S(1)}, u32[]{:S(2)}, u32[]{:S(2)}) collective-permute-start(bf16[16,3584]{1,0:T(8,128)(2,1)S(1)} %project.1.a_ref), channel_id=1, source_target_pairs={{0,2},{2,0},{4,6},{6,4},{8,10},{10,8},{12,14},{14,12},{1,3},{3,1},... | collective-permute-start | bytes 344072 | tf_op jit(solution)/shard_map/ppermute | solution.py:383
  35.8 4.9 %collective-permute-start.2 = (bf16[16,3584]{1,0:T(8,128)(2,1)S(1)}, bf16[16,3584]{1,0:T(8,128)(2,1)S(1)}, u32[]{:S(2)}, u32[]{:S(2)}) collective-permute-start(bf16[16,3584]{1,0:T(8,128)(2,1)S(1)} %add.3.a_ref), channel_id=1, source_target_pairs={{0,4},{2,6},{4,0},{6,2},{8,12},{10,14},{12,8},{14,10},{1,5},{3,7},... | collective-permute-start | bytes 344072 | tf_op jit(solution)/shard_map/ppermute | solution.py:383
  40.6 8.5 %slice-start.2 = ((s8[8257536]{0:T(1024)(128)(4,1)}), s8[4194304]{0:T(1024)(128)(4,1)S(1)}, s32[]{:S(2)}) async-start(s8[8257536]{0:T(1024)(128)(4,1)} %bitcast.16), calls=%async_computation.4 | async-start | bytes 8388608
  40.6 8.5 %slice-start.4 = ((s8[8257536]{0:T(1024)(128)(4,1)}), s8[4194304]{0:T(1024)(128)(4,1)S(1)}, s32[]{:S(2)}) async-start(s8[8257536]{0:T(1024)(128)(4,1)} %bitcast.19), calls=%async_computation.6 | async-start | bytes 8388608
  40.7 8.5 %slice-start.3 = ((s8[8257536]{0:T(1024)(128)(4,1)}), s8[4063232]{0:T(1024)(128)(4,1)S(1)}, s32[]{:S(2)}) async-start(s8[8257536]{0:T(1024)(128)(4,1)} %bitcast.16), calls=%async_computation.5 | async-start | bytes 8126464
  40.7 8.4 %slice-start.5 = ((s8[8257536]{0:T(1024)(128)(4,1)}), s8[4063232]{0:T(1024)(128)(4,1)S(1)}, s32[]{:S(2)}) async-start(s8[8257536]{0:T(1024)(128)(4,1)} %bitcast.19), calls=%async_computation.7 | async-start | bytes 8126464
  40.7 8.4 %copy-start.4 = (bf16[7168]{0:T(1024)(128)(2,1)S(1)}, bf16[7168]{0:T(1024)(128)(2,1)}, u32[]{:S(2)}) copy-start(bf16[7168]{0:T(1024)(128)(2,1)} %gain_ref.1) | copy-start | bytes 43012
  40.7 7.0 %collective-permute-start.3 = (bf16[16,3584]{1,0:T(8,128)(2,1)S(1)}, bf16[16,3584]{1,0:T(8,128)(2,1)S(1)}, u32[]{:S(2)}, u32[]{:S(2)}) collective-permute-start(bf16[16,3584]{1,0:T(8,128)(2,1)S(1)} %add.4.a_ref), channel_id=1, source_target_pairs={{0,8},{2,10},{4,12},{6,14},{8,0},{10,2},{12,4},{14,6},{1,9},{3,11}... | collective-permute-start | bytes 344072 | tf_op jit(solution)/shard_map/ppermute | solution.py:383
  47.7 24.3 %slice-start = ((s8[8257536]{0:T(1024)(128)(4,1)}), s8[4194304]{0:T(1024)(128)(4,1)S(1)}, s32[]{:S(2)}) async-start(s8[8257536]{0:T(1024)(128)(4,1)} %bitcast.13), calls=%async_computation.2 | async-start | bytes 8388608
  47.7 1.4 %collective-permute-start.4 = (bf16[16,3584]{1,0:T(8,128)(2,1)S(1)}, bf16[16,3584]{1,0:T(8,128)(2,1)S(1)}, u32[]{:S(2)}, u32[]{:S(2)}) collective-permute-start(bf16[16,3584]{1,0:T(8,128)(2,1)S(1)} %add.5.own_ref), channel_id=1, source_target_pairs={{0,1},{1,0},{2,3},{3,2},{4,5},{5,4},{6,7},{7,6},{8,9},{9,8},{10,11... | collective-permute-start | bytes 344072 | tf_op jit(solution)/shard_map/ppermute | solution.py:311
  49.2 22.8 %slice-start.1 = ((s8[8257536]{0:T(1024)(128)(4,1)}), s8[4063232]{0:T(1024)(128)(4,1)S(1)}, s32[]{:S(2)}) async-start(s8[8257536]{0:T(1024)(128)(4,1)} %bitcast.13), calls=%async_computation.3 | async-start | bytes 8126464
  70.6 1.4 %collective-permute-start.5 = (bf16[8,16,576]{2,1,0:T(8,128)(2,1)S(1)}, bf16[8,16,576]{2,1,0:T(8,128)(2,1)S(1)}, u32[]{:S(2)}, u32[]{:S(2)}) collective-permute-start(bf16[8,16,576]{2,1,0:T(8,128)(2,1)S(1)} %get-tuple-element.13.own_ref), channel_id=1, source_target_pairs={{0,1},{1,0},{2,3},{3,2},{4,5},{5,4},{6,7},{7,6},{8,9},{9,8},{10,11... | collective-permute-start | bytes 442376 | tf_op jit(solution)/shard_map/ppermute | solution.py:311

commit v5 on v4

--- a/solution.py
+++ b/solution.py
@@ -127,7 +127,7 @@
 
 
 def attend_kernel(
-    scale, n_dp, n_sub, latent, lengths, moves, at_ref, q_ref, fresh_ref, cache_ref, kept_ref, out_ref
+    scale, n_dp, n_sub, latent, lengths, moves, at_ref, q_ref, fresh_ref, cache_ref, kept_ref, out_ref, near_ref, far_ref
 ):
     width, cap = cache_ref.shape
     half = cap // 2
@@ -156,14 +156,11 @@
     )
     o_lat = (acc / total).astype(jnp.bfloat16)
     share = heads // n_dp
-    rows = half // n_dp
-    upper = jnp.where(sending, appended.T[half:], 0.0)
+    upper = appended.T[half:].astype(jnp.bfloat16)
+    near_ref[...] = upper[: half // 2]
+    far_ref[...] = upper[half // 2 :]
     for peer in range(n_dp):
-        out_ref[peer, 0:share, 0:latent] = o_lat[peer * share : (peer + 1) * share]
-        out_ref[peer, 0:share, latent:width] = jnp.zeros((share, width - latent), jnp.bfloat16)
-        out_ref[peer, share : share + rows, :] = upper[peer * rows : (peer + 1) * rows].astype(
-            jnp.bfloat16
-        )
+        out_ref[peer] = o_lat[peer * share : (peer + 1) * share]
 
 
 def values_kernel(got_ref, uv_ref, resid_ref, out_ref, wide):
@@ -195,7 +192,7 @@
     return jnp.dot(pick, both, preferred_element_type=jnp.float32).astype(jnp.bfloat16)
 
 
-def project_kernel(n_sub, own_ref, peer_ref, w_ref, out_ref, weights, sems):
+def project_kernel(n_sub, own_ref, peer_ref, w_ref, sum_ref, out_ref, weights, sems):
     requests, half = out_ref.shape
     n_dp = requests // n_sub
     depth = w_ref.shape[0]
@@ -231,25 +228,61 @@
         part = jnp.dot(values, weights[i], preferred_element_type=jnp.float32)
         near = jnp.where(row % n_sub == core, mine[:, span], theirs[:, span])
         part = part + jnp.where(row // n_sub == rank, near, 0.0)
+        sum_ref[:, span] = part
         out_ref[:, span] = part.astype(jnp.bfloat16)
 
 
-def add_kernel(a_ref, b_ref, out_ref):
-    out_ref[...] = (a_ref[...].astype(jnp.float32) + b_ref[...].astype(jnp.float32)).astype(
-        jnp.bfloat16
-    )
-
-
-def unpack_kernel(got_ref, hidden_ref, spare_ref):
-    n_dp, share, _ = hidden_ref.shape
-    rows = spare_ref.shape[0] // n_dp
-    for src in range(n_dp):
-        hidden_ref[src] = got_ref[src, 0:share, :]
-        spare_ref[src * rows : (src + 1) * rows, :] = got_ref[src, share : share + rows, :]
+def add_kernel(own_ref, peer_ref, sum_ref, send_ref):
+    total = own_ref[...] + peer_ref[...].astype(jnp.float32)
+    sum_ref[...] = total
+    send_ref[...] = total.astype(jnp.bfloat16)
+
+
+def last_add_kernel(own_ref, peer_ref, out_ref):
+    out_ref[...] = (own_ref[...] + peer_ref[...].astype(jnp.float32)).astype(jnp.bfloat16)
+
+
+def crosses(moves, core, step):
+    return (moves[core, 1] // step) % 2 != (moves[core, 2] // step) % 2
+
+
+def hop_kernel(n_sub, step, moves, kept_ref, come_ref, out_ref):
+    _, core, _ = place(n_sub)
+    crossing = crosses(moves, core, step)
+
+    @pl.when(crossing)
+    def _():
+        out_ref[...] = come_ref[...]
+
+    @pl.when(jnp.logical_not(crossing))
+    def _():
+        out_ref[...] = kept_ref[...]
+
+
+def finish_kernel(n_sub, steps, moves, near_ref, near_come_ref, far_ref, far_come_ref, out_ref):
+    rank, core, _ = place(n_sub)
+    rows = near_ref.shape[0]
+    wanted = rank == moves[core, 2]
+    pairs = ((near_ref, near_come_ref), (far_ref, far_come_ref))
+    for part, (step, (kept_ref, come_ref)) in enumerate(zip(steps, pairs)):
+        crossing = crosses(moves, core, step)
+        span = slice(part * rows, (part + 1) * rows)
+
+        @pl.when(wanted & crossing)
+        def _():
+            out_ref[span, :] = come_ref[...]
+
+        @pl.when(wanted & jnp.logical_not(crossing))
+        def _():
+            out_ref[span, :] = kept_ref[...]
+
+        @pl.when(jnp.logical_not(wanted))
+        def _():
+            out_ref[span, :] = jnp.zeros_like(kept_ref)
 
 
 def gate_up_kernel(
-    n_sub, moves, own_ref, peer_ref, gain_ref, got_ref, gate_ref, up_ref, out_ref, base_ref, whole
+    n_sub, own_ref, peer_ref, gain_ref, gate_ref, up_ref, out_ref, base_ref, whole
 ):
     half = own_ref.shape[1]
     cols = base_ref.shape[1]
@@ -268,25 +301,8 @@
     gate = lax.dot_general(gate_ref[...], normed, NT, preferred_element_type=jnp.float32)
     up = lax.dot_general(up_ref[...], normed, NT, preferred_element_type=jnp.float32)
     hidden = (gate * jax.nn.sigmoid(gate) * up).T.astype(jnp.bfloat16)
-    requests = hidden.shape[0]
-    rows = out_ref.shape[1] - requests
-    from_row = got_ref.shape[1] - rows
     for dst in range(out_ref.shape[0]):
-        out_ref[dst, 0:requests, :] = hidden
-        source = jnp.int32(0)
-        found = jnp.int32(0)
-        for row in range(moves.shape[0]):
-            hit = (moves[row, 2] == dst) & (moves[row, 0] % n_sub == core)
-            source = jnp.where(hit, moves[row, 1], source)
-            found = jnp.where(hit, 1, found)
-
-        @pl.when(found == 1)
-        def _():
-            out_ref[dst, requests:, :] = got_ref[source, from_row:, :]
-
-        @pl.when(found == 0)
-        def _():
-            out_ref[dst, requests:, :] = jnp.zeros((rows, out_ref.shape[2]), jnp.bfloat16)
+        out_ref[dst] = hidden
 
 
 def down_kernel(n_sub, own_ref, peer_ref, base_ref, down_ref, out_ref, hidden):
@@ -324,7 +340,6 @@
     heads = queries.shape[1]
     share, latent, vh = w_uv.shape
     half = cap // 2
-    rows = half // n_dp
     dim = w_out.shape[1]
     requests = n_dp * n_sub
     units = w_gate.shape[1]
@@ -340,19 +355,21 @@
         cost_estimate=cost(40),
         name="positions",
     )()
-    kept, sent = pl.pallas_call(
+    kept, sent, near, far = pl.pallas_call(
         functools.partial(attend_kernel, scale, n_dp, n_sub, latent),
         out_shape=(
             jax.ShapeDtypeStruct((width, cap), bf16),
-            jax.ShapeDtypeStruct((n_dp, share + rows, width), bf16),
+            jax.ShapeDtypeStruct((n_dp, share, latent), bf16),
+            jax.ShapeDtypeStruct((half // 2, width), bf16),
+            jax.ShapeDtypeStruct((half // 2, width), bf16),
         ),
         in_specs=[SMEM] * 2 + [VMEM] * 4,
-        out_specs=(VMEM, VMEM),
+        out_specs=(VMEM,) * 4,
         compiler_params=params(8),
         cost_estimate=cost(24),
         name="attend",
     )(lengths, moves, positions, queries[0].T, new_latent, cache[0].T)
-    got = exchange(sent)
+    got, near, far = lax.optimization_barrier((exchange(sent), near, far))
     wide_half = dim // n_sub
     values = pl.pallas_call(
         values_kernel,
@@ -365,11 +382,44 @@
         name="values",
     )(got, w_uv, resid)
     peer_values = swap(values, n_sub)
-    x_half = pl.pallas_call(
+    def cross(x, step):
+        return lax.ppermute(x, "dp", [(i, i ^ step) for i in range(n_dp)])
+
+    def hop(step, here, come):
+        return pl.pallas_call(
+            functools.partial(hop_kernel, n_sub, step),
+            out_shape=jax.ShapeDtypeStruct((half // 2, width), bf16),
+            in_specs=[SMEM, VMEM, VMEM],
+            out_specs=VMEM,
+            compiler_params=params(8),
+            cost_estimate=cost(1),
+            name="hop",
+        )(moves, here, come)
+
+    def add(total, come):
+        return pl.pallas_call(
+            add_kernel,
+            out_shape=(
+                jax.ShapeDtypeStruct((requests, wide_half), f32),
+                jax.ShapeDtypeStruct((requests, wide_half), bf16),
+            ),
+            in_specs=[VMEM] * 2,
+            out_specs=(VMEM, VMEM),
+            compiler_params=params(8),
+            cost_estimate=cost(1),
+            name="add",
+        )(total, come)
+
+    near_come = cross(near, 4)
+    far_come = cross(far, 2)
+    total, part = pl.pallas_call(
         functools.partial(project_kernel, n_sub),
-        out_shape=jax.ShapeDtypeStruct((requests, wide_half), bf16),
+        out_shape=(
+            jax.ShapeDtypeStruct((requests, wide_half), f32),
+            jax.ShapeDtypeStruct((requests, wide_half), bf16),
+        ),
         in_specs=[VMEM, VMEM, HBM],
-        out_specs=VMEM,
+        out_specs=(VMEM, VMEM),
         scratch_shapes=[
             pltpu.VMEM((4, share * vh, wide_half // 4), bf16),
             pltpu.SemaphoreType.DMA((4,)),
@@ -378,44 +428,43 @@
         cost_estimate=cost(24),
         name="project",
     )(values, peer_values, w_out)
-    step = 1
-    while step < n_dp:
-        other = lax.ppermute(x_half, "dp", [(i, i ^ step) for i in range(n_dp)])
-        x_half = pl.pallas_call(
-            add_kernel,
-            out_shape=jax.ShapeDtypeStruct((requests, wide_half), bf16),
-            in_specs=[VMEM] * 2,
-            out_specs=VMEM,
-            compiler_params=params(8),
-            cost_estimate=cost(24),
-            name="add",
-        )(x_half, other)
-        step *= 2
-    sent, base = pl.pallas_call(
+    near_come, far_come, part = lax.optimization_barrier((near_come, far_come, part))
+    near = hop(4, near, near_come)
+    far = hop(2, far, far_come)
+    near_come = cross(near, 2)
+    total, part = add(total, cross(part, 1))
+    near_come, part = lax.optimization_barrier((near_come, part))
+    near = hop(2, near, near_come)
+    near_come = cross(near, 1)
+    far_come = cross(far, 1)
+    total, part = add(total, cross(part, 2))
+    far = hop(1, far, far_come)
+    come, near_come, far = lax.optimization_barrier((cross(part, 4), near_come, far))
+    x_half = pl.pallas_call(
+        last_add_kernel,
+        out_shape=jax.ShapeDtypeStruct((requests, wide_half), bf16),
+        in_specs=[VMEM] * 2,
+        out_specs=VMEM,
+        compiler_params=params(8),
+        cost_estimate=cost(1),
+        name="last_add",
+    )(total, come)
+    far_come = cross(far, 4)
+    hidden, base = pl.pallas_call(
         functools.partial(gate_up_kernel, n_sub),
         out_shape=(
-            jax.ShapeDtypeStruct((n_dp, requests + rows, units), bf16),
+            jax.ShapeDtypeStruct((n_dp, requests, units), bf16),
             jax.ShapeDtypeStruct((requests, cols), bf16),
         ),
-        in_specs=[SMEM] + [VMEM] * 6,
+        in_specs=[VMEM] * 5,
         out_specs=(VMEM, VMEM),
         scratch_shapes=[pltpu.VMEM((requests, dim), f32)],
         compiler_params=params(24),
         cost_estimate=cost(24),
         name="gate_up",
-    )(moves, x_half, swap(x_half, n_sub), norm_gain, got, w_gate.T, w_up.T)
-    every, spare = pl.pallas_call(
-        unpack_kernel,
-        out_shape=(
-            jax.ShapeDtypeStruct((n_dp, requests, units), bf16),
-            jax.ShapeDtypeStruct((half, width), bf16),
-        ),
-        in_specs=[VMEM],
-        out_specs=(VMEM, VMEM),
-        compiler_params=params(8),
-        cost_estimate=cost(1),
-        name="unpack",
-    )(exchange(sent))
+    )(x_half, swap(x_half, n_sub), norm_gain, w_gate.T, w_up.T)
+    hidden, far_come = lax.optimization_barrier((hidden, far_come))
+    every = exchange(hidden)
     mixed = pl.pallas_call(
         functools.partial(down_kernel, n_sub),
         out_shape=jax.ShapeDtypeStruct((requests, cols), bf16),
@@ -426,18 +475,28 @@
         cost_estimate=cost(1),
         name="down",
     )(every, swap(every, n_sub), base, w_down.T)
+    spare = pl.pallas_call(
+        functools.partial(finish_kernel, n_sub, (1, 4)),
+        out_shape=jax.ShapeDtypeStruct((half, width), bf16),
+        in_specs=[SMEM] + [VMEM] * 4,
+        out_specs=VMEM,
+        compiler_params=params(8),
+        cost_estimate=cost(1),
+        name="finish",
+    )(moves, near, near_come, far, far_come)
     return (kept.T[None], spare[None], mixed)
 
 
 def per_device(*args):
-    queries, cache, w_uv, w_out = args[0], args[2], args[6], args[7]
+    queries, cache, moves, w_uv, w_out = args[0], args[2], args[4], args[6], args[7]
     w_gate, w_down = args[9], args[11]
     n_dp = lax.axis_size("dp")
     n_sub = lax.axis_size("sub")
     fits = (
         n_sub == 2
         and n_dp == 8
-        and cache.shape[1] % (2 * 8 * n_dp) == 0
+        and moves.shape[0] == n_sub
+        and cache.shape[1] % 128 == 0
         and queries.shape[1] // n_dp == 16
         and w_uv.shape[1] == 512
         and w_out.shape[1] % (n_sub * 4 * 128) == 0

time: 75.2 us -> 70.5 us (0.938)
  blocking collectives: 34.7 us -> 25.8 us
  starting transfers between devices: 3.37 us -> 8.49 us
  waiting for transfers between devices: 17.8 us -> 13.9 us
  Pallas kernels: 17.1 us -> 20.3 us
    all_to_all x2, blocking collectives: 34.7 us -> 25.8 us  [exchange(): return lax.all_to_all(x, 'dp', split_axis=0, concat_axis=0, tiled=True)]
    ppermute x3 -> x9, starting transfers between devices: 3.22 us -> 8.34 us  [cross(): return lax.ppermute(x, 'dp', [(i, i ^ step) for i in range(n_dp)])]
    ppermute x3, waiting for transfers between devices: 3.92 us -> 0.1 us  [swap(): return lax.ppermute(x, 'sub', [(i, (i + 1) % n_sub) for i in range(n_sub)])]
    pallas_call x5 -> x9, Pallas kernels: 6.81 us -> 10.5 us  [the longest x1 6.75 us: per_device_fast(): pl.pallas_call(functools.partial(project_kernel, n_sub), out_shape=(jax.S...]
    ppermute x3 -> x9, waiting for transfers between devices: 13.9 us -> 13.8 us  [cross(): return lax.ppermute(x, 'dp', [(i, i ^ step) for i in range(n_dp)])]
  transfers between devices with their start and end apart: 6 -> 12, of which waited for: 6 -> 7; matrix products, arithmetic and copies ran while one was open for 0% -> 0% of each run, Pallas kernels for 0% -> 22%
where the time goes in v5:
time: 70.5 us; the launch traced here: 70.3 us
  blocking collectives  25.8 us (37%)
  Pallas kernels  20.3 us (29%)
  waiting for transfers between devices  13.9 us (20%)
  starting transfers between devices  8.49 us (12%)
  local copies, waits for them, and re-layouts  1.09 us (2%)
  between operations  0.85 us (1%)
    all_to_all x2, blocking collectives, exchange(): return lax.all_to_all(x, 'dp', split_axis=0, concat_axis=0, tiled=True)  25.8 us
    ppermute x9, waiting for transfers between devices, cross(): return lax.ppermute(x, 'dp', [(i, i ^ step) for i in range(n_dp)])  13.8 us
    ppermute x9, starting transfers between devices, cross(): return lax.ppermute(x, 'dp', [(i, i ^ step) for i in range(n_dp)])  8.34 us
    pallas_call x1, Pallas kernels, per_device_fast(): pl.pallas_call(functools.partial(project_kernel, n_sub), out_shape=(jax.S...  6.75 us
    pallas_call x1, Pallas kernels, per_device_fast(): pl.pallas_call(functools.partial(gate_up_kernel, n_sub), out_shape=(jax.S...  4.66 us
    pallas_call x1, Pallas kernels, per_device_fast(): pl.pallas_call(functools.partial(down_kernel, n_sub), out_shape=jax.Shape...  2.95 us
    pallas_call x4, Pallas kernels, hop(): pl.pallas_call(functools.partial(hop_kernel, n_sub, step), out_shape=jax....  2.35 us
    pallas_call x1, Pallas kernels, per_device_fast(): pl.pallas_call(functools.partial(attend_kernel, scale, n_dp, n_sub, laten...  1.67 us
  transfers between devices with their start and end apart: 12, of which 7 were waited for; matrix products, arithmetic and copies ran while one was open for 0% of the time, Pallas kernels for 22%

profile of v5, /device:TPU:0, one launch (start us, length us, event | category | flops | bytes accessed | tf_op | source)
XLA Modules:
  0.0 70.3 jit_solution(17257788595414801537)
XLA Ops:
  0.6 0.0 copy-start.6
  0.6 0.0 copy-start.7
  0.7 0.0 copy-start.2
  0.7 0.0 copy-start.5
  0.7 0.0 copy-start.3
  0.7 0.6 copy-done.6
  1.3 0.4 copy-done.2
  1.7 0.0 copy-done.3
  1.7 1.7 %attend.1 = (bf16[576,384]{1,0:T(8,128)(2,1)}, bf16[8,16,512]{2,1,0:T(8,128)(2,1)S(1)}, bf16[96,576]{1,0:T(8,128)(2,1)S(1)}, bf16[96,576]{1,0:T(8,128)(2,1)S(1)}) custom-call(s32[16]{0:T(128)S(1)} %copy-done.7, s32[2,3]{1,0:T(2,128)S(1)} %copy-done.6, s32[8,384]{1,0:T(8,128)S(1)} %positions.1.at_ref, bf16[576,128]{1,0:T(8,128)(2,1)S(1)} %bitcast.23, ...), custom_call_target="tpu_custom_call" | custom-call | flops 7549747200 | bytes 25165824 | tf_op jit(solution)/shard_map/attend/pallas_call | solution.py:358
  3.4 14.4 %all_to_all.10.got_ref = bf16[8,16,512]{2,1,0:T(8,128)(2,1)S(1)} all-to-all(bf16[8,16,512]{2,1,0:T(8,128)(2,1)S(1)} %get-tuple-element.29), channel_id=1, replica_groups=mesh['groups'=2,'dp'=8,'sub'=2] {'dp'}, dimensions={0} | all-to-all | bytes 262144 | tf_op jit(solution)/shard_map/all_to_all | solution.py:331
  17.8 0.5 values.1.own_ref
  18.3 0.0 slice-start.3
  18.3 0.0 slice-start.5
  18.3 0.0 copy-start.4
  18.3 0.1 collective-permute-start.2
  18.4 0.5 collective-permute-start
  18.8 0.7 %collective-permute-start.1 = (bf16[96,576]{1,0:T(8,128)(2,1)S(1)}, bf16[96,576]{1,0:T(8,128)(2,1)S(1)}, u32[]{:S(2)}, u32[]{:S(2)}) collective-permute-start(bf16[96,576]{1,0:T(8,128)(2,1)S(1)} %get-tuple-element.33.kept_ref), channel_id=1, source_target_pairs={{0,4},{2,6},{4,0},{6,2},{8,12},{10,14},{12,8},{14,10},{1,5},{3,7},... | collective-permute-start | bytes 331784 | tf_op jit(solution)/shard_map/ppermute | solution.py:386
  19.6 0.0 collective-permute-done.2.peer_ref
  19.6 6.8 %project.1 = (f32[16,3584]{1,0:T(8,128)S(1)}, bf16[16,3584]{1,0:T(8,128)(2,1)S(1)}) custom-call(bf16[8,2944]{1,0:T(8,128)(2,1)S(1)} %values.1.own_ref, bf16[8,2944]{1,0:T(8,128)(2,1)S(1)} %collective-permute-done.2.peer_ref, bf16[2048,7168]{1,0:T(8,128)(2,1)} %w_ref.1), custom_call_target="tpu_custom_call" | custom-call | flops 7549747200 | bytes 25165824 | tf_op jit(solution)/shard_map/project/pallas_call | solution.py:415
  26.4 0.6 collective-permute-done.come_ref
  27.0 0.0 collective-permute-done.1.come_ref
  27.0 0.9 %collective-permute-start.4 = (bf16[16,3584]{1,0:T(8,128)(2,1)S(1)}, bf16[16,3584]{1,0:T(8,128)(2,1)S(1)}, u32[]{:S(2)}, u32[]{:S(2)}) collective-permute-start(bf16[16,3584]{1,0:T(8,128)(2,1)S(1)} %get-tuple-element.38), channel_id=1, source_target_pairs={{0,2},{2,0},{4,6},{6,4},{8,10},{10,8},{12,14},{14,12},{1,3},{3,1},... | collective-permute-start | bytes 344072 | tf_op jit(solution)/shard_map/ppermute | solution.py:386
  27.9 0.6 hop.4.kept_ref
  28.5 0.1 collective-permute-start.3
  28.6 3.5 %collective-permute-done.4.peer_ref = bf16[16,3584]{1,0:T(8,128)(2,1)S(1)} collective-permute-done((bf16[16,3584]{1,0:T(8,128)(2,1)S(1)}, bf16[16,3584]{1,0:T(8,128)(2,1)S(1)}, u32[]{:S(2)}, u32[]{:S(2)}) %collective-permute-start.4) | collective-permute-done | bytes 114720 | tf_op jit(solution)/shard_map/ppermute | solution.py:386
  32.1 1.3 %collective-permute-done.3.come_ref = bf16[96,576]{1,0:T(8,128)(2,1)S(1)} collective-permute-done((bf16[96,576]{1,0:T(8,128)(2,1)S(1)}, bf16[96,576]{1,0:T(8,128)(2,1)S(1)}, u32[]{:S(2)}, u32[]{:S(2)}) %collective-permute-start.3) | collective-permute-done | bytes 110624 | tf_op jit(solution)/shard_map/ppermute | solution.py:386
  33.4 0.1 collective-permute-start.5
  33.5 0.6 hop.6.kept_ref
  34.1 1.8 %collective-permute-start.8 = (bf16[96,576]{1,0:T(8,128)(2,1)S(1)}, bf16[96,576]{1,0:T(8,128)(2,1)S(1)}, u32[]{:S(2)}, u32[]{:S(2)}) collective-permute-start(bf16[96,576]{1,0:T(8,128)(2,1)S(1)} %hop.6.kept_ref), channel_id=1, source_target_pairs={{0,2},{2,0},{4,6},{6,4},{8,10},{10,8},{12,14},{14,12},{1,3},{3,1},... | collective-permute-start | bytes 331784 | tf_op jit(solution)/shard_map/ppermute | solution.py:386
  36.0 2.2 %collective-permute-done.5.peer_ref = bf16[16,3584]{1,0:T(8,128)(2,1)S(1)} collective-permute-done((bf16[16,3584]{1,0:T(8,128)(2,1)S(1)}, bf16[16,3584]{1,0:T(8,128)(2,1)S(1)}, u32[]{:S(2)}, u32[]{:S(2)}) %collective-permute-start.5) | collective-permute-done | bytes 114720 | tf_op jit(solution)/shard_map/ppermute | solution.py:386
  38.3 1.4 %collective-permute-start.6 = (bf16[16,3584]{1,0:T(8,128)(2,1)S(1)}, bf16[16,3584]{1,0:T(8,128)(2,1)S(1)}, u32[]{:S(2)}, u32[]{:S(2)}) collective-permute-start(bf16[16,3584]{1,0:T(8,128)(2,1)S(1)} %get-tuple-element.43), channel_id=1, source_target_pairs={{0,8},{2,10},{4,12},{6,14},{8,0},{10,2},{12,4},{14,6},{1,9},{3,11}... | collective-permute-start | bytes 344072 | tf_op jit(solution)/shard_map/ppermute | solution.py:386
  39.7 0.6 hop.5.near_ref
  40.3 1.1 %collective-permute-start.7 = (bf16[96,576]{1,0:T(8,128)(2,1)S(1)}, bf16[96,576]{1,0:T(8,128)(2,1)S(1)}, u32[]{:S(2)}, u32[]{:S(2)}) collective-permute-start(bf16[96,576]{1,0:T(8,128)(2,1)S(1)} %hop.5.near_ref), channel_id=1, source_target_pairs={{0,2},{2,0},{4,6},{6,4},{8,10},{10,8},{12,14},{14,12},{1,3},{3,1},... | collective-permute-start | bytes 331784 | tf_op jit(solution)/shard_map/ppermute | solution.py:386
  41.4 0.0 collective-permute-done.8.come_ref
  41.4 0.6 hop.7.far_ref
  42.0 3.2 %collective-permute-done.7.near_come_ref = bf16[96,576]{1,0:T(8,128)(2,1)S(1)} collective-permute-done((bf16[96,576]{1,0:T(8,128)(2,1)S(1)}, bf16[96,576]{1,0:T(8,128)(2,1)S(1)}, u32[]{:S(2)}, u32[]{:S(2)}) %collective-permute-start.7) | collective-permute-done | bytes 110624 | tf_op jit(solution)/shard_map/ppermute | solution.py:386
  45.2 0.0 collective-permute-done.6.peer_ref
  45.3 0.1 collective-permute-start.9
  45.3 1.6 %collective-permute-start.10 = (bf16[96,576]{1,0:T(8,128)(2,1)S(1)}, bf16[96,576]{1,0:T(8,128)(2,1)S(1)}, u32[]{:S(2)}, u32[]{:S(2)}) collective-permute-start(bf16[96,576]{1,0:T(8,128)(2,1)S(1)} %hop.7.far_ref), channel_id=1, source_target_pairs={{0,8},{2,10},{4,12},{6,14},{8,0},{10,2},{12,4},{14,6},{1,9},{3,11}... | collective-permute-start | bytes 331784 | tf_op jit(solution)/shard_map/ppermute | solution.py:386
  47.0 0.0 collective-permute-done.9.peer_ref
  47.0 0.0 slice-start.1
  47.0 4.7 %gate_up.1 = (bf16[8,16,576]{2,1,0:T(8,128)(2,1)S(1)}, bf16[16,448]{1,0:T(8,128)(2,1)S(1)}) custom-call(bf16[16,3584]{1,0:T(8,128)(2,1)S(1)} %last_add.1.own_ref, bf16[16,3584]{1,0:T(8,128)(2,1)S(1)} %collective-permute-done.9.peer_ref, bf16[7168]{0:T(1024)(128)(2,1)S(1)} %copy-done.4, bf16[576,7168]{1,0:T(8,128)(2,1)S(1)} %bitcast.18, ...), custom_call_target="tpu_custom_call" | custom-call | flops 7549747200 | bytes 25165824 | tf_op jit(solution)/shard_map/gate_up/pallas_call | solution.py:453
  51.7 2.9 %collective-permute-done.10.far_come_ref = bf16[96,576]{1,0:T(8,128)(2,1)S(1)} collective-permute-done((bf16[96,576]{1,0:T(8,128)(2,1)S(1)}, bf16[96,576]{1,0:T(8,128)(2,1)S(1)}, u32[]{:S(2)}, u32[]{:S(2)}) %collective-permute-start.10) | collective-permute-done | bytes 110624 | tf_op jit(solution)/shard_map/ppermute | solution.py:386
  54.6 11.4 %all_to_all.11.own_ref = bf16[8,16,576]{2,1,0:T(8,128)(2,1)S(1)} all-to-all(bf16[8,16,576]{2,1,0:T(8,128)(2,1)S(1)} %get-tuple-element.51), channel_id=1, replica_groups=mesh['groups'=2,'dp'=8,'sub'=2] {'dp'}, dimensions={0} | all-to-all | bytes 294912 | tf_op jit(solution)/shard_map/all_to_all | solution.py:331
  66.0 0.0 collective-permute-start.11
  66.0 1.3 %finish.1 = bf16[192,576]{1,0:T(8,128)(2,1)} custom-call(s32[2,3]{1,0:T(2,128)S(1)} %copy-done.6, bf16[96,576]{1,0:T(8,128)(2,1)S(1)} %hop.5.near_ref, bf16[96,576]{1,0:T(8,128)(2,1)S(1)} %collective-permute-done.7.near_come_ref, bf16[96,576]{1,0:T(8,128)(2,1)S(1)} %hop.7.far_ref, bf16[96,576]{1,0:T(8,128)(2,1)S(1)} %collective-permute-done.10.far_come_ref), custom_call_target="tpu_custom_call" | custom-call | flops 314572800 | bytes 1048576 | tf_op jit(solution)/shard_map/finish/pallas_call | solution.py:478
  67.3 0.1 collective-permute-done.11.peer_ref
  67.4 2.9 %down.1 = bf16[16,448]{1,0:T(8,128)(2,1)} custom-call(bf16[8,16,576]{2,1,0:T(8,128)(2,1)S(1)} %all_to_all.11.own_ref, bf16[8,16,576]{2,1,0:T(8,128)(2,1)S(1)} %collective-permute-done.11.peer_ref, bf16[16,448]{1,0:T(8,128)(2,1)S(1)} %get-tuple-element.52.base_ref, bf16[448,9216]{1,0:T(8,128)(2,1)S(1)} %bitcast.15), custom_call_target="tpu_custom_call" | custom-call | flops 314572800 | bytes 1048576 | tf_op jit(solution)/shard_map/down/pallas_call | solution.py:468
  (23 shorter events, 0.1 us)
Async XLA Ops:
  0.6 0.7 copy-start.6
  0.6 0.7 copy-start.7
  0.7 1.0 %copy-start.2 = (bf16[1,384,576]{1,2,0:T(8,128)(2,1)S(1)}, bf16[1,384,576]{1,2,0:T(8,128)(2,1)}, u32[]{:S(2)}) copy-start(bf16[1,384,576]{1,2,0:T(8,128)(2,1)} %param.14) | copy-start | bytes 1327108
  0.7 1.0 %copy-start.5 = (bf16[1,576]{1,0:T(2,128)(2,1)S(1)}, bf16[1,576]{1,0:T(2,128)(2,1)}, u32[]{:S(2)}) copy-start(bf16[1,576]{1,0:T(2,128)(2,1)} %fresh_ref.1) | copy-start | bytes 3460
  0.7 1.1 %copy-start.3 = (bf16[1,128,576]{1,2,0:T(8,128)(2,1)S(1)}, bf16[1,128,576]{1,2,0:T(8,128)(2,1)}, u32[]{:S(2)}) copy-start(bf16[1,128,576]{1,2,0:T(8,128)(2,1)} %param.12) | copy-start | bytes 442372
  1.7 16.1 %copy-start = (bf16[16,512,128]{2,1,0:T(8,128)(2,1)S(1)}, bf16[16,512,128]{2,1,0:T(8,128)(2,1)}, u32[]{:S(2)}) copy-start(bf16[16,512,128]{2,1,0:T(8,128)(2,1)} %uv_ref.1) | copy-start | bytes 6291460
  1.7 16.1 %copy-start.1 = (bf16[1,7168]{1,0:T(2,128)(2,1)S(1)}, bf16[1,7168]{1,0:T(2,128)(2,1)}, u32[]{:S(2)}) copy-start(bf16[1,7168]{1,0:T(2,128)(2,1)} %resid_ref.1) | copy-start | bytes 43012
  17.8 29.2 %slice-start.2 = ((s8[8257536]{0:T(1024)(128)(4,1)}), s8[4194304]{0:T(1024)(128)(4,1)S(1)}, s32[]{:S(2)}) async-start(s8[8257536]{0:T(1024)(128)(4,1)} %bitcast.16), calls=%async_computation.4 | async-start | bytes 8388608
  17.8 29.2 %slice-start.4 = ((s8[8257536]{0:T(1024)(128)(4,1)}), s8[4194304]{0:T(1024)(128)(4,1)S(1)}, s32[]{:S(2)}) async-start(s8[8257536]{0:T(1024)(128)(4,1)} %bitcast.19), calls=%async_computation.6 | async-start | bytes 8388608
  18.3 28.7 %slice-start.3 = ((s8[8257536]{0:T(1024)(128)(4,1)}), s8[4063232]{0:T(1024)(128)(4,1)S(1)}, s32[]{:S(2)}) async-start(s8[8257536]{0:T(1024)(128)(4,1)} %bitcast.16), calls=%async_computation.5 | async-start | bytes 8126464
  18.3 28.7 %slice-start.5 = ((s8[8257536]{0:T(1024)(128)(4,1)}), s8[4063232]{0:T(1024)(128)(4,1)S(1)}, s32[]{:S(2)}) async-start(s8[8257536]{0:T(1024)(128)(4,1)} %bitcast.19), calls=%async_computation.7 | async-start | bytes 8126464
  18.3 28.7 %copy-start.4 = (bf16[7168]{0:T(1024)(128)(2,1)S(1)}, bf16[7168]{0:T(1024)(128)(2,1)}, u32[]{:S(2)}) copy-start(bf16[7168]{0:T(1024)(128)(2,1)} %gain_ref.1) | copy-start | bytes 43012
  18.3 1.3 %collective-permute-start.2 = (bf16[8,2944]{1,0:T(8,128)(2,1)S(1)}, bf16[8,2944]{1,0:T(8,128)(2,1)S(1)}, u32[]{:S(2)}, u32[]{:S(2)}) collective-permute-start(bf16[8,2944]{1,0:T(8,128)(2,1)S(1)} %values.1.own_ref), channel_id=1, source_target_pairs={{0,1},{1,0},{2,3},{3,2},{4,5},{5,4},{6,7},{7,6},{8,9},{9,8},{10,11... | collective-permute-start | bytes 141320 | tf_op jit(solution)/shard_map/ppermute | solution.py:327
  18.4 8.6 %collective-permute-start = (bf16[96,576]{1,0:T(8,128)(2,1)S(1)}, bf16[96,576]{1,0:T(8,128)(2,1)S(1)}, u32[]{:S(2)}, u32[]{:S(2)}) collective-permute-start(bf16[96,576]{1,0:T(8,128)(2,1)S(1)} %get-tuple-element.32.kept_ref), channel_id=1, source_target_pairs={{0,8},{2,10},{4,12},{6,14},{8,0},{10,2},{12,4},{14,6},{1,9},{3,11}... | collective-permute-start | bytes 331784 | tf_op jit(solution)/shard_map/ppermute | solution.py:386
  18.8 8.1 %collective-permute-start.1 = (bf16[96,576]{1,0:T(8,128)(2,1)S(1)}, bf16[96,576]{1,0:T(8,128)(2,1)S(1)}, u32[]{:S(2)}, u32[]{:S(2)}) collective-permute-start(bf16[96,576]{1,0:T(8,128)(2,1)S(1)} %get-tuple-element.33.kept_ref), channel_id=1, source_target_pairs={{0,4},{2,6},{4,0},{6,2},{8,12},{10,14},{12,8},{14,10},{1,5},{3,7},... | collective-permute-start | bytes 331784 | tf_op jit(solution)/shard_map/ppermute | solution.py:386
  27.0 5.1 %collective-permute-start.4 = (bf16[16,3584]{1,0:T(8,128)(2,1)S(1)}, bf16[16,3584]{1,0:T(8,128)(2,1)S(1)}, u32[]{:S(2)}, u32[]{:S(2)}) collective-permute-start(bf16[16,3584]{1,0:T(8,128)(2,1)S(1)} %get-tuple-element.38), channel_id=1, source_target_pairs={{0,2},{2,0},{4,6},{6,4},{8,10},{10,8},{12,14},{14,12},{1,3},{3,1},... | collective-permute-start | bytes 344072 | tf_op jit(solution)/shard_map/ppermute | solution.py:386
  28.5 4.9 %collective-permute-start.3 = (bf16[96,576]{1,0:T(8,128)(2,1)S(1)}, bf16[96,576]{1,0:T(8,128)(2,1)S(1)}, u32[]{:S(2)}, u32[]{:S(2)}) collective-permute-start(bf16[96,576]{1,0:T(8,128)(2,1)S(1)} %hop.4.kept_ref), channel_id=1, source_target_pairs={{0,4},{2,6},{4,0},{6,2},{8,12},{10,14},{12,8},{14,10},{1,5},{3,7},... | collective-permute-start | bytes 331784 | tf_op jit(solution)/shard_map/ppermute | solution.py:386
  33.4 4.8 %collective-permute-start.5 = (bf16[16,3584]{1,0:T(8,128)(2,1)S(1)}, bf16[16,3584]{1,0:T(8,128)(2,1)S(1)}, u32[]{:S(2)}, u32[]{:S(2)}) collective-permute-start(bf16[16,3584]{1,0:T(8,128)(2,1)S(1)} %get-tuple-element.42), channel_id=1, source_target_pairs={{0,4},{2,6},{4,0},{6,2},{8,12},{10,14},{12,8},{14,10},{1,5},{3,7},... | collective-permute-start | bytes 344072 | tf_op jit(solution)/shard_map/ppermute | solution.py:386
  34.1 7.2 %collective-permute-start.8 = (bf16[96,576]{1,0:T(8,128)(2,1)S(1)}, bf16[96,576]{1,0:T(8,128)(2,1)S(1)}, u32[]{:S(2)}, u32[]{:S(2)}) collective-permute-start(bf16[96,576]{1,0:T(8,128)(2,1)S(1)} %hop.6.kept_ref), channel_id=1, source_target_pairs={{0,2},{2,0},{4,6},{6,4},{8,10},{10,8},{12,14},{14,12},{1,3},{3,1},... | collective-permute-start | bytes 331784 | tf_op jit(solution)/shard_map/ppermute | solution.py:386
  38.3 7.0 %collective-permute-start.6 = (bf16[16,3584]{1,0:T(8,128)(2,1)S(1)}, bf16[16,3584]{1,0:T(8,128)(2,1)S(1)}, u32[]{:S(2)}, u32[]{:S(2)}) collective-permute-start(bf16[16,3584]{1,0:T(8,128)(2,1)S(1)} %get-tuple-element.43), channel_id=1, source_target_pairs={{0,8},{2,10},{4,12},{6,14},{8,0},{10,2},{12,4},{14,6},{1,9},{3,11}... | collective-permute-start | bytes 344072 | tf_op jit(solution)/shard_map/ppermute | solution.py:386
  40.3 4.9 %collective-permute-start.7 = (bf16[96,576]{1,0:T(8,128)(2,1)S(1)}, bf16[96,576]{1,0:T(8,128)(2,1)S(1)}, u32[]{:S(2)}, u32[]{:S(2)}) collective-permute-start(bf16[96,576]{1,0:T(8,128)(2,1)S(1)} %hop.5.near_ref), channel_id=1, source_target_pairs={{0,2},{2,0},{4,6},{6,4},{8,10},{10,8},{12,14},{14,12},{1,3},{3,1},... | collective-permute-start | bytes 331784 | tf_op jit(solution)/shard_map/ppermute | solution.py:386
  41.4 26.0 %slice-start = ((s8[8257536]{0:T(1024)(128)(4,1)}), s8[4194304]{0:T(1024)(128)(4,1)S(1)}, s32[]{:S(2)}) async-start(s8[8257536]{0:T(1024)(128)(4,1)} %bitcast.13), calls=%async_computation.2 | async-start | bytes 8388608
  45.3 1.7 %collective-permute-start.9 = (bf16[16,3584]{1,0:T(8,128)(2,1)S(1)}, bf16[16,3584]{1,0:T(8,128)(2,1)S(1)}, u32[]{:S(2)}, u32[]{:S(2)}) collective-permute-start(bf16[16,3584]{1,0:T(8,128)(2,1)S(1)} %last_add.1.own_ref), channel_id=1, source_target_pairs={{0,1},{1,0},{2,3},{3,2},{4,5},{5,4},{6,7},{7,6},{8,9},{9,8},{10,11... | collective-permute-start | bytes 344072 | tf_op jit(solution)/shard_map/ppermute | solution.py:327
  45.3 9.3 %collective-permute-start.10 = (bf16[96,576]{1,0:T(8,128)(2,1)S(1)}, bf16[96,576]{1,0:T(8,128)(2,1)S(1)}, u32[]{:S(2)}, u32[]{:S(2)}) collective-permute-start(bf16[96,576]{1,0:T(8,128)(2,1)S(1)} %hop.7.far_ref), channel_id=1, source_target_pairs={{0,8},{2,10},{4,12},{6,14},{8,0},{10,2},{12,4},{14,6},{1,9},{3,11}... | collective-permute-start | bytes 331784 | tf_op jit(solution)/shard_map/ppermute | solution.py:386
  47.0 20.4 %slice-start.1 = ((s8[8257536]{0:T(1024)(128)(4,1)}), s8[4063232]{0:T(1024)(128)(4,1)S(1)}, s32[]{:S(2)}) async-start(s8[8257536]{0:T(1024)(128)(4,1)} %bitcast.13), calls=%async_computation.3 | async-start | bytes 8126464
  66.0 1.4 %collective-permute-start.11 = (bf16[8,16,576]{2,1,0:T(8,128)(2,1)S(1)}, bf16[8,16,576]{2,1,0:T(8,128)(2,1)S(1)}, u32[]{:S(2)}, u32[]{:S(2)}) collective-permute-start(bf16[8,16,576]{2,1,0:T(8,128)(2,1)S(1)} %all_to_all.11.own_ref), channel_id=1, source_target_pairs={{0,1},{1,0},{2,3},{3,2},{4,5},{5,4},{6,7},{7,6},{8,9},{9,8},{10,11... | collective-permute-start | bytes 442376 | tf_op jit(solution)/shard_map/ppermute | solution.py:327

commit v6 on v5

--- a/solution.py
+++ b/solution.py
@@ -126,6 +126,22 @@
     out_ref[...] = lax.broadcasted_iota(jnp.int32, out_ref.shape, 1)
 
 
+def pack(x):
+    rows, width = x.shape
+    whole = width // 128 * 128
+    pieces = [x[:, i : i + 128] for i in range(0, whole, 128)]
+    rest = jnp.concatenate([x[: rows // 2, whole:], x[rows // 2 :, whole:]], axis=1)
+    return jnp.concatenate(pieces + [rest], axis=0)
+
+
+def unpack(x, rows, width):
+    whole = width // 128 * 128
+    pieces = [x[rows * i : rows * (i + 1)] for i in range(whole // 128)]
+    rest = x[rows * (whole // 128) :]
+    tail = jnp.concatenate([rest[:, : width - whole], rest[:, width - whole :]], axis=0)
+    return jnp.concatenate(pieces + [tail], axis=1)
+
+
 def attend_kernel(
     scale, n_dp, n_sub, latent, lengths, moves, at_ref, q_ref, fresh_ref, cache_ref, kept_ref, out_ref, near_ref, far_ref
 ):
@@ -156,9 +172,9 @@
     )
     o_lat = (acc / total).astype(jnp.bfloat16)
     share = heads // n_dp
-    upper = appended.T[half:].astype(jnp.bfloat16)
-    near_ref[...] = upper[: half // 2]
-    far_ref[...] = upper[half // 2 :]
+    upper = appended.T[half:]
+    near_ref[...] = pack(upper[: half // 2]).astype(jnp.bfloat16)
+    far_ref[...] = pack(upper[half // 2 :]).astype(jnp.bfloat16)
     for peer in range(n_dp):
         out_ref[peer] = o_lat[peer * share : (peer + 1) * share]
 
@@ -243,7 +259,9 @@
 
 
 def crosses(moves, core, step):
-    return (moves[core, 1] // step) % 2 != (moves[core, 2] // step) % 2
+    source, target = moves[core, 1], moves[core, 2]
+    bits = {1: (1,), 2: (2, 4), 6: (4,)}[step]
+    return sum(source // bit + target // bit for bit in bits) % 2 != 0
 
 
 def hop_kernel(n_sub, step, moves, kept_ref, come_ref, out_ref):
@@ -261,24 +279,24 @@
 
 def finish_kernel(n_sub, steps, moves, near_ref, near_come_ref, far_ref, far_come_ref, out_ref):
     rank, core, _ = place(n_sub)
-    rows = near_ref.shape[0]
+    rows = out_ref.shape[0] // 2
+    width = out_ref.shape[1]
     wanted = rank == moves[core, 2]
     pairs = ((near_ref, near_come_ref), (far_ref, far_come_ref))
-    for part, (step, (kept_ref, come_ref)) in enumerate(zip(steps, pairs)):
-        crossing = crosses(moves, core, step)
-        span = slice(part * rows, (part + 1) * rows)
-
-        @pl.when(wanted & crossing)
-        def _():
-            out_ref[span, :] = come_ref[...]
-
-        @pl.when(wanted & jnp.logical_not(crossing))
-        def _():
-            out_ref[span, :] = kept_ref[...]
-
-        @pl.when(jnp.logical_not(wanted))
-        def _():
-            out_ref[span, :] = jnp.zeros_like(kept_ref)
+
+    @pl.when(jnp.logical_not(wanted))
+    def _():
+        out_ref[...] = jnp.zeros_like(out_ref)
+
+    @pl.when(wanted)
+    def _():
+        for part, (step, (kept_ref, come_ref)) in enumerate(zip(steps, pairs)):
+            kept = kept_ref[...].astype(jnp.float32)
+            come = come_ref[...].astype(jnp.float32)
+            picked = jnp.where(crosses(moves, core, step), come, kept)
+            out_ref[part * rows : (part + 1) * rows, :] = unpack(picked, rows, width).astype(
+                jnp.bfloat16
+            )
 
 
 def gate_up_kernel(
@@ -300,18 +318,19 @@
     base_ref[...] = jnp.where(core == 0, near[:, :cols], near[:, 64:]).astype(jnp.bfloat16)
     gate = lax.dot_general(gate_ref[...], normed, NT, preferred_element_type=jnp.float32)
     up = lax.dot_general(up_ref[...], normed, NT, preferred_element_type=jnp.float32)
-    hidden = (gate * jax.nn.sigmoid(gate) * up).T.astype(jnp.bfloat16)
+    hidden = pack((gate * jax.nn.sigmoid(gate) * up).T).astype(jnp.bfloat16)
     for dst in range(out_ref.shape[0]):
         out_ref[dst] = hidden
 
 
 def down_kernel(n_sub, own_ref, peer_ref, base_ref, down_ref, out_ref, hidden):
-    units = own_ref.shape[2]
+    requests = out_ref.shape[0]
+    units = own_ref.shape[1] * 128 // requests
     _, core, _ = place(n_sub)
 
     for src in range(own_ref.shape[0]):
-        own = own_ref[src].astype(jnp.float32)
-        peer = peer_ref[src].astype(jnp.float32)
+        own = unpack(own_ref[src].astype(jnp.float32), requests, units)
+        peer = unpack(peer_ref[src].astype(jnp.float32), requests, units)
         first = jnp.where(core == 0, own, peer)
         second = jnp.where(core == 0, peer, own)
         hidden[:, src * n_sub * units : (src + 1) * n_sub * units] = jnp.concatenate(
@@ -360,8 +379,8 @@
         out_shape=(
             jax.ShapeDtypeStruct((width, cap), bf16),
             jax.ShapeDtypeStruct((n_dp, share, latent), bf16),
-            jax.ShapeDtypeStruct((half // 2, width), bf16),
-            jax.ShapeDtypeStruct((half // 2, width), bf16),
+            jax.ShapeDtypeStruct((half // 2 * width // 128, 128), bf16),
+            jax.ShapeDtypeStruct((half // 2 * width // 128, 128), bf16),
         ),
         in_specs=[SMEM] * 2 + [VMEM] * 4,
         out_specs=(VMEM,) * 4,
@@ -388,7 +407,7 @@
     def hop(step, here, come):
         return pl.pallas_call(
             functools.partial(hop_kernel, n_sub, step),
-            out_shape=jax.ShapeDtypeStruct((half // 2, width), bf16),
+            out_shape=jax.ShapeDtypeStruct(here.shape, bf16),
             in_specs=[SMEM, VMEM, VMEM],
             out_specs=VMEM,
             compiler_params=params(8),
@@ -410,7 +429,7 @@
             name="add",
         )(total, come)
 
-    near_come = cross(near, 4)
+    near_come = cross(near, 6)
     far_come = cross(far, 2)
     total, part = pl.pallas_call(
         functools.partial(project_kernel, n_sub),
@@ -429,17 +448,16 @@
         name="project",
     )(values, peer_values, w_out)
     near_come, far_come, part = lax.optimization_barrier((near_come, far_come, part))
-    near = hop(4, near, near_come)
+    near = hop(6, near, near_come)
     far = hop(2, far, far_come)
     near_come = cross(near, 2)
     total, part = add(total, cross(part, 1))
-    near_come, part = lax.optimization_barrier((near_come, part))
     near = hop(2, near, near_come)
     near_come = cross(near, 1)
     far_come = cross(far, 1)
     total, part = add(total, cross(part, 2))
     far = hop(1, far, far_come)
-    come, near_come, far = lax.optimization_barrier((cross(part, 4), near_come, far))
+    come, near_come, far = lax.optimization_barrier((cross(part, 6), near_come, far))
     x_half = pl.pallas_call(
         last_add_kernel,
         out_shape=jax.ShapeDtypeStruct((requests, wide_half), bf16),
@@ -449,11 +467,11 @@
         cost_estimate=cost(1),
         name="last_add",
     )(total, come)
-    far_come = cross(far, 4)
+    far_come = cross(far, 6)
     hidden, base = pl.pallas_call(
         functools.partial(gate_up_kernel, n_sub),
         out_shape=(
-            jax.ShapeDtypeStruct((n_dp, requests, units), bf16),
+            jax.ShapeDtypeStruct((n_dp, requests * units // 128, 128), bf16),
             jax.ShapeDtypeStruct((requests, cols), bf16),
         ),
         in_specs=[VMEM] * 5,
@@ -476,7 +494,7 @@
         name="down",
     )(every, swap(every, n_sub), base, w_down.T)
     spare = pl.pallas_call(
-        functools.partial(finish_kernel, n_sub, (1, 4)),
+        functools.partial(finish_kernel, n_sub, (1, 6)),
         out_shape=jax.ShapeDtypeStruct((half, width), bf16),
         in_specs=[SMEM] + [VMEM] * 4,
         out_specs=VMEM,
@@ -500,7 +518,8 @@
         and queries.shape[1] // n_dp == 16
         and w_uv.shape[1] == 512
         and w_out.shape[1] % (n_sub * 4 * 128) == 0
-        and w_gate.shape[1] == cache.shape[2]
+        and w_gate.shape[1] % 128 == 64
+        and cache.shape[2] % 128 == 64
         and w_down.shape[1] % 64 == 0
     )
     return per_device_fast(*args) if fits else per_device_any(*args)

time: 70.5 us -> 67.8 us (0.962)
  waiting for transfers between devices: 13.9 us -> 10.5 us
  starting transfers between devices: 8.49 us -> 9.86 us
  blocking collectives: 25.8 us -> 24.9 us
    ppermute x9, waiting for transfers between devices: 13.8 us -> 10.3 us  [cross(): return lax.ppermute(x, 'dp', [(i, i ^ step) for i in range(n_dp)])]
    ppermute x9, starting transfers between devices: 8.34 us -> 9.72 us  [cross(): return lax.ppermute(x, 'dp', [(i, i ^ step) for i in range(n_dp)])]
    all_to_all x2, blocking collectives: 25.8 us -> 24.9 us  [exchange(): return lax.all_to_all(x, 'dp', split_axis=0, concat_axis=0, tiled=True)]
  transfers between devices with their start and end apart: 12 -> 12, of which waited for: 7 -> 6; matrix products, arithmetic and copies ran while one was open for 0% -> 0% of each run, Pallas kernels for 22% -> 23%
where the time goes in v6:
time: 67.8 us; the launch traced here: 67.6 us
  blocking collectives  24.9 us (37%)
  Pallas kernels  20.4 us (30%)
  waiting for transfers between devices  10.5 us (15%)
  starting transfers between devices  9.86 us (15%)
  local copies, waits for them, and re-layouts  1.09 us (2%)
  between operations  0.87 us (1%)
    all_to_all x2, blocking collectives, exchange(): return lax.all_to_all(x, 'dp', split_axis=0, concat_axis=0, tiled=True)  24.9 us
    ppermute x9, waiting for transfers between devices, cross(): return lax.ppermute(x, 'dp', [(i, i ^ step) for i in range(n_dp)])  10.3 us
    ppermute x9, starting transfers between devices, cross(): return lax.ppermute(x, 'dp', [(i, i ^ step) for i in range(n_dp)])  9.72 us
    pallas_call x1, Pallas kernels, per_device_fast(): pl.pallas_call(functools.partial(project_kernel, n_sub), out_shape=(jax.S...  6.75 us
    pallas_call x1, Pallas kernels, per_device_fast(): pl.pallas_call(functools.partial(gate_up_kernel, n_sub), out_shape=(jax.S...  4.7 us
    pallas_call x1, Pallas kernels, per_device_fast(): pl.pallas_call(functools.partial(down_kernel, n_sub), out_shape=jax.Shape...  2.94 us
    pallas_call x4, Pallas kernels, hop(): pl.pallas_call(functools.partial(hop_kernel, n_sub, step), out_shape=jax....  2.35 us
    pallas_call x1, Pallas kernels, per_device_fast(): pl.pallas_call(functools.partial(attend_kernel, scale, n_dp, n_sub, laten...  1.64 us
  transfers between devices with their start and end apart: 12, of which 6 were waited for; matrix products, arithmetic and copies ran while one was open for 0% of the time, Pallas kernels for 23%

profile of v6, /device:TPU:0, one launch (start us, length us, event | category | flops | bytes accessed | tf_op | source)
XLA Modules:
  0.0 67.6 jit_solution(10730296861411175573)
XLA Ops:
  0.6 0.0 copy-start.6
  0.7 0.6 copy-done.6
  1.3 0.4 copy-done.2
  1.7 0.0 copy-done.5
  1.7 0.0 copy-done.3
  1.7 1.6 %attend.1 = (bf16[576,384]{1,0:T(8,128)(2,1)}, bf16[8,16,512]{2,1,0:T(8,128)(2,1)S(1)}, bf16[432,128]{1,0:T(8,128)(2,1)S(1)}, bf16[432,128]{1,0:T(8,128)(2,1)S(1)}) custom-call(s32[16]{0:T(128)S(1)} %copy-done.7, s32[2,3]{1,0:T(2,128)S(1)} %copy-done.6, s32[8,384]{1,0:T(8,128)S(1)} %positions.1.at_ref, bf16[576,128]{1,0:T(8,128)(2,1)S(1)} %bitcast.23, ...), custom_call_target="tpu_custom_call" | custom-call | flops 7549747200 | bytes 25165824 | tf_op jit(solution)/shard_map/attend/pallas_call | solution.py:377
  3.4 14.4 %all_to_all.10.got_ref = bf16[8,16,512]{2,1,0:T(8,128)(2,1)S(1)} all-to-all(bf16[8,16,512]{2,1,0:T(8,128)(2,1)S(1)} %get-tuple-element.27), channel_id=1, replica_groups=mesh['groups'=2,'dp'=8,'sub'=2] {'dp'}, dimensions={0} | all-to-all | bytes 262144 | tf_op jit(solution)/shard_map/all_to_all | solution.py:350
  17.8 0.5 values.1.own_ref
  18.2 0.0 slice-start.3
  18.3 0.0 slice-start.5
  18.3 0.0 copy-start.4
  18.3 0.1 collective-permute-start.2
  18.4 0.6 collective-permute-start
  19.0 0.4 collective-permute-start.1
  19.4 0.2 collective-permute-done.2.peer_ref
  19.6 6.8 %project.1 = (f32[16,3584]{1,0:T(8,128)S(1)}, bf16[16,3584]{1,0:T(8,128)(2,1)S(1)}) custom-call(bf16[8,2944]{1,0:T(8,128)(2,1)S(1)} %values.1.own_ref, bf16[8,2944]{1,0:T(8,128)(2,1)S(1)} %collective-permute-done.2.peer_ref, bf16[2048,7168]{1,0:T(8,128)(2,1)} %w_ref.1), custom_call_target="tpu_custom_call" | custom-call | flops 7549747200 | bytes 25165824 | tf_op jit(solution)/shard_map/project/pallas_call | solution.py:434
  26.3 0.0 collective-permute-done.come_ref
  26.3 0.1 collective-permute-done.1.come_ref
  26.5 1.1 %collective-permute-start.4 = (bf16[16,3584]{1,0:T(8,128)(2,1)S(1)}, bf16[16,3584]{1,0:T(8,128)(2,1)S(1)}, u32[]{:S(2)}, u32[]{:S(2)}) collective-permute-start(bf16[16,3584]{1,0:T(8,128)(2,1)S(1)} %get-tuple-element.36), channel_id=1, source_target_pairs={{0,2},{2,0},{4,6},{6,4},{8,10},{10,8},{12,14},{14,12},{1,3},{3,1},... | collective-permute-start | bytes 344072 | tf_op jit(solution)/shard_map/ppermute | solution.py:405
  27.6 4.1 %collective-permute-done.4.peer_ref = bf16[16,3584]{1,0:T(8,128)(2,1)S(1)} collective-permute-done((bf16[16,3584]{1,0:T(8,128)(2,1)S(1)}, bf16[16,3584]{1,0:T(8,128)(2,1)S(1)}, u32[]{:S(2)}, u32[]{:S(2)}) %collective-permute-start.4) | collective-permute-done | bytes 114720 | tf_op jit(solution)/shard_map/ppermute | solution.py:405
  31.7 1.1 %collective-permute-start.5 = (bf16[16,3584]{1,0:T(8,128)(2,1)S(1)}, bf16[16,3584]{1,0:T(8,128)(2,1)S(1)}, u32[]{:S(2)}, u32[]{:S(2)}) collective-permute-start(bf16[16,3584]{1,0:T(8,128)(2,1)S(1)} %get-tuple-element.38), channel_id=1, source_target_pairs={{0,4},{2,6},{4,0},{6,2},{8,12},{10,14},{12,8},{14,10},{1,5},{3,7},... | collective-permute-start | bytes 344072 | tf_op jit(solution)/shard_map/ppermute | solution.py:405
  32.8 0.6 hop.4.kept_ref
  33.4 1.1 %collective-permute-start.3 = (bf16[432,128]{1,0:T(8,128)(2,1)S(1)}, bf16[432,128]{1,0:T(8,128)(2,1)S(1)}, u32[]{:S(2)}, u32[]{:S(2)}) collective-permute-start(bf16[432,128]{1,0:T(8,128)(2,1)S(1)} %hop.4.kept_ref), channel_id=1, source_target_pairs={{0,4},{2,6},{4,0},{6,2},{8,12},{10,14},{12,8},{14,10},{1,5},{3,7},... | collective-permute-start | bytes 331784 | tf_op jit(solution)/shard_map/ppermute | solution.py:405
  34.4 0.6 hop.6.kept_ref
  35.0 0.8 %collective-permute-start.8 = (bf16[432,128]{1,0:T(8,128)(2,1)S(1)}, bf16[432,128]{1,0:T(8,128)(2,1)S(1)}, u32[]{:S(2)}, u32[]{:S(2)}) collective-permute-start(bf16[432,128]{1,0:T(8,128)(2,1)S(1)} %hop.6.kept_ref), channel_id=1, source_target_pairs={{0,2},{2,0},{4,6},{6,4},{8,10},{10,8},{12,14},{14,12},{1,3},{3,1},... | collective-permute-start | bytes 331784 | tf_op jit(solution)/shard_map/ppermute | solution.py:405
  35.8 1.4 %collective-permute-done.5.peer_ref = bf16[16,3584]{1,0:T(8,128)(2,1)S(1)} collective-permute-done((bf16[16,3584]{1,0:T(8,128)(2,1)S(1)}, bf16[16,3584]{1,0:T(8,128)(2,1)S(1)}, u32[]{:S(2)}, u32[]{:S(2)}) %collective-permute-start.5) | collective-permute-done | bytes 114720 | tf_op jit(solution)/shard_map/ppermute | solution.py:405
  37.3 2.5 %collective-permute-start.6 = (bf16[16,3584]{1,0:T(8,128)(2,1)S(1)}, bf16[16,3584]{1,0:T(8,128)(2,1)S(1)}, u32[]{:S(2)}, u32[]{:S(2)}) collective-permute-start(bf16[16,3584]{1,0:T(8,128)(2,1)S(1)} %get-tuple-element.39), channel_id=1, source_target_pairs={{0,12},{2,14},{4,8},{6,10},{8,4},{10,6},{12,0},{14,2},{1,13},{3,15... | collective-permute-start | bytes 344072 | tf_op jit(solution)/shard_map/ppermute | solution.py:405
  39.8 0.0 collective-permute-done.3.come_ref
  39.8 0.6 hop.5.near_ref
  40.4 0.7 %collective-permute-start.7 = (bf16[432,128]{1,0:T(8,128)(2,1)S(1)}, bf16[432,128]{1,0:T(8,128)(2,1)S(1)}, u32[]{:S(2)}, u32[]{:S(2)}) collective-permute-start(bf16[432,128]{1,0:T(8,128)(2,1)S(1)} %hop.5.near_ref), channel_id=1, source_target_pairs={{0,2},{2,0},{4,6},{6,4},{8,10},{10,8},{12,14},{14,12},{1,3},{3,1},... | collective-permute-start | bytes 331784 | tf_op jit(solution)/shard_map/ppermute | solution.py:405
  41.1 0.0 collective-permute-done.8.come_ref
  41.2 0.6 hop.7.far_ref
  41.7 3.5 %collective-permute-done.7.near_come_ref = bf16[432,128]{1,0:T(8,128)(2,1)S(1)} collective-permute-done((bf16[432,128]{1,0:T(8,128)(2,1)S(1)}, bf16[432,128]{1,0:T(8,128)(2,1)S(1)}, u32[]{:S(2)}, u32[]{:S(2)}) %collective-permute-start.7) | collective-permute-done | bytes 110624 | tf_op jit(solution)/shard_map/ppermute | solution.py:405
  45.2 0.0 collective-permute-done.6.peer_ref
  45.3 0.1 collective-permute-start.9
  45.4 1.4 %collective-permute-start.10 = (bf16[432,128]{1,0:T(8,128)(2,1)S(1)}, bf16[432,128]{1,0:T(8,128)(2,1)S(1)}, u32[]{:S(2)}, u32[]{:S(2)}) collective-permute-start(bf16[432,128]{1,0:T(8,128)(2,1)S(1)} %hop.7.far_ref), channel_id=1, source_target_pairs={{0,12},{2,14},{4,8},{6,10},{8,4},{10,6},{12,0},{14,2},{1,13},{3,15... | collective-permute-start | bytes 331784 | tf_op jit(solution)/shard_map/ppermute | solution.py:405
  46.8 0.0 collective-permute-done.9.peer_ref
  46.8 0.0 slice-done.3
  46.8 0.0 slice-done.5
  46.8 0.0 copy-done.4
  46.8 0.0 slice-start.1
  46.9 4.7 %gate_up.1 = (bf16[8,72,128]{2,1,0:T(8,128)(2,1)S(1)}, bf16[16,448]{1,0:T(8,128)(2,1)S(1)}) custom-call(bf16[16,3584]{1,0:T(8,128)(2,1)S(1)} %last_add.1.own_ref, bf16[16,3584]{1,0:T(8,128)(2,1)S(1)} %collective-permute-done.9.peer_ref, bf16[7168]{0:T(1024)(128)(2,1)S(1)} %copy-done.4, bf16[576,7168]{1,0:T(8,128)(2,1)S(1)} %bitcast.18, ...), custom_call_target="tpu_custom_call" | custom-call | flops 7549747200 | bytes 25165824 | tf_op jit(solution)/shard_map/gate_up/pallas_call | solution.py:471
  51.6 1.1 %collective-permute-done.10.far_come_ref = bf16[432,128]{1,0:T(8,128)(2,1)S(1)} collective-permute-done((bf16[432,128]{1,0:T(8,128)(2,1)S(1)}, bf16[432,128]{1,0:T(8,128)(2,1)S(1)}, u32[]{:S(2)}, u32[]{:S(2)}) %collective-permute-start.10) | collective-permute-done | bytes 110624 | tf_op jit(solution)/shard_map/ppermute | solution.py:405
  52.6 10.5 %all_to_all.11.own_ref = bf16[8,72,128]{2,1,0:T(8,128)(2,1)S(1)} all-to-all(bf16[8,72,128]{2,1,0:T(8,128)(2,1)S(1)} %get-tuple-element.47), channel_id=1, replica_groups=mesh['groups'=2,'dp'=8,'sub'=2] {'dp'}, dimensions={0} | all-to-all | bytes 294912 | tf_op jit(solution)/shard_map/all_to_all | solution.py:350
  63.2 0.0 collective-permute-start.11
  63.2 1.4 %finish.1 = bf16[192,576]{1,0:T(8,128)(2,1)} custom-call(s32[2,3]{1,0:T(2,128)S(1)} %copy-done.6, bf16[432,128]{1,0:T(8,128)(2,1)S(1)} %hop.5.near_ref, bf16[432,128]{1,0:T(8,128)(2,1)S(1)} %collective-permute-done.7.near_come_ref, bf16[432,128]{1,0:T(8,128)(2,1)S(1)} %hop.7.far_ref, bf16[432,128]{1,0:T(8,128)(2,1)S(1)} %collective-permute-done.10.far_come_ref), custom_call_target="tpu_custom_call" | custom-call | flops 314572800 | bytes 1048576 | tf_op jit(solution)/shard_map/finish/pallas_call | solution.py:496
  64.6 0.0 collective-permute-done.11.peer_ref
  64.6 2.9 %down.1 = bf16[16,448]{1,0:T(8,128)(2,1)} custom-call(bf16[8,72,128]{2,1,0:T(8,128)(2,1)S(1)} %all_to_all.11.own_ref, bf16[8,72,128]{2,1,0:T(8,128)(2,1)S(1)} %collective-permute-done.11.peer_ref, bf16[16,448]{1,0:T(8,128)(2,1)S(1)} %get-tuple-element.48.base_ref, bf16[448,9216]{1,0:T(8,128)(2,1)S(1)} %bitcast.15), custom_call_target="tpu_custom_call" | custom-call | flops 314572800 | bytes 1048576 | tf_op jit(solution)/shard_map/down/pallas_call | solution.py:486
  (23 shorter events, 0.1 us)
Async XLA Ops:
  0.6 0.7 %copy-start.6 = (s32[2,3]{1,0:T(2,128)S(1)}, s32[2,3]{1,0:T(2,128)}, u32[]{:S(2)}) copy-start(s32[2,3]{1,0:T(2,128)} %moves.11) | copy-start | bytes 76
  0.6 0.7 copy-start.7
  0.7 1.0 %copy-start.2 = (bf16[1,384,576]{1,2,0:T(8,128)(2,1)S(1)}, bf16[1,384,576]{1,2,0:T(8,128)(2,1)}, u32[]{:S(2)}) copy-start(bf16[1,384,576]{1,2,0:T(8,128)(2,1)} %param.14) | copy-start | bytes 1327108
  0.7 1.0 %copy-start.5 = (bf16[1,576]{1,0:T(2,128)(2,1)S(1)}, bf16[1,576]{1,0:T(2,128)(2,1)}, u32[]{:S(2)}) copy-start(bf16[1,576]{1,0:T(2,128)(2,1)} %fresh_ref.1) | copy-start | bytes 3460
  0.7 1.1 %copy-start.3 = (bf16[1,128,576]{1,2,0:T(8,128)(2,1)S(1)}, bf16[1,128,576]{1,2,0:T(8,128)(2,1)}, u32[]{:S(2)}) copy-start(bf16[1,128,576]{1,2,0:T(8,128)(2,1)} %param.12) | copy-start | bytes 442372
  1.7 16.0 %copy-start = (bf16[16,512,128]{2,1,0:T(8,128)(2,1)S(1)}, bf16[16,512,128]{2,1,0:T(8,128)(2,1)}, u32[]{:S(2)}) copy-start(bf16[16,512,128]{2,1,0:T(8,128)(2,1)} %uv_ref.1) | copy-start | bytes 6291460
  1.7 16.0 %copy-start.1 = (bf16[1,7168]{1,0:T(2,128)(2,1)S(1)}, bf16[1,7168]{1,0:T(2,128)(2,1)}, u32[]{:S(2)}) copy-start(bf16[1,7168]{1,0:T(2,128)(2,1)} %resid_ref.1) | copy-start | bytes 43012
  17.8 29.0 %slice-start.2 = ((s8[8257536]{0:T(1024)(128)(4,1)}), s8[4194304]{0:T(1024)(128)(4,1)S(1)}, s32[]{:S(2)}) async-start(s8[8257536]{0:T(1024)(128)(4,1)} %bitcast.16), calls=%async_computation.4 | async-start | bytes 8388608
  17.8 29.0 %slice-start.4 = ((s8[8257536]{0:T(1024)(128)(4,1)}), s8[4194304]{0:T(1024)(128)(4,1)S(1)}, s32[]{:S(2)}) async-start(s8[8257536]{0:T(1024)(128)(4,1)} %bitcast.19), calls=%async_computation.6 | async-start | bytes 8388608
  18.2 28.6 %slice-start.3 = ((s8[8257536]{0:T(1024)(128)(4,1)}), s8[4063232]{0:T(1024)(128)(4,1)S(1)}, s32[]{:S(2)}) async-start(s8[8257536]{0:T(1024)(128)(4,1)} %bitcast.16), calls=%async_computation.5 | async-start | bytes 8126464
  18.3 28.6 %slice-start.5 = ((s8[8257536]{0:T(1024)(128)(4,1)}), s8[4063232]{0:T(1024)(128)(4,1)S(1)}, s32[]{:S(2)}) async-start(s8[8257536]{0:T(1024)(128)(4,1)} %bitcast.19), calls=%async_computation.7 | async-start | bytes 8126464
  18.3 28.6 %copy-start.4 = (bf16[7168]{0:T(1024)(128)(2,1)S(1)}, bf16[7168]{0:T(1024)(128)(2,1)}, u32[]{:S(2)}) copy-start(bf16[7168]{0:T(1024)(128)(2,1)} %gain_ref.1) | copy-start | bytes 43012
  18.3 1.3 %collective-permute-start.2 = (bf16[8,2944]{1,0:T(8,128)(2,1)S(1)}, bf16[8,2944]{1,0:T(8,128)(2,1)S(1)}, u32[]{:S(2)}, u32[]{:S(2)}) collective-permute-start(bf16[8,2944]{1,0:T(8,128)(2,1)S(1)} %values.1.own_ref), channel_id=1, source_target_pairs={{0,1},{1,0},{2,3},{3,2},{4,5},{5,4},{6,7},{7,6},{8,9},{9,8},{10,11... | collective-permute-start | bytes 141320 | tf_op jit(solution)/shard_map/ppermute | solution.py:346
  18.4 8.0 %collective-permute-start = (bf16[432,128]{1,0:T(8,128)(2,1)S(1)}, bf16[432,128]{1,0:T(8,128)(2,1)S(1)}, u32[]{:S(2)}, u32[]{:S(2)}) collective-permute-start(bf16[432,128]{1,0:T(8,128)(2,1)S(1)} %get-tuple-element.30.kept_ref), channel_id=1, source_target_pairs={{0,12},{2,14},{4,8},{6,10},{8,4},{10,6},{12,0},{14,2},{1,13},{3,15... | collective-permute-start | bytes 331784 | tf_op jit(solution)/shard_map/ppermute | solution.py:405
  19.0 7.5 %collective-permute-start.1 = (bf16[432,128]{1,0:T(8,128)(2,1)S(1)}, bf16[432,128]{1,0:T(8,128)(2,1)S(1)}, u32[]{:S(2)}, u32[]{:S(2)}) collective-permute-start(bf16[432,128]{1,0:T(8,128)(2,1)S(1)} %get-tuple-element.31.kept_ref), channel_id=1, source_target_pairs={{0,4},{2,6},{4,0},{6,2},{8,12},{10,14},{12,8},{14,10},{1,5},{3,7},... | collective-permute-start | bytes 331784 | tf_op jit(solution)/shard_map/ppermute | solution.py:405
  26.5 5.2 %collective-permute-start.4 = (bf16[16,3584]{1,0:T(8,128)(2,1)S(1)}, bf16[16,3584]{1,0:T(8,128)(2,1)S(1)}, u32[]{:S(2)}, u32[]{:S(2)}) collective-permute-start(bf16[16,3584]{1,0:T(8,128)(2,1)S(1)} %get-tuple-element.36), channel_id=1, source_target_pairs={{0,2},{2,0},{4,6},{6,4},{8,10},{10,8},{12,14},{14,12},{1,3},{3,1},... | collective-permute-start | bytes 344072 | tf_op jit(solution)/shard_map/ppermute | solution.py:405
  31.7 5.6 %collective-permute-start.5 = (bf16[16,3584]{1,0:T(8,128)(2,1)S(1)}, bf16[16,3584]{1,0:T(8,128)(2,1)S(1)}, u32[]{:S(2)}, u32[]{:S(2)}) collective-permute-start(bf16[16,3584]{1,0:T(8,128)(2,1)S(1)} %get-tuple-element.38), channel_id=1, source_target_pairs={{0,4},{2,6},{4,0},{6,2},{8,12},{10,14},{12,8},{14,10},{1,5},{3,7},... | collective-permute-start | bytes 344072 | tf_op jit(solution)/shard_map/ppermute | solution.py:405
  33.4 6.5 %collective-permute-start.3 = (bf16[432,128]{1,0:T(8,128)(2,1)S(1)}, bf16[432,128]{1,0:T(8,128)(2,1)S(1)}, u32[]{:S(2)}, u32[]{:S(2)}) collective-permute-start(bf16[432,128]{1,0:T(8,128)(2,1)S(1)} %hop.4.kept_ref), channel_id=1, source_target_pairs={{0,4},{2,6},{4,0},{6,2},{8,12},{10,14},{12,8},{14,10},{1,5},{3,7},... | collective-permute-start | bytes 331784 | tf_op jit(solution)/shard_map/ppermute | solution.py:405
  35.0 6.1 %collective-permute-start.8 = (bf16[432,128]{1,0:T(8,128)(2,1)S(1)}, bf16[432,128]{1,0:T(8,128)(2,1)S(1)}, u32[]{:S(2)}, u32[]{:S(2)}) collective-permute-start(bf16[432,128]{1,0:T(8,128)(2,1)S(1)} %hop.6.kept_ref), channel_id=1, source_target_pairs={{0,2},{2,0},{4,6},{6,4},{8,10},{10,8},{12,14},{14,12},{1,3},{3,1},... | collective-permute-start | bytes 331784 | tf_op jit(solution)/shard_map/ppermute | solution.py:405
  37.3 7.9 %collective-permute-start.6 = (bf16[16,3584]{1,0:T(8,128)(2,1)S(1)}, bf16[16,3584]{1,0:T(8,128)(2,1)S(1)}, u32[]{:S(2)}, u32[]{:S(2)}) collective-permute-start(bf16[16,3584]{1,0:T(8,128)(2,1)S(1)} %get-tuple-element.39), channel_id=1, source_target_pairs={{0,12},{2,14},{4,8},{6,10},{8,4},{10,6},{12,0},{14,2},{1,13},{3,15... | collective-permute-start | bytes 344072 | tf_op jit(solution)/shard_map/ppermute | solution.py:405
  40.4 4.8 %collective-permute-start.7 = (bf16[432,128]{1,0:T(8,128)(2,1)S(1)}, bf16[432,128]{1,0:T(8,128)(2,1)S(1)}, u32[]{:S(2)}, u32[]{:S(2)}) collective-permute-start(bf16[432,128]{1,0:T(8,128)(2,1)S(1)} %hop.5.near_ref), channel_id=1, source_target_pairs={{0,2},{2,0},{4,6},{6,4},{8,10},{10,8},{12,14},{14,12},{1,3},{3,1},... | collective-permute-start | bytes 331784 | tf_op jit(solution)/shard_map/ppermute | solution.py:405
  41.1 23.4 %slice-start = ((s8[8257536]{0:T(1024)(128)(4,1)}), s8[4194304]{0:T(1024)(128)(4,1)S(1)}, s32[]{:S(2)}) async-start(s8[8257536]{0:T(1024)(128)(4,1)} %bitcast.13), calls=%async_computation.2 | async-start | bytes 8388608
  45.3 1.5 %collective-permute-start.9 = (bf16[16,3584]{1,0:T(8,128)(2,1)S(1)}, bf16[16,3584]{1,0:T(8,128)(2,1)S(1)}, u32[]{:S(2)}, u32[]{:S(2)}) collective-permute-start(bf16[16,3584]{1,0:T(8,128)(2,1)S(1)} %last_add.1.own_ref), channel_id=1, source_target_pairs={{0,1},{1,0},{2,3},{3,2},{4,5},{5,4},{6,7},{7,6},{8,9},{9,8},{10,11... | collective-permute-start | bytes 344072 | tf_op jit(solution)/shard_map/ppermute | solution.py:346
  45.4 7.3 %collective-permute-start.10 = (bf16[432,128]{1,0:T(8,128)(2,1)S(1)}, bf16[432,128]{1,0:T(8,128)(2,1)S(1)}, u32[]{:S(2)}, u32[]{:S(2)}) collective-permute-start(bf16[432,128]{1,0:T(8,128)(2,1)S(1)} %hop.7.far_ref), channel_id=1, source_target_pairs={{0,12},{2,14},{4,8},{6,10},{8,4},{10,6},{12,0},{14,2},{1,13},{3,15... | collective-permute-start | bytes 331784 | tf_op jit(solution)/shard_map/ppermute | solution.py:405
  46.8 17.8 %slice-start.1 = ((s8[8257536]{0:T(1024)(128)(4,1)}), s8[4063232]{0:T(1024)(128)(4,1)S(1)}, s32[]{:S(2)}) async-start(s8[8257536]{0:T(1024)(128)(4,1)} %bitcast.13), calls=%async_computation.3 | async-start | bytes 8126464
  63.2 1.4 %collective-permute-start.11 = (bf16[8,72,128]{2,1,0:T(8,128)(2,1)S(1)}, bf16[8,72,128]{2,1,0:T(8,128)(2,1)S(1)}, u32[]{:S(2)}, u32[]{:S(2)}) collective-permute-start(bf16[8,72,128]{2,1,0:T(8,128)(2,1)S(1)} %all_to_all.11.own_ref), channel_id=1, source_target_pairs={{0,1},{1,0},{2,3},{3,2},{4,5},{5,4},{6,7},{7,6},{8,9},{9,8},{10,11... | collective-permute-start | bytes 442376 | tf_op jit(solution)/shard_map/ppermute | solution.py:346

commit v7 on v6

--- a/solution.py
+++ b/solution.py
@@ -173,8 +173,9 @@
     o_lat = (acc / total).astype(jnp.bfloat16)
     share = heads // n_dp
     upper = appended.T[half:]
-    near_ref[...] = pack(upper[: half // 2]).astype(jnp.bfloat16)
-    far_ref[...] = pack(upper[half // 2 :]).astype(jnp.bfloat16)
+    cut = near_ref.shape[0] * 128 // width
+    near_ref[...] = pack(upper[:cut]).astype(jnp.bfloat16)
+    far_ref[...] = pack(upper[cut:]).astype(jnp.bfloat16)
     for peer in range(n_dp):
         out_ref[peer] = o_lat[peer * share : (peer + 1) * share]
 
@@ -279,7 +280,6 @@
 
 def finish_kernel(n_sub, steps, moves, near_ref, near_come_ref, far_ref, far_come_ref, out_ref):
     rank, core, _ = place(n_sub)
-    rows = out_ref.shape[0] // 2
     width = out_ref.shape[1]
     wanted = rank == moves[core, 2]
     pairs = ((near_ref, near_come_ref), (far_ref, far_come_ref))
@@ -294,9 +294,9 @@
             kept = kept_ref[...].astype(jnp.float32)
             come = come_ref[...].astype(jnp.float32)
             picked = jnp.where(crosses(moves, core, step), come, kept)
-            out_ref[part * rows : (part + 1) * rows, :] = unpack(picked, rows, width).astype(
-                jnp.bfloat16
-            )
+            rows = kept_ref.shape[0] * 128 // width
+            first = part * (out_ref.shape[0] - rows)
+            out_ref[first : first + rows, :] = unpack(picked, rows, width).astype(jnp.bfloat16)
 
 
 def gate_up_kernel(
@@ -363,6 +363,7 @@
     requests = n_dp * n_sub
     units = w_gate.shape[1]
     cols = w_down.shape[1]
+    cut = half * 2//3 // 32 * 32
     scale = (vh + width - latent) ** (-0.5)
     bf16, f32 = jnp.bfloat16, jnp.float32
 
@@ -379,8 +380,8 @@
         out_shape=(
             jax.ShapeDtypeStruct((width, cap), bf16),
             jax.ShapeDtypeStruct((n_dp, share, latent), bf16),
-            jax.ShapeDtypeStruct((half // 2 * width // 128, 128), bf16),
-            jax.ShapeDtypeStruct((half // 2 * width // 128, 128), bf16),
+            jax.ShapeDtypeStruct((cut * width // 128, 128), bf16),
+            jax.ShapeDtypeStruct(((half - cut) * width // 128, 128), bf16),
         ),
         in_specs=[SMEM] * 2 + [VMEM] * 4,
         out_specs=(VMEM,) * 4,
@@ -452,6 +453,7 @@
     far = hop(2, far, far_come)
     near_come = cross(near, 2)
     total, part = add(total, cross(part, 1))
+    far, part = lax.optimization_barrier((far, part))
     near = hop(2, near, near_come)
     near_come = cross(near, 1)
     far_come = cross(far, 1)

time: 67.8 us -> 66.4 us (0.979)
  waiting for transfers between devices: 10.5 us -> 4.55 us
  starting transfers between devices: 9.86 us -> 14.1 us
    ppermute x9, waiting for transfers between devices: 10.3 us -> 4.54 us  [cross(): return lax.ppermute(x, 'dp', [(i, i ^ step) for i in range(n_dp)])]
    ppermute x9, starting transfers between devices: 9.72 us -> 14 us  [cross(): return lax.ppermute(x, 'dp', [(i, i ^ step) for i in range(n_dp)])]
  transfers between devices with their start and end apart: 12 -> 12, of which waited for: 6 -> 4; matrix products, arithmetic and copies ran while one was open for 0% -> 0% of each run, Pallas kernels for 23% -> 23%
where the time goes in v7:
time: 66.4 us; the launch traced here: 66.2 us
  blocking collectives  25.2 us (38%)
  Pallas kernels  20.4 us (31%)
  starting transfers between devices  14.1 us (21%)
  waiting for transfers between devices  4.55 us (7%)
  local copies, waits for them, and re-layouts  1.09 us (2%)
  between operations  0.9 us (1%)
    all_to_all x2, blocking collectives, exchange(): return lax.all_to_all(x, 'dp', split_axis=0, concat_axis=0, tiled=True)  25.2 us
    ppermute x9, starting transfers between devices, cross(): return lax.ppermute(x, 'dp', [(i, i ^ step) for i in range(n_dp)])  14 us
    pallas_call x1, Pallas kernels, per_device_fast(): pl.pallas_call(functools.partial(project_kernel, n_sub), out_shape=(jax.S...  6.76 us
    pallas_call x1, Pallas kernels, per_device_fast(): pl.pallas_call(functools.partial(gate_up_kernel, n_sub), out_shape=(jax.S...  4.7 us
    ppermute x9, waiting for transfers between devices, cross(): return lax.ppermute(x, 'dp', [(i, i ^ step) for i in range(n_dp)])  4.54 us
    pallas_call x1, Pallas kernels, per_device_fast(): pl.pallas_call(functools.partial(down_kernel, n_sub), out_shape=jax.Shape...  2.94 us
    pallas_call x4, Pallas kernels, hop(): pl.pallas_call(functools.partial(hop_kernel, n_sub, step), out_shape=jax....  2.35 us
    pallas_call x1, Pallas kernels, per_device_fast(): pl.pallas_call(functools.partial(attend_kernel, scale, n_dp, n_sub, laten...  1.64 us
  transfers between devices with their start and end apart: 12, of which 4 were waited for; matrix products, arithmetic and copies ran while one was open for 0% of the time, Pallas kernels for 23%

profile of v7, /device:TPU:0, one launch (start us, length us, event | category | flops | bytes accessed | tf_op | source)
XLA Modules:
  0.0 66.2 jit_solution(4590807512598002925)
XLA Ops:
  0.7 0.6 copy-done.6
  1.3 0.0 copy-done.7
  1.3 0.4 copy-done.2
  1.7 0.0 copy-done.3
  1.7 1.6 %attend.1 = (bf16[576,384]{1,0:T(8,128)(2,1)}, bf16[8,16,512]{2,1,0:T(8,128)(2,1)S(1)}, bf16[576,128]{1,0:T(8,128)(2,1)S(1)}, bf16[288,128]{1,0:T(8,128)(2,1)S(1)}) custom-call(s32[16]{0:T(128)S(1)} %copy-done.7, s32[2,3]{1,0:T(2,128)S(1)} %copy-done.6, s32[8,384]{1,0:T(8,128)S(1)} %positions.1.at_ref, bf16[576,128]{1,0:T(8,128)(2,1)S(1)} %bitcast.23, ...), custom_call_target="tpu_custom_call" | custom-call | flops 7549747200 | bytes 25165824 | tf_op jit(solution)/shard_map/attend/pallas_call | solution.py:378
  3.4 14.4 %all_to_all.10.got_ref = bf16[8,16,512]{2,1,0:T(8,128)(2,1)S(1)} all-to-all(bf16[8,16,512]{2,1,0:T(8,128)(2,1)S(1)} %get-tuple-element.29), channel_id=1, replica_groups=mesh['groups'=2,'dp'=8,'sub'=2] {'dp'}, dimensions={0} | all-to-all | bytes 262144 | tf_op jit(solution)/shard_map/all_to_all | solution.py:350
  17.8 0.0 copy-done.1
  17.8 0.5 values.1.own_ref
  18.2 0.0 slice-start.3
  18.3 0.0 slice-start.5
  18.3 0.0 copy-start.4
  18.3 0.1 collective-permute-start.2
  18.4 0.1 collective-permute-start.1
  18.4 1.8 %collective-permute-start = (bf16[576,128]{1,0:T(8,128)(2,1)S(1)}, bf16[576,128]{1,0:T(8,128)(2,1)S(1)}, u32[]{:S(2)}, u32[]{:S(2)}) collective-permute-start(bf16[576,128]{1,0:T(8,128)(2,1)S(1)} %get-tuple-element.32.kept_ref), channel_id=1, source_target_pairs={{0,12},{2,14},{4,8},{6,10},{8,4},{10,6},{12,0},{14,2},{1,13},{3,15... | collective-permute-start | bytes 442376 | tf_op jit(solution)/shard_map/ppermute | solution.py:406
  20.3 0.0 collective-permute-done.2.peer_ref
  20.3 6.8 %project.1 = (f32[16,3584]{1,0:T(8,128)S(1)}, bf16[16,3584]{1,0:T(8,128)(2,1)S(1)}) custom-call(bf16[8,2944]{1,0:T(8,128)(2,1)S(1)} %values.1.own_ref, bf16[8,2944]{1,0:T(8,128)(2,1)S(1)} %collective-permute-done.2.peer_ref, bf16[2048,7168]{1,0:T(8,128)(2,1)} %w_ref.1), custom_call_target="tpu_custom_call" | custom-call | flops 7549747200 | bytes 25165824 | tf_op jit(solution)/shard_map/project/pallas_call | solution.py:435
  27.1 0.0 collective-permute-done.1.come_ref
  27.1 0.0 collective-permute-done.come_ref
  27.1 0.5 collective-permute-start.4
  27.6 0.6 hop.4.kept_ref
  28.1 2.3 %collective-permute-start.3 = (bf16[576,128]{1,0:T(8,128)(2,1)S(1)}, bf16[576,128]{1,0:T(8,128)(2,1)S(1)}, u32[]{:S(2)}, u32[]{:S(2)}) collective-permute-start(bf16[576,128]{1,0:T(8,128)(2,1)S(1)} %hop.4.kept_ref), channel_id=1, source_target_pairs={{0,4},{2,6},{4,0},{6,2},{8,12},{10,14},{12,8},{14,10},{1,5},{3,7},... | collective-permute-start | bytes 442376 | tf_op jit(solution)/shard_map/ppermute | solution.py:406
  30.4 0.6 hop.6.kept_ref
  31.0 1.1 %collective-permute-done.4.peer_ref = bf16[16,3584]{1,0:T(8,128)(2,1)S(1)} collective-permute-done((bf16[16,3584]{1,0:T(8,128)(2,1)S(1)}, bf16[16,3584]{1,0:T(8,128)(2,1)S(1)}, u32[]{:S(2)}, u32[]{:S(2)}) %collective-permute-start.4) | collective-permute-done | bytes 114720 | tf_op jit(solution)/shard_map/ppermute | solution.py:406
  32.1 2.3 %collective-permute-start.5 = (bf16[16,3584]{1,0:T(8,128)(2,1)S(1)}, bf16[16,3584]{1,0:T(8,128)(2,1)S(1)}, u32[]{:S(2)}, u32[]{:S(2)}) collective-permute-start(bf16[16,3584]{1,0:T(8,128)(2,1)S(1)} %get-tuple-element.42), channel_id=1, source_target_pairs={{0,4},{2,6},{4,0},{6,2},{8,12},{10,14},{12,8},{14,10},{1,5},{3,7},... | collective-permute-start | bytes 344072 | tf_op jit(solution)/shard_map/ppermute | solution.py:406
  34.4 0.0 collective-permute-done.3.come_ref
  34.4 0.6 hop.5.near_ref
  35.0 2.1 %collective-permute-start.7 = (bf16[576,128]{1,0:T(8,128)(2,1)S(1)}, bf16[576,128]{1,0:T(8,128)(2,1)S(1)}, u32[]{:S(2)}, u32[]{:S(2)}) collective-permute-start(bf16[576,128]{1,0:T(8,128)(2,1)S(1)} %hop.5.near_ref), channel_id=1, source_target_pairs={{0,2},{2,0},{4,6},{6,4},{8,10},{10,8},{12,14},{14,12},{1,3},{3,1},... | collective-permute-start | bytes 442376 | tf_op jit(solution)/shard_map/ppermute | solution.py:406
  37.1 0.1 collective-permute-done.5.peer_ref
  37.2 1.7 %collective-permute-start.6 = (bf16[16,3584]{1,0:T(8,128)(2,1)S(1)}, bf16[16,3584]{1,0:T(8,128)(2,1)S(1)}, u32[]{:S(2)}, u32[]{:S(2)}) collective-permute-start(bf16[16,3584]{1,0:T(8,128)(2,1)S(1)} %get-tuple-element.43), channel_id=1, source_target_pairs={{0,12},{2,14},{4,8},{6,10},{8,4},{10,6},{12,0},{14,2},{1,13},{3,15... | collective-permute-start | bytes 344072 | tf_op jit(solution)/shard_map/ppermute | solution.py:406
  39.0 1.1 %collective-permute-start.8 = (bf16[288,128]{1,0:T(8,128)(2,1)S(1)}, bf16[288,128]{1,0:T(8,128)(2,1)S(1)}, u32[]{:S(2)}, u32[]{:S(2)}) collective-permute-start(bf16[288,128]{1,0:T(8,128)(2,1)S(1)} %hop.6.kept_ref), channel_id=1, source_target_pairs={{0,2},{2,0},{4,6},{6,4},{8,10},{10,8},{12,14},{14,12},{1,3},{3,1},... | collective-permute-start | bytes 221192 | tf_op jit(solution)/shard_map/ppermute | solution.py:406
  40.0 3.3 %collective-permute-done.8.come_ref = bf16[288,128]{1,0:T(8,128)(2,1)S(1)} collective-permute-done((bf16[288,128]{1,0:T(8,128)(2,1)S(1)}, bf16[288,128]{1,0:T(8,128)(2,1)S(1)}, u32[]{:S(2)}, u32[]{:S(2)}) %collective-permute-start.8) | collective-permute-done | bytes 73760 | tf_op jit(solution)/shard_map/ppermute | solution.py:406
  43.3 0.6 hop.7.far_ref
  43.9 0.0 collective-permute-done.7.near_come_ref
  43.9 0.1 collective-permute-done.6.peer_ref
  44.0 0.1 collective-permute-start.9
  44.1 2.2 %collective-permute-start.10 = (bf16[288,128]{1,0:T(8,128)(2,1)S(1)}, bf16[288,128]{1,0:T(8,128)(2,1)S(1)}, u32[]{:S(2)}, u32[]{:S(2)}) collective-permute-start(bf16[288,128]{1,0:T(8,128)(2,1)S(1)} %hop.7.far_ref), channel_id=1, source_target_pairs={{0,12},{2,14},{4,8},{6,10},{8,4},{10,6},{12,0},{14,2},{1,13},{3,15... | collective-permute-start | bytes 221192 | tf_op jit(solution)/shard_map/ppermute | solution.py:406
  46.3 0.0 collective-permute-done.9.peer_ref
  46.3 0.0 slice-done.4
  46.3 0.0 slice-done.3
  46.3 0.0 slice-done.5
  46.3 0.0 slice-start.1
  46.3 4.7 %gate_up.1 = (bf16[8,72,128]{2,1,0:T(8,128)(2,1)S(1)}, bf16[16,448]{1,0:T(8,128)(2,1)S(1)}) custom-call(bf16[16,3584]{1,0:T(8,128)(2,1)S(1)} %last_add.1.own_ref, bf16[16,3584]{1,0:T(8,128)(2,1)S(1)} %collective-permute-done.9.peer_ref, bf16[7168]{0:T(1024)(128)(2,1)S(1)} %copy-done.4, bf16[576,7168]{1,0:T(8,128)(2,1)S(1)} %bitcast.18, ...), custom_call_target="tpu_custom_call" | custom-call | flops 7549747200 | bytes 25165824 | tf_op jit(solution)/shard_map/gate_up/pallas_call | solution.py:473
  51.0 0.0 collective-permute-done.10.far_come_ref
  51.0 10.8 %all_to_all.11.own_ref = bf16[8,72,128]{2,1,0:T(8,128)(2,1)S(1)} all-to-all(bf16[8,72,128]{2,1,0:T(8,128)(2,1)S(1)} %get-tuple-element.51), channel_id=1, replica_groups=mesh['groups'=2,'dp'=8,'sub'=2] {'dp'}, dimensions={0} | all-to-all | bytes 294912 | tf_op jit(solution)/shard_map/all_to_all | solution.py:350
  61.9 0.0 collective-permute-start.11
  61.9 1.4 %finish.1 = bf16[192,576]{1,0:T(8,128)(2,1)} custom-call(s32[2,3]{1,0:T(2,128)S(1)} %copy-done.6, bf16[576,128]{1,0:T(8,128)(2,1)S(1)} %hop.5.near_ref, bf16[576,128]{1,0:T(8,128)(2,1)S(1)} %collective-permute-done.7.near_come_ref, bf16[288,128]{1,0:T(8,128)(2,1)S(1)} %hop.7.far_ref, bf16[288,128]{1,0:T(8,128)(2,1)S(1)} %collective-permute-done.10.far_come_ref), custom_call_target="tpu_custom_call" | custom-call | flops 314572800 | bytes 1048576 | tf_op jit(solution)/shard_map/finish/pallas_call | solution.py:498
  63.3 0.0 collective-permute-done.11.peer_ref
  63.3 2.9 %down.1 = bf16[16,448]{1,0:T(8,128)(2,1)} custom-call(bf16[8,72,128]{2,1,0:T(8,128)(2,1)S(1)} %all_to_all.11.own_ref, bf16[8,72,128]{2,1,0:T(8,128)(2,1)S(1)} %collective-permute-done.11.peer_ref, bf16[16,448]{1,0:T(8,128)(2,1)S(1)} %get-tuple-element.52.base_ref, bf16[448,9216]{1,0:T(8,128)(2,1)S(1)} %bitcast.15), custom_call_target="tpu_custom_call" | custom-call | flops 314572800 | bytes 1048576 | tf_op jit(solution)/shard_map/down/pallas_call | solution.py:488
  (23 shorter events, 0.1 us)
Async XLA Ops:
  0.6 0.7 %copy-start.6 = (s32[2,3]{1,0:T(2,128)S(1)}, s32[2,3]{1,0:T(2,128)}, u32[]{:S(2)}) copy-start(s32[2,3]{1,0:T(2,128)} %moves.11) | copy-start | bytes 76
  0.6 0.7 %copy-start.7 = (s32[16]{0:T(128)S(1)}, s32[16]{0:T(128)}, u32[]{:S(2)}) copy-start(s32[16]{0:T(128)} %lengths.1) | copy-start | bytes 196
  0.7 1.0 %copy-start.2 = (bf16[1,384,576]{1,2,0:T(8,128)(2,1)S(1)}, bf16[1,384,576]{1,2,0:T(8,128)(2,1)}, u32[]{:S(2)}) copy-start(bf16[1,384,576]{1,2,0:T(8,128)(2,1)} %param.14) | copy-start | bytes 1327108
  0.7 1.0 %copy-start.5 = (bf16[1,576]{1,0:T(2,128)(2,1)S(1)}, bf16[1,576]{1,0:T(2,128)(2,1)}, u32[]{:S(2)}) copy-start(bf16[1,576]{1,0:T(2,128)(2,1)} %fresh_ref.1) | copy-start | bytes 3460
  0.7 1.1 %copy-start.3 = (bf16[1,128,576]{1,2,0:T(8,128)(2,1)S(1)}, bf16[1,128,576]{1,2,0:T(8,128)(2,1)}, u32[]{:S(2)}) copy-start(bf16[1,128,576]{1,2,0:T(8,128)(2,1)} %param.12) | copy-start | bytes 442372
  1.7 16.0 %copy-start = (bf16[16,512,128]{2,1,0:T(8,128)(2,1)S(1)}, bf16[16,512,128]{2,1,0:T(8,128)(2,1)}, u32[]{:S(2)}) copy-start(bf16[16,512,128]{2,1,0:T(8,128)(2,1)} %uv_ref.1) | copy-start | bytes 6291460
  1.7 16.0 %copy-start.1 = (bf16[1,7168]{1,0:T(2,128)(2,1)S(1)}, bf16[1,7168]{1,0:T(2,128)(2,1)}, u32[]{:S(2)}) copy-start(bf16[1,7168]{1,0:T(2,128)(2,1)} %resid_ref.1) | copy-start | bytes 43012
  17.8 28.5 %slice-start.2 = ((s8[8257536]{0:T(1024)(128)(4,1)}), s8[4194304]{0:T(1024)(128)(4,1)S(1)}, s32[]{:S(2)}) async-start(s8[8257536]{0:T(1024)(128)(4,1)} %bitcast.16), calls=%async_computation.4 | async-start | bytes 8388608
  17.8 28.5 %slice-start.4 = ((s8[8257536]{0:T(1024)(128)(4,1)}), s8[4194304]{0:T(1024)(128)(4,1)S(1)}, s32[]{:S(2)}) async-start(s8[8257536]{0:T(1024)(128)(4,1)} %bitcast.19), calls=%async_computation.6 | async-start | bytes 8388608
  18.2 28.0 %slice-start.3 = ((s8[8257536]{0:T(1024)(128)(4,1)}), s8[4063232]{0:T(1024)(128)(4,1)S(1)}, s32[]{:S(2)}) async-start(s8[8257536]{0:T(1024)(128)(4,1)} %bitcast.16), calls=%async_computation.5 | async-start | bytes 8126464
  18.3 28.0 %slice-start.5 = ((s8[8257536]{0:T(1024)(128)(4,1)}), s8[4063232]{0:T(1024)(128)(4,1)S(1)}, s32[]{:S(2)}) async-start(s8[8257536]{0:T(1024)(128)(4,1)} %bitcast.19), calls=%async_computation.7 | async-start | bytes 8126464
  18.3 28.0 %copy-start.4 = (bf16[7168]{0:T(1024)(128)(2,1)S(1)}, bf16[7168]{0:T(1024)(128)(2,1)}, u32[]{:S(2)}) copy-start(bf16[7168]{0:T(1024)(128)(2,1)} %gain_ref.1) | copy-start | bytes 43012
  18.3 2.0 %collective-permute-start.2 = (bf16[8,2944]{1,0:T(8,128)(2,1)S(1)}, bf16[8,2944]{1,0:T(8,128)(2,1)S(1)}, u32[]{:S(2)}, u32[]{:S(2)}) collective-permute-start(bf16[8,2944]{1,0:T(8,128)(2,1)S(1)} %values.1.own_ref), channel_id=1, source_target_pairs={{0,1},{1,0},{2,3},{3,2},{4,5},{5,4},{6,7},{7,6},{8,9},{9,8},{10,11... | collective-permute-start | bytes 141320 | tf_op jit(solution)/shard_map/ppermute | solution.py:346
  18.4 8.7 %collective-permute-start.1 = (bf16[288,128]{1,0:T(8,128)(2,1)S(1)}, bf16[288,128]{1,0:T(8,128)(2,1)S(1)}, u32[]{:S(2)}, u32[]{:S(2)}) collective-permute-start(bf16[288,128]{1,0:T(8,128)(2,1)S(1)} %get-tuple-element.33.kept_ref), channel_id=1, source_target_pairs={{0,4},{2,6},{4,0},{6,2},{8,12},{10,14},{12,8},{14,10},{1,5},{3,7},... | collective-permute-start | bytes 221192 | tf_op jit(solution)/shard_map/ppermute | solution.py:406
  18.4 8.6 %collective-permute-start = (bf16[576,128]{1,0:T(8,128)(2,1)S(1)}, bf16[576,128]{1,0:T(8,128)(2,1)S(1)}, u32[]{:S(2)}, u32[]{:S(2)}) collective-permute-start(bf16[576,128]{1,0:T(8,128)(2,1)S(1)} %get-tuple-element.32.kept_ref), channel_id=1, source_target_pairs={{0,12},{2,14},{4,8},{6,10},{8,4},{10,6},{12,0},{14,2},{1,13},{3,15... | collective-permute-start | bytes 442376 | tf_op jit(solution)/shard_map/ppermute | solution.py:406
  27.1 5.0 %collective-permute-start.4 = (bf16[16,3584]{1,0:T(8,128)(2,1)S(1)}, bf16[16,3584]{1,0:T(8,128)(2,1)S(1)}, u32[]{:S(2)}, u32[]{:S(2)}) collective-permute-start(bf16[16,3584]{1,0:T(8,128)(2,1)S(1)} %get-tuple-element.38), channel_id=1, source_target_pairs={{0,2},{2,0},{4,6},{6,4},{8,10},{10,8},{12,14},{14,12},{1,3},{3,1},... | collective-permute-start | bytes 344072 | tf_op jit(solution)/shard_map/ppermute | solution.py:406
  28.1 6.3 %collective-permute-start.3 = (bf16[576,128]{1,0:T(8,128)(2,1)S(1)}, bf16[576,128]{1,0:T(8,128)(2,1)S(1)}, u32[]{:S(2)}, u32[]{:S(2)}) collective-permute-start(bf16[576,128]{1,0:T(8,128)(2,1)S(1)} %hop.4.kept_ref), channel_id=1, source_target_pairs={{0,4},{2,6},{4,0},{6,2},{8,12},{10,14},{12,8},{14,10},{1,5},{3,7},... | collective-permute-start | bytes 442376 | tf_op jit(solution)/shard_map/ppermute | solution.py:406
  32.1 5.1 %collective-permute-start.5 = (bf16[16,3584]{1,0:T(8,128)(2,1)S(1)}, bf16[16,3584]{1,0:T(8,128)(2,1)S(1)}, u32[]{:S(2)}, u32[]{:S(2)}) collective-permute-start(bf16[16,3584]{1,0:T(8,128)(2,1)S(1)} %get-tuple-element.42), channel_id=1, source_target_pairs={{0,4},{2,6},{4,0},{6,2},{8,12},{10,14},{12,8},{14,10},{1,5},{3,7},... | collective-permute-start | bytes 344072 | tf_op jit(solution)/shard_map/ppermute | solution.py:406
  35.0 8.9 %collective-permute-start.7 = (bf16[576,128]{1,0:T(8,128)(2,1)S(1)}, bf16[576,128]{1,0:T(8,128)(2,1)S(1)}, u32[]{:S(2)}, u32[]{:S(2)}) collective-permute-start(bf16[576,128]{1,0:T(8,128)(2,1)S(1)} %hop.5.near_ref), channel_id=1, source_target_pairs={{0,2},{2,0},{4,6},{6,4},{8,10},{10,8},{12,14},{14,12},{1,3},{3,1},... | collective-permute-start | bytes 442376 | tf_op jit(solution)/shard_map/ppermute | solution.py:406
  37.2 6.8 %collective-permute-start.6 = (bf16[16,3584]{1,0:T(8,128)(2,1)S(1)}, bf16[16,3584]{1,0:T(8,128)(2,1)S(1)}, u32[]{:S(2)}, u32[]{:S(2)}) collective-permute-start(bf16[16,3584]{1,0:T(8,128)(2,1)S(1)} %get-tuple-element.43), channel_id=1, source_target_pairs={{0,12},{2,14},{4,8},{6,10},{8,4},{10,6},{12,0},{14,2},{1,13},{3,15... | collective-permute-start | bytes 344072 | tf_op jit(solution)/shard_map/ppermute | solution.py:406
  39.0 4.4 %collective-permute-start.8 = (bf16[288,128]{1,0:T(8,128)(2,1)S(1)}, bf16[288,128]{1,0:T(8,128)(2,1)S(1)}, u32[]{:S(2)}, u32[]{:S(2)}) collective-permute-start(bf16[288,128]{1,0:T(8,128)(2,1)S(1)} %hop.6.kept_ref), channel_id=1, source_target_pairs={{0,2},{2,0},{4,6},{6,4},{8,10},{10,8},{12,14},{14,12},{1,3},{3,1},... | collective-permute-start | bytes 221192 | tf_op jit(solution)/shard_map/ppermute | solution.py:406
  43.3 20.0 %slice-start = ((s8[8257536]{0:T(1024)(128)(4,1)}), s8[4194304]{0:T(1024)(128)(4,1)S(1)}, s32[]{:S(2)}) async-start(s8[8257536]{0:T(1024)(128)(4,1)} %bitcast.13), calls=%async_computation.2 | async-start | bytes 8388608
  44.0 2.2 %collective-permute-start.9 = (bf16[16,3584]{1,0:T(8,128)(2,1)S(1)}, bf16[16,3584]{1,0:T(8,128)(2,1)S(1)}, u32[]{:S(2)}, u32[]{:S(2)}) collective-permute-start(bf16[16,3584]{1,0:T(8,128)(2,1)S(1)} %last_add.1.own_ref), channel_id=1, source_target_pairs={{0,1},{1,0},{2,3},{3,2},{4,5},{5,4},{6,7},{7,6},{8,9},{9,8},{10,11... | collective-permute-start | bytes 344072 | tf_op jit(solution)/shard_map/ppermute | solution.py:346
  44.1 6.9 %collective-permute-start.10 = (bf16[288,128]{1,0:T(8,128)(2,1)S(1)}, bf16[288,128]{1,0:T(8,128)(2,1)S(1)}, u32[]{:S(2)}, u32[]{:S(2)}) collective-permute-start(bf16[288,128]{1,0:T(8,128)(2,1)S(1)} %hop.7.far_ref), channel_id=1, source_target_pairs={{0,12},{2,14},{4,8},{6,10},{8,4},{10,6},{12,0},{14,2},{1,13},{3,15... | collective-permute-start | bytes 221192 | tf_op jit(solution)/shard_map/ppermute | solution.py:406
  46.3 17.0 %slice-start.1 = ((s8[8257536]{0:T(1024)(128)(4,1)}), s8[4063232]{0:T(1024)(128)(4,1)S(1)}, s32[]{:S(2)}) async-start(s8[8257536]{0:T(1024)(128)(4,1)} %bitcast.13), calls=%async_computation.3 | async-start | bytes 8126464
  61.9 1.4 %collective-permute-start.11 = (bf16[8,72,128]{2,1,0:T(8,128)(2,1)S(1)}, bf16[8,72,128]{2,1,0:T(8,128)(2,1)S(1)}, u32[]{:S(2)}, u32[]{:S(2)}) collective-permute-start(bf16[8,72,128]{2,1,0:T(8,128)(2,1)S(1)} %all_to_all.11.own_ref), channel_id=1, source_target_pairs={{0,1},{1,0},{2,3},{3,2},{4,5},{5,4},{6,7},{7,6},{8,9},{9,8},{10,11... | collective-permute-start | bytes 442376 | tf_op jit(solution)/shard_map/ppermute | solution.py:346

commit v8 on v7

--- a/solution.py
+++ b/solution.py
@@ -189,8 +189,10 @@
                 src, 0:share, 128 * k : 128 * (k + 1)
             ].astype(jnp.float32)
     piece = resid_ref.shape[1] // n_dp
-    for src in range(n_dp):
-        out_ref[src : src + 1, share * vh :] = resid_ref[:, src * piece : (src + 1) * piece]
+    row = resid_ref[...].astype(jnp.float32)
+    out_ref[:, share * vh :] = jnp.concatenate(
+        [row[:, src * piece : (src + 1) * piece] for src in range(n_dp)], axis=0
+    ).astype(jnp.bfloat16)
     for head in range(share):
         rows = jnp.concatenate(
             [wide[k, pl.ds(head, n_dp, stride=share), :] for k in range(latent // 128)], axis=1

time: 66.4 us -> 66.4 us (level)
  transfers between devices with their start and end apart: 12 -> 12, of which waited for: 4 -> 3; matrix products, arithmetic and copies ran while one was open for 0% -> 0% of each run, Pallas kernels for 23% -> 23%
where the time goes in v8:
time: 66.4 us; the launch traced here: 66.2 us
  blocking collectives  25.2 us (38%)
  Pallas kernels  20.4 us (31%)
  starting transfers between devices  14.1 us (21%)
  waiting for transfers between devices  4.55 us (7%)
  local copies, waits for them, and re-layouts  1.08 us (2%)
  between operations  0.89 us (1%)
    all_to_all x2, blocking collectives, exchange(): return lax.all_to_all(x, 'dp', split_axis=0, concat_axis=0, tiled=True)  25.2 us
    ppermute x9, starting transfers between devices, cross(): return lax.ppermute(x, 'dp', [(i, i ^ step) for i in range(n_dp)])  14 us
    pallas_call x1, Pallas kernels, per_device_fast(): pl.pallas_call(functools.partial(project_kernel, n_sub), out_shape=(jax.S...  6.76 us
    pallas_call x1, Pallas kernels, per_device_fast(): pl.pallas_call(functools.partial(gate_up_kernel, n_sub), out_shape=(jax.S...  4.69 us
    ppermute x9, waiting for transfers between devices, cross(): return lax.ppermute(x, 'dp', [(i, i ^ step) for i in range(n_dp)])  4.54 us
    pallas_call x1, Pallas kernels, per_device_fast(): pl.pallas_call(functools.partial(down_kernel, n_sub), out_shape=jax.Shape...  2.94 us
    pallas_call x4, Pallas kernels, hop(): pl.pallas_call(functools.partial(hop_kernel, n_sub, step), out_shape=jax....  2.35 us
    pallas_call x1, Pallas kernels, per_device_fast(): pl.pallas_call(functools.partial(attend_kernel, scale, n_dp, n_sub, laten...  1.64 us
  transfers between devices with their start and end apart: 12, of which 3 were waited for; matrix products, arithmetic and copies ran while one was open for 0% of the time, Pallas kernels for 23%

profile of v8, /device:TPU:0, one launch (start us, length us, event | category | flops | bytes accessed | tf_op | source)
XLA Modules:
  0.0 66.2 jit_solution(11742623176674384149)
XLA Ops:
  0.6 0.0 copy-start.6
  0.6 0.0 copy-start.7
  0.7 0.0 copy-start.2
  0.7 0.0 copy-start.5
  0.7 0.0 copy-start.3
  0.7 0.6 copy-done.6
  1.3 0.4 copy-done.2
  1.7 0.0 copy-done.3
  1.7 1.6 %attend.1 = (bf16[576,384]{1,0:T(8,128)(2,1)}, bf16[8,16,512]{2,1,0:T(8,128)(2,1)S(1)}, bf16[576,128]{1,0:T(8,128)(2,1)S(1)}, bf16[288,128]{1,0:T(8,128)(2,1)S(1)}) custom-call(s32[16]{0:T(128)S(1)} %copy-done.7, s32[2,3]{1,0:T(2,128)S(1)} %copy-done.6, s32[8,384]{1,0:T(8,128)S(1)} %positions.1.at_ref, bf16[576,128]{1,0:T(8,128)(2,1)S(1)} %bitcast.23, ...), custom_call_target="tpu_custom_call" | custom-call | flops 7549747200 | bytes 25165824 | tf_op jit(solution)/shard_map/attend/pallas_call | solution.py:380
  3.4 14.4 %all_to_all.10.got_ref = bf16[8,16,512]{2,1,0:T(8,128)(2,1)S(1)} all-to-all(bf16[8,16,512]{2,1,0:T(8,128)(2,1)S(1)} %get-tuple-element.29), channel_id=1, replica_groups=mesh['groups'=2,'dp'=8,'sub'=2] {'dp'}, dimensions={0} | all-to-all | bytes 262144 | tf_op jit(solution)/shard_map/all_to_all | solution.py:352
  17.8 0.5 values.1.own_ref
  18.2 0.0 slice-start.3
  18.2 0.0 slice-start.5
  18.3 0.0 copy-start.4
  18.3 0.1 collective-permute-start.2
  18.4 0.1 collective-permute-start.1
  18.4 1.8 %collective-permute-start = (bf16[576,128]{1,0:T(8,128)(2,1)S(1)}, bf16[576,128]{1,0:T(8,128)(2,1)S(1)}, u32[]{:S(2)}, u32[]{:S(2)}) collective-permute-start(bf16[576,128]{1,0:T(8,128)(2,1)S(1)} %get-tuple-element.32.kept_ref), channel_id=1, source_target_pairs={{0,12},{2,14},{4,8},{6,10},{8,4},{10,6},{12,0},{14,2},{1,13},{3,15... | collective-permute-start | bytes 442376 | tf_op jit(solution)/shard_map/ppermute | solution.py:408
  20.3 0.0 collective-permute-done.2.peer_ref
  20.3 6.8 %project.1 = (f32[16,3584]{1,0:T(8,128)S(1)}, bf16[16,3584]{1,0:T(8,128)(2,1)S(1)}) custom-call(bf16[8,2944]{1,0:T(8,128)(2,1)S(1)} %values.1.own_ref, bf16[8,2944]{1,0:T(8,128)(2,1)S(1)} %collective-permute-done.2.peer_ref, bf16[2048,7168]{1,0:T(8,128)(2,1)} %w_ref.1), custom_call_target="tpu_custom_call" | custom-call | flops 7549747200 | bytes 25165824 | tf_op jit(solution)/shard_map/project/pallas_call | solution.py:437
  27.0 0.0 collective-permute-done.1.come_ref
  27.0 0.0 collective-permute-done.come_ref
  27.1 0.5 collective-permute-start.4
  27.5 0.6 hop.4.kept_ref
  28.1 2.3 %collective-permute-start.3 = (bf16[576,128]{1,0:T(8,128)(2,1)S(1)}, bf16[576,128]{1,0:T(8,128)(2,1)S(1)}, u32[]{:S(2)}, u32[]{:S(2)}) collective-permute-start(bf16[576,128]{1,0:T(8,128)(2,1)S(1)} %hop.4.kept_ref), channel_id=1, source_target_pairs={{0,4},{2,6},{4,0},{6,2},{8,12},{10,14},{12,8},{14,10},{1,5},{3,7},... | collective-permute-start | bytes 442376 | tf_op jit(solution)/shard_map/ppermute | solution.py:408
  30.4 0.6 hop.6.kept_ref
  31.0 1.1 %collective-permute-done.4.peer_ref = bf16[16,3584]{1,0:T(8,128)(2,1)S(1)} collective-permute-done((bf16[16,3584]{1,0:T(8,128)(2,1)S(1)}, bf16[16,3584]{1,0:T(8,128)(2,1)S(1)}, u32[]{:S(2)}, u32[]{:S(2)}) %collective-permute-start.4) | collective-permute-done | bytes 114720 | tf_op jit(solution)/shard_map/ppermute | solution.py:408
  32.1 2.3 %collective-permute-start.5 = (bf16[16,3584]{1,0:T(8,128)(2,1)S(1)}, bf16[16,3584]{1,0:T(8,128)(2,1)S(1)}, u32[]{:S(2)}, u32[]{:S(2)}) collective-permute-start(bf16[16,3584]{1,0:T(8,128)(2,1)S(1)} %get-tuple-element.42), channel_id=1, source_target_pairs={{0,4},{2,6},{4,0},{6,2},{8,12},{10,14},{12,8},{14,10},{1,5},{3,7},... | collective-permute-start | bytes 344072 | tf_op jit(solution)/shard_map/ppermute | solution.py:408
  34.4 0.0 collective-permute-done.3.come_ref
  34.4 0.6 hop.5.near_ref
  35.0 2.1 %collective-permute-start.7 = (bf16[576,128]{1,0:T(8,128)(2,1)S(1)}, bf16[576,128]{1,0:T(8,128)(2,1)S(1)}, u32[]{:S(2)}, u32[]{:S(2)}) collective-permute-start(bf16[576,128]{1,0:T(8,128)(2,1)S(1)} %hop.5.near_ref), channel_id=1, source_target_pairs={{0,2},{2,0},{4,6},{6,4},{8,10},{10,8},{12,14},{14,12},{1,3},{3,1},... | collective-permute-start | bytes 442376 | tf_op jit(solution)/shard_map/ppermute | solution.py:408
  37.1 0.1 collective-permute-done.5.peer_ref
  37.2 1.8 %collective-permute-start.6 = (bf16[16,3584]{1,0:T(8,128)(2,1)S(1)}, bf16[16,3584]{1,0:T(8,128)(2,1)S(1)}, u32[]{:S(2)}, u32[]{:S(2)}) collective-permute-start(bf16[16,3584]{1,0:T(8,128)(2,1)S(1)} %get-tuple-element.43), channel_id=1, source_target_pairs={{0,12},{2,14},{4,8},{6,10},{8,4},{10,6},{12,0},{14,2},{1,13},{3,15... | collective-permute-start | bytes 344072 | tf_op jit(solution)/shard_map/ppermute | solution.py:408
  39.0 1.0 %collective-permute-start.8 = (bf16[288,128]{1,0:T(8,128)(2,1)S(1)}, bf16[288,128]{1,0:T(8,128)(2,1)S(1)}, u32[]{:S(2)}, u32[]{:S(2)}) collective-permute-start(bf16[288,128]{1,0:T(8,128)(2,1)S(1)} %hop.6.kept_ref), channel_id=1, source_target_pairs={{0,2},{2,0},{4,6},{6,4},{8,10},{10,8},{12,14},{14,12},{1,3},{3,1},... | collective-permute-start | bytes 221192 | tf_op jit(solution)/shard_map/ppermute | solution.py:408
  40.0 3.3 %collective-permute-done.8.come_ref = bf16[288,128]{1,0:T(8,128)(2,1)S(1)} collective-permute-done((bf16[288,128]{1,0:T(8,128)(2,1)S(1)}, bf16[288,128]{1,0:T(8,128)(2,1)S(1)}, u32[]{:S(2)}, u32[]{:S(2)}) %collective-permute-start.8) | collective-permute-done | bytes 73760 | tf_op jit(solution)/shard_map/ppermute | solution.py:408
  43.3 0.6 hop.7.far_ref
  43.9 0.0 collective-permute-done.7.near_come_ref
  43.9 0.0 collective-permute-done.6.peer_ref
  44.0 0.1 collective-permute-start.9
  44.1 2.2 %collective-permute-start.10 = (bf16[288,128]{1,0:T(8,128)(2,1)S(1)}, bf16[288,128]{1,0:T(8,128)(2,1)S(1)}, u32[]{:S(2)}, u32[]{:S(2)}) collective-permute-start(bf16[288,128]{1,0:T(8,128)(2,1)S(1)} %hop.7.far_ref), channel_id=1, source_target_pairs={{0,12},{2,14},{4,8},{6,10},{8,4},{10,6},{12,0},{14,2},{1,13},{3,15... | collective-permute-start | bytes 221192 | tf_op jit(solution)/shard_map/ppermute | solution.py:408
  46.2 0.0 collective-permute-done.9.peer_ref
  46.3 0.0 slice-start.1
  46.3 4.7 %gate_up.1 = (bf16[8,72,128]{2,1,0:T(8,128)(2,1)S(1)}, bf16[16,448]{1,0:T(8,128)(2,1)S(1)}) custom-call(bf16[16,3584]{1,0:T(8,128)(2,1)S(1)} %last_add.1.own_ref, bf16[16,3584]{1,0:T(8,128)(2,1)S(1)} %collective-permute-done.9.peer_ref, bf16[7168]{0:T(1024)(128)(2,1)S(1)} %copy-done.4, bf16[576,7168]{1,0:T(8,128)(2,1)S(1)} %bitcast.18, ...), custom_call_target="tpu_custom_call" | custom-call | flops 7549747200 | bytes 25165824 | tf_op jit(solution)/shard_map/gate_up/pallas_call | solution.py:475
  51.0 0.0 collective-permute-done.10.far_come_ref
  51.0 10.8 %all_to_all.11.own_ref = bf16[8,72,128]{2,1,0:T(8,128)(2,1)S(1)} all-to-all(bf16[8,72,128]{2,1,0:T(8,128)(2,1)S(1)} %get-tuple-element.51), channel_id=1, replica_groups=mesh['groups'=2,'dp'=8,'sub'=2] {'dp'}, dimensions={0} | all-to-all | bytes 294912 | tf_op jit(solution)/shard_map/all_to_all | solution.py:352
  61.9 0.0 collective-permute-start.11
  61.9 1.4 %finish.1 = bf16[192,576]{1,0:T(8,128)(2,1)} custom-call(s32[2,3]{1,0:T(2,128)S(1)} %copy-done.6, bf16[576,128]{1,0:T(8,128)(2,1)S(1)} %hop.5.near_ref, bf16[576,128]{1,0:T(8,128)(2,1)S(1)} %collective-permute-done.7.near_come_ref, bf16[288,128]{1,0:T(8,128)(2,1)S(1)} %hop.7.far_ref, bf16[288,128]{1,0:T(8,128)(2,1)S(1)} %collective-permute-done.10.far_come_ref), custom_call_target="tpu_custom_call" | custom-call | flops 314572800 | bytes 1048576 | tf_op jit(solution)/shard_map/finish/pallas_call | solution.py:500
  63.3 0.0 collective-permute-done.11.peer_ref
  63.3 2.9 %down.1 = bf16[16,448]{1,0:T(8,128)(2,1)} custom-call(bf16[8,72,128]{2,1,0:T(8,128)(2,1)S(1)} %all_to_all.11.own_ref, bf16[8,72,128]{2,1,0:T(8,128)(2,1)S(1)} %collective-permute-done.11.peer_ref, bf16[16,448]{1,0:T(8,128)(2,1)S(1)} %get-tuple-element.52.base_ref, bf16[448,9216]{1,0:T(8,128)(2,1)S(1)} %bitcast.15), custom_call_target="tpu_custom_call" | custom-call | flops 314572800 | bytes 1048576 | tf_op jit(solution)/shard_map/down/pallas_call | solution.py:490
  (23 shorter events, 0.1 us)
Async XLA Ops:
  0.6 0.7 %copy-start.6 = (s32[2,3]{1,0:T(2,128)S(1)}, s32[2,3]{1,0:T(2,128)}, u32[]{:S(2)}) copy-start(s32[2,3]{1,0:T(2,128)} %moves.11) | copy-start | bytes 76
  0.6 0.7 %copy-start.7 = (s32[16]{0:T(128)S(1)}, s32[16]{0:T(128)}, u32[]{:S(2)}) copy-start(s32[16]{0:T(128)} %lengths.1) | copy-start | bytes 196
  0.7 1.0 %copy-start.2 = (bf16[1,384,576]{1,2,0:T(8,128)(2,1)S(1)}, bf16[1,384,576]{1,2,0:T(8,128)(2,1)}, u32[]{:S(2)}) copy-start(bf16[1,384,576]{1,2,0:T(8,128)(2,1)} %param.14) | copy-start | bytes 1327108
  0.7 1.0 %copy-start.5 = (bf16[1,576]{1,0:T(2,128)(2,1)S(1)}, bf16[1,576]{1,0:T(2,128)(2,1)}, u32[]{:S(2)}) copy-start(bf16[1,576]{1,0:T(2,128)(2,1)} %fresh_ref.1) | copy-start | bytes 3460
  0.7 1.1 %copy-start.3 = (bf16[1,128,576]{1,2,0:T(8,128)(2,1)S(1)}, bf16[1,128,576]{1,2,0:T(8,128)(2,1)}, u32[]{:S(2)}) copy-start(bf16[1,128,576]{1,2,0:T(8,128)(2,1)} %param.12) | copy-start | bytes 442372
  1.7 16.0 %copy-start = (bf16[16,512,128]{2,1,0:T(8,128)(2,1)S(1)}, bf16[16,512,128]{2,1,0:T(8,128)(2,1)}, u32[]{:S(2)}) copy-start(bf16[16,512,128]{2,1,0:T(8,128)(2,1)} %uv_ref.1) | copy-start | bytes 6291460
  1.7 16.0 %copy-start.1 = (bf16[1,7168]{1,0:T(2,128)(2,1)S(1)}, bf16[1,7168]{1,0:T(2,128)(2,1)}, u32[]{:S(2)}) copy-start(bf16[1,7168]{1,0:T(2,128)(2,1)} %resid_ref.1) | copy-start | bytes 43012
  17.8 28.5 %slice-start.2 = ((s8[8257536]{0:T(1024)(128)(4,1)}), s8[4194304]{0:T(1024)(128)(4,1)S(1)}, s32[]{:S(2)}) async-start(s8[8257536]{0:T(1024)(128)(4,1)} %bitcast.16), calls=%async_computation.4 | async-start | bytes 8388608
  17.8 28.5 %slice-start.4 = ((s8[8257536]{0:T(1024)(128)(4,1)}), s8[4194304]{0:T(1024)(128)(4,1)S(1)}, s32[]{:S(2)}) async-start(s8[8257536]{0:T(1024)(128)(4,1)} %bitcast.19), calls=%async_computation.6 | async-start | bytes 8388608
  18.2 28.0 %slice-start.3 = ((s8[8257536]{0:T(1024)(128)(4,1)}), s8[4063232]{0:T(1024)(128)(4,1)S(1)}, s32[]{:S(2)}) async-start(s8[8257536]{0:T(1024)(128)(4,1)} %bitcast.16), calls=%async_computation.5 | async-start | bytes 8126464
  18.2 28.0 %slice-start.5 = ((s8[8257536]{0:T(1024)(128)(4,1)}), s8[4063232]{0:T(1024)(128)(4,1)S(1)}, s32[]{:S(2)}) async-start(s8[8257536]{0:T(1024)(128)(4,1)} %bitcast.19), calls=%async_computation.7 | async-start | bytes 8126464
  18.3 28.0 %copy-start.4 = (bf16[7168]{0:T(1024)(128)(2,1)S(1)}, bf16[7168]{0:T(1024)(128)(2,1)}, u32[]{:S(2)}) copy-start(bf16[7168]{0:T(1024)(128)(2,1)} %gain_ref.1) | copy-start | bytes 43012
  18.3 2.0 %collective-permute-start.2 = (bf16[8,2944]{1,0:T(8,128)(2,1)S(1)}, bf16[8,2944]{1,0:T(8,128)(2,1)S(1)}, u32[]{:S(2)}, u32[]{:S(2)}) collective-permute-start(bf16[8,2944]{1,0:T(8,128)(2,1)S(1)} %values.1.own_ref), channel_id=1, source_target_pairs={{0,1},{1,0},{2,3},{3,2},{4,5},{5,4},{6,7},{7,6},{8,9},{9,8},{10,11... | collective-permute-start | bytes 141320 | tf_op jit(solution)/shard_map/ppermute | solution.py:348
  18.4 8.7 %collective-permute-start.1 = (bf16[288,128]{1,0:T(8,128)(2,1)S(1)}, bf16[288,128]{1,0:T(8,128)(2,1)S(1)}, u32[]{:S(2)}, u32[]{:S(2)}) collective-permute-start(bf16[288,128]{1,0:T(8,128)(2,1)S(1)} %get-tuple-element.33.kept_ref), channel_id=1, source_target_pairs={{0,4},{2,6},{4,0},{6,2},{8,12},{10,14},{12,8},{14,10},{1,5},{3,7},... | collective-permute-start | bytes 221192 | tf_op jit(solution)/shard_map/ppermute | solution.py:408
  18.4 8.6 %collective-permute-start = (bf16[576,128]{1,0:T(8,128)(2,1)S(1)}, bf16[576,128]{1,0:T(8,128)(2,1)S(1)}, u32[]{:S(2)}, u32[]{:S(2)}) collective-permute-start(bf16[576,128]{1,0:T(8,128)(2,1)S(1)} %get-tuple-element.32.kept_ref), channel_id=1, source_target_pairs={{0,12},{2,14},{4,8},{6,10},{8,4},{10,6},{12,0},{14,2},{1,13},{3,15... | collective-permute-start | bytes 442376 | tf_op jit(solution)/shard_map/ppermute | solution.py:408
  27.1 5.0 %collective-permute-start.4 = (bf16[16,3584]{1,0:T(8,128)(2,1)S(1)}, bf16[16,3584]{1,0:T(8,128)(2,1)S(1)}, u32[]{:S(2)}, u32[]{:S(2)}) collective-permute-start(bf16[16,3584]{1,0:T(8,128)(2,1)S(1)} %get-tuple-element.38), channel_id=1, source_target_pairs={{0,2},{2,0},{4,6},{6,4},{8,10},{10,8},{12,14},{14,12},{1,3},{3,1},... | collective-permute-start | bytes 344072 | tf_op jit(solution)/shard_map/ppermute | solution.py:408
  28.1 6.3 %collective-permute-start.3 = (bf16[576,128]{1,0:T(8,128)(2,1)S(1)}, bf16[576,128]{1,0:T(8,128)(2,1)S(1)}, u32[]{:S(2)}, u32[]{:S(2)}) collective-permute-start(bf16[576,128]{1,0:T(8,128)(2,1)S(1)} %hop.4.kept_ref), channel_id=1, source_target_pairs={{0,4},{2,6},{4,0},{6,2},{8,12},{10,14},{12,8},{14,10},{1,5},{3,7},... | collective-permute-start | bytes 442376 | tf_op jit(solution)/shard_map/ppermute | solution.py:408
  32.1 5.1 %collective-permute-start.5 = (bf16[16,3584]{1,0:T(8,128)(2,1)S(1)}, bf16[16,3584]{1,0:T(8,128)(2,1)S(1)}, u32[]{:S(2)}, u32[]{:S(2)}) collective-permute-start(bf16[16,3584]{1,0:T(8,128)(2,1)S(1)} %get-tuple-element.42), channel_id=1, source_target_pairs={{0,4},{2,6},{4,0},{6,2},{8,12},{10,14},{12,8},{14,10},{1,5},{3,7},... | collective-permute-start | bytes 344072 | tf_op jit(solution)/shard_map/ppermute | solution.py:408
  35.0 8.9 %collective-permute-start.7 = (bf16[576,128]{1,0:T(8,128)(2,1)S(1)}, bf16[576,128]{1,0:T(8,128)(2,1)S(1)}, u32[]{:S(2)}, u32[]{:S(2)}) collective-permute-start(bf16[576,128]{1,0:T(8,128)(2,1)S(1)} %hop.5.near_ref), channel_id=1, source_target_pairs={{0,2},{2,0},{4,6},{6,4},{8,10},{10,8},{12,14},{14,12},{1,3},{3,1},... | collective-permute-start | bytes 442376 | tf_op jit(solution)/shard_map/ppermute | solution.py:408
  37.2 6.8 %collective-permute-start.6 = (bf16[16,3584]{1,0:T(8,128)(2,1)S(1)}, bf16[16,3584]{1,0:T(8,128)(2,1)S(1)}, u32[]{:S(2)}, u32[]{:S(2)}) collective-permute-start(bf16[16,3584]{1,0:T(8,128)(2,1)S(1)} %get-tuple-element.43), channel_id=1, source_target_pairs={{0,12},{2,14},{4,8},{6,10},{8,4},{10,6},{12,0},{14,2},{1,13},{3,15... | collective-permute-start | bytes 344072 | tf_op jit(solution)/shard_map/ppermute | solution.py:408
  39.0 4.4 %collective-permute-start.8 = (bf16[288,128]{1,0:T(8,128)(2,1)S(1)}, bf16[288,128]{1,0:T(8,128)(2,1)S(1)}, u32[]{:S(2)}, u32[]{:S(2)}) collective-permute-start(bf16[288,128]{1,0:T(8,128)(2,1)S(1)} %hop.6.kept_ref), channel_id=1, source_target_pairs={{0,2},{2,0},{4,6},{6,4},{8,10},{10,8},{12,14},{14,12},{1,3},{3,1},... | collective-permute-start | bytes 221192 | tf_op jit(solution)/shard_map/ppermute | solution.py:408
  43.3 19.9 %slice-start = ((s8[8257536]{0:T(1024)(128)(4,1)}), s8[4194304]{0:T(1024)(128)(4,1)S(1)}, s32[]{:S(2)}) async-start(s8[8257536]{0:T(1024)(128)(4,1)} %bitcast.13), calls=%async_computation.2 | async-start | bytes 8388608
  44.0 2.2 %collective-permute-start.9 = (bf16[16,3584]{1,0:T(8,128)(2,1)S(1)}, bf16[16,3584]{1,0:T(8,128)(2,1)S(1)}, u32[]{:S(2)}, u32[]{:S(2)}) collective-permute-start(bf16[16,3584]{1,0:T(8,128)(2,1)S(1)} %last_add.1.own_ref), channel_id=1, source_target_pairs={{0,1},{1,0},{2,3},{3,2},{4,5},{5,4},{6,7},{7,6},{8,9},{9,8},{10,11... | collective-permute-start | bytes 344072 | tf_op jit(solution)/shard_map/ppermute | solution.py:348
  44.1 6.9 %collective-permute-start.10 = (bf16[288,128]{1,0:T(8,128)(2,1)S(1)}, bf16[288,128]{1,0:T(8,128)(2,1)S(1)}, u32[]{:S(2)}, u32[]{:S(2)}) collective-permute-start(bf16[288,128]{1,0:T(8,128)(2,1)S(1)} %hop.7.far_ref), channel_id=1, source_target_pairs={{0,12},{2,14},{4,8},{6,10},{8,4},{10,6},{12,0},{14,2},{1,13},{3,15... | collective-permute-start | bytes 221192 | tf_op jit(solution)/shard_map/ppermute | solution.py:408
  46.3 17.0 %slice-start.1 = ((s8[8257536]{0:T(1024)(128)(4,1)}), s8[4063232]{0:T(1024)(128)(4,1)S(1)}, s32[]{:S(2)}) async-start(s8[8257536]{0:T(1024)(128)(4,1)} %bitcast.13), calls=%async_computation.3 | async-start | bytes 8126464
  61.9 1.4 %collective-permute-start.11 = (bf16[8,72,128]{2,1,0:T(8,128)(2,1)S(1)}, bf16[8,72,128]{2,1,0:T(8,128)(2,1)S(1)}, u32[]{:S(2)}, u32[]{:S(2)}) collective-permute-start(bf16[8,72,128]{2,1,0:T(8,128)(2,1)S(1)} %all_to_all.11.own_ref), channel_id=1, source_target_pairs={{0,1},{1,0},{2,3},{3,2},{4,5},{5,4},{6,7},{7,6},{8,9},{9,8},{10,11... | collective-permute-start | bytes 442376 | tf_op jit(solution)/shard_map/ppermute | solution.py:348

commit v9 on v8

--- a/solution.py
+++ b/solution.py
@@ -172,7 +172,8 @@
     )
     o_lat = (acc / total).astype(jnp.bfloat16)
     share = heads // n_dp
-    upper = appended.T[half:]
+    low = half // 128 * 128
+    upper = appended[:, low:].T[half - low :]
     cut = near_ref.shape[0] * 128 // width
     near_ref[...] = pack(upper[:cut]).astype(jnp.bfloat16)
     far_ref[...] = pack(upper[cut:]).astype(jnp.bfloat16)

time: 66.4 us -> 66.4 us (level)
  no operation moved by 1% of the time
where the time goes in v9:
time: 66.4 us; the launch traced here: 66.2 us
  blocking collectives  25.2 us (38%)
  Pallas kernels  20.4 us (31%)
  starting transfers between devices  14.1 us (21%)
  waiting for transfers between devices  4.55 us (7%)
  local copies, waits for them, and re-layouts  1.08 us (2%)
  between operations  0.89 us (1%)
    all_to_all x2, blocking collectives, exchange(): return lax.all_to_all(x, 'dp', split_axis=0, concat_axis=0, tiled=True)  25.2 us
    ppermute x9, starting transfers between devices, cross(): return lax.ppermute(x, 'dp', [(i, i ^ step) for i in range(n_dp)])  14 us
    pallas_call x1, Pallas kernels, per_device_fast(): pl.pallas_call(functools.partial(project_kernel, n_sub), out_shape=(jax.S...  6.76 us
    pallas_call x1, Pallas kernels, per_device_fast(): pl.pallas_call(functools.partial(gate_up_kernel, n_sub), out_shape=(jax.S...  4.69 us
    ppermute x9, waiting for transfers between devices, cross(): return lax.ppermute(x, 'dp', [(i, i ^ step) for i in range(n_dp)])  4.54 us
    pallas_call x1, Pallas kernels, per_device_fast(): pl.pallas_call(functools.partial(down_kernel, n_sub), out_shape=jax.Shape...  2.94 us
    pallas_call x4, Pallas kernels, hop(): pl.pallas_call(functools.partial(hop_kernel, n_sub, step), out_shape=jax....  2.35 us
    pallas_call x1, Pallas kernels, per_device_fast(): pl.pallas_call(functools.partial(attend_kernel, scale, n_dp, n_sub, laten...  1.64 us
  transfers between devices with their start and end apart: 12, of which 3 were waited for; matrix products, arithmetic and copies ran while one was open for 0% of the time, Pallas kernels for 23%

profile of v9, /device:TPU:0, one launch (start us, length us, event | category | flops | bytes accessed | tf_op | source)
XLA Modules:
  0.0 66.2 jit_solution(11742623176674384149)
XLA Ops:
  0.6 0.0 copy-start.6
  0.6 0.0 copy-start.7
  0.7 0.0 copy-start.2
  0.7 0.0 copy-start.5
  0.7 0.0 copy-start.3
  0.7 0.6 copy-done.6
  1.3 0.4 copy-done.2
  1.7 0.0 copy-done.3
  1.7 1.6 %attend.1 = (bf16[576,384]{1,0:T(8,128)(2,1)}, bf16[8,16,512]{2,1,0:T(8,128)(2,1)S(1)}, bf16[576,128]{1,0:T(8,128)(2,1)S(1)}, bf16[288,128]{1,0:T(8,128)(2,1)S(1)}) custom-call(s32[16]{0:T(128)S(1)} %copy-done.7, s32[2,3]{1,0:T(2,128)S(1)} %copy-done.6, s32[8,384]{1,0:T(8,128)S(1)} %positions.1.at_ref, bf16[576,128]{1,0:T(8,128)(2,1)S(1)} %bitcast.23, ...), custom_call_target="tpu_custom_call" | custom-call | flops 7549747200 | bytes 25165824 | tf_op jit(solution)/shard_map/attend/pallas_call | solution.py:381
  3.4 14.4 %all_to_all.10.got_ref = bf16[8,16,512]{2,1,0:T(8,128)(2,1)S(1)} all-to-all(bf16[8,16,512]{2,1,0:T(8,128)(2,1)S(1)} %get-tuple-element.29), channel_id=1, replica_groups=mesh['groups'=2,'dp'=8,'sub'=2] {'dp'}, dimensions={0} | all-to-all | bytes 262144 | tf_op jit(solution)/shard_map/all_to_all | solution.py:353
  17.8 0.5 values.1.own_ref
  18.2 0.0 slice-start.3
  18.2 0.0 slice-start.5
  18.3 0.0 copy-start.4
  18.3 0.1 collective-permute-start.2
  18.4 0.1 collective-permute-start.1
  18.4 1.8 %collective-permute-start = (bf16[576,128]{1,0:T(8,128)(2,1)S(1)}, bf16[576,128]{1,0:T(8,128)(2,1)S(1)}, u32[]{:S(2)}, u32[]{:S(2)}) collective-permute-start(bf16[576,128]{1,0:T(8,128)(2,1)S(1)} %get-tuple-element.32.kept_ref), channel_id=1, source_target_pairs={{0,12},{2,14},{4,8},{6,10},{8,4},{10,6},{12,0},{14,2},{1,13},{3,15... | collective-permute-start | bytes 442376 | tf_op jit(solution)/shard_map/ppermute | solution.py:409
  20.3 0.0 collective-permute-done.2.peer_ref
  20.3 6.8 %project.1 = (f32[16,3584]{1,0:T(8,128)S(1)}, bf16[16,3584]{1,0:T(8,128)(2,1)S(1)}) custom-call(bf16[8,2944]{1,0:T(8,128)(2,1)S(1)} %values.1.own_ref, bf16[8,2944]{1,0:T(8,128)(2,1)S(1)} %collective-permute-done.2.peer_ref, bf16[2048,7168]{1,0:T(8,128)(2,1)} %w_ref.1), custom_call_target="tpu_custom_call" | custom-call | flops 7549747200 | bytes 25165824 | tf_op jit(solution)/shard_map/project/pallas_call | solution.py:438
  27.0 0.0 collective-permute-done.1.come_ref
  27.0 0.0 collective-permute-done.come_ref
  27.1 0.5 collective-permute-start.4
  27.5 0.6 hop.4.kept_ref
  28.1 2.3 %collective-permute-start.3 = (bf16[576,128]{1,0:T(8,128)(2,1)S(1)}, bf16[576,128]{1,0:T(8,128)(2,1)S(1)}, u32[]{:S(2)}, u32[]{:S(2)}) collective-permute-start(bf16[576,128]{1,0:T(8,128)(2,1)S(1)} %hop.4.kept_ref), channel_id=1, source_target_pairs={{0,4},{2,6},{4,0},{6,2},{8,12},{10,14},{12,8},{14,10},{1,5},{3,7},... | collective-permute-start | bytes 442376 | tf_op jit(solution)/shard_map/ppermute | solution.py:409
  30.4 0.6 hop.6.kept_ref
  31.0 1.1 %collective-permute-done.4.peer_ref = bf16[16,3584]{1,0:T(8,128)(2,1)S(1)} collective-permute-done((bf16[16,3584]{1,0:T(8,128)(2,1)S(1)}, bf16[16,3584]{1,0:T(8,128)(2,1)S(1)}, u32[]{:S(2)}, u32[]{:S(2)}) %collective-permute-start.4) | collective-permute-done | bytes 114720 | tf_op jit(solution)/shard_map/ppermute | solution.py:409
  32.1 2.3 %collective-permute-start.5 = (bf16[16,3584]{1,0:T(8,128)(2,1)S(1)}, bf16[16,3584]{1,0:T(8,128)(2,1)S(1)}, u32[]{:S(2)}, u32[]{:S(2)}) collective-permute-start(bf16[16,3584]{1,0:T(8,128)(2,1)S(1)} %get-tuple-element.42), channel_id=1, source_target_pairs={{0,4},{2,6},{4,0},{6,2},{8,12},{10,14},{12,8},{14,10},{1,5},{3,7},... | collective-permute-start | bytes 344072 | tf_op jit(solution)/shard_map/ppermute | solution.py:409
  34.4 0.0 collective-permute-done.3.come_ref
  34.4 0.6 hop.5.near_ref
  35.0 2.1 %collective-permute-start.7 = (bf16[576,128]{1,0:T(8,128)(2,1)S(1)}, bf16[576,128]{1,0:T(8,128)(2,1)S(1)}, u32[]{:S(2)}, u32[]{:S(2)}) collective-permute-start(bf16[576,128]{1,0:T(8,128)(2,1)S(1)} %hop.5.near_ref), channel_id=1, source_target_pairs={{0,2},{2,0},{4,6},{6,4},{8,10},{10,8},{12,14},{14,12},{1,3},{3,1},... | collective-permute-start | bytes 442376 | tf_op jit(solution)/shard_map/ppermute | solution.py:409
  37.1 0.1 collective-permute-done.5.peer_ref
  37.2 1.8 %collective-permute-start.6 = (bf16[16,3584]{1,0:T(8,128)(2,1)S(1)}, bf16[16,3584]{1,0:T(8,128)(2,1)S(1)}, u32[]{:S(2)}, u32[]{:S(2)}) collective-permute-start(bf16[16,3584]{1,0:T(8,128)(2,1)S(1)} %get-tuple-element.43), channel_id=1, source_target_pairs={{0,12},{2,14},{4,8},{6,10},{8,4},{10,6},{12,0},{14,2},{1,13},{3,15... | collective-permute-start | bytes 344072 | tf_op jit(solution)/shard_map/ppermute | solution.py:409
  39.0 1.0 %collective-permute-start.8 = (bf16[288,128]{1,0:T(8,128)(2,1)S(1)}, bf16[288,128]{1,0:T(8,128)(2,1)S(1)}, u32[]{:S(2)}, u32[]{:S(2)}) collective-permute-start(bf16[288,128]{1,0:T(8,128)(2,1)S(1)} %hop.6.kept_ref), channel_id=1, source_target_pairs={{0,2},{2,0},{4,6},{6,4},{8,10},{10,8},{12,14},{14,12},{1,3},{3,1},... | collective-permute-start | bytes 221192 | tf_op jit(solution)/shard_map/ppermute | solution.py:409
  40.0 3.3 %collective-permute-done.8.come_ref = bf16[288,128]{1,0:T(8,128)(2,1)S(1)} collective-permute-done((bf16[288,128]{1,0:T(8,128)(2,1)S(1)}, bf16[288,128]{1,0:T(8,128)(2,1)S(1)}, u32[]{:S(2)}, u32[]{:S(2)}) %collective-permute-start.8) | collective-permute-done | bytes 73760 | tf_op jit(solution)/shard_map/ppermute | solution.py:409
  43.3 0.6 hop.7.far_ref
  43.9 0.0 collective-permute-done.7.near_come_ref
  43.9 0.0 collective-permute-done.6.peer_ref
  44.0 0.1 collective-permute-start.9
  44.1 2.2 %collective-permute-start.10 = (bf16[288,128]{1,0:T(8,128)(2,1)S(1)}, bf16[288,128]{1,0:T(8,128)(2,1)S(1)}, u32[]{:S(2)}, u32[]{:S(2)}) collective-permute-start(bf16[288,128]{1,0:T(8,128)(2,1)S(1)} %hop.7.far_ref), channel_id=1, source_target_pairs={{0,12},{2,14},{4,8},{6,10},{8,4},{10,6},{12,0},{14,2},{1,13},{3,15... | collective-permute-start | bytes 221192 | tf_op jit(solution)/shard_map/ppermute | solution.py:409
  46.2 0.0 collective-permute-done.9.peer_ref
  46.3 0.0 slice-start.1
  46.3 4.7 %gate_up.1 = (bf16[8,72,128]{2,1,0:T(8,128)(2,1)S(1)}, bf16[16,448]{1,0:T(8,128)(2,1)S(1)}) custom-call(bf16[16,3584]{1,0:T(8,128)(2,1)S(1)} %last_add.1.own_ref, bf16[16,3584]{1,0:T(8,128)(2,1)S(1)} %collective-permute-done.9.peer_ref, bf16[7168]{0:T(1024)(128)(2,1)S(1)} %copy-done.4, bf16[576,7168]{1,0:T(8,128)(2,1)S(1)} %bitcast.18, ...), custom_call_target="tpu_custom_call" | custom-call | flops 7549747200 | bytes 25165824 | tf_op jit(solution)/shard_map/gate_up/pallas_call | solution.py:476
  51.0 0.0 collective-permute-done.10.far_come_ref
  51.0 10.8 %all_to_all.11.own_ref = bf16[8,72,128]{2,1,0:T(8,128)(2,1)S(1)} all-to-all(bf16[8,72,128]{2,1,0:T(8,128)(2,1)S(1)} %get-tuple-element.51), channel_id=1, replica_groups=mesh['groups'=2,'dp'=8,'sub'=2] {'dp'}, dimensions={0} | all-to-all | bytes 294912 | tf_op jit(solution)/shard_map/all_to_all | solution.py:353
  61.9 0.0 collective-permute-start.11
  61.9 1.4 %finish.1 = bf16[192,576]{1,0:T(8,128)(2,1)} custom-call(s32[2,3]{1,0:T(2,128)S(1)} %copy-done.6, bf16[576,128]{1,0:T(8,128)(2,1)S(1)} %hop.5.near_ref, bf16[576,128]{1,0:T(8,128)(2,1)S(1)} %collective-permute-done.7.near_come_ref, bf16[288,128]{1,0:T(8,128)(2,1)S(1)} %hop.7.far_ref, bf16[288,128]{1,0:T(8,128)(2,1)S(1)} %collective-permute-done.10.far_come_ref), custom_call_target="tpu_custom_call" | custom-call | flops 314572800 | bytes 1048576 | tf_op jit(solution)/shard_map/finish/pallas_call | solution.py:501
  63.3 0.0 collective-permute-done.11.peer_ref
  63.3 2.9 %down.1 = bf16[16,448]{1,0:T(8,128)(2,1)} custom-call(bf16[8,72,128]{2,1,0:T(8,128)(2,1)S(1)} %all_to_all.11.own_ref, bf16[8,72,128]{2,1,0:T(8,128)(2,1)S(1)} %collective-permute-done.11.peer_ref, bf16[16,448]{1,0:T(8,128)(2,1)S(1)} %get-tuple-element.52.base_ref, bf16[448,9216]{1,0:T(8,128)(2,1)S(1)} %bitcast.15), custom_call_target="tpu_custom_call" | custom-call | flops 314572800 | bytes 1048576 | tf_op jit(solution)/shard_map/down/pallas_call | solution.py:491
  (23 shorter events, 0.1 us)
Async XLA Ops:
  0.6 0.7 %copy-start.6 = (s32[2,3]{1,0:T(2,128)S(1)}, s32[2,3]{1,0:T(2,128)}, u32[]{:S(2)}) copy-start(s32[2,3]{1,0:T(2,128)} %moves.11) | copy-start | bytes 76
  0.6 0.7 %copy-start.7 = (s32[16]{0:T(128)S(1)}, s32[16]{0:T(128)}, u32[]{:S(2)}) copy-start(s32[16]{0:T(128)} %lengths.1) | copy-start | bytes 196
  0.7 1.0 %copy-start.2 = (bf16[1,384,576]{1,2,0:T(8,128)(2,1)S(1)}, bf16[1,384,576]{1,2,0:T(8,128)(2,1)}, u32[]{:S(2)}) copy-start(bf16[1,384,576]{1,2,0:T(8,128)(2,1)} %param.14) | copy-start | bytes 1327108
  0.7 1.0 %copy-start.5 = (bf16[1,576]{1,0:T(2,128)(2,1)S(1)}, bf16[1,576]{1,0:T(2,128)(2,1)}, u32[]{:S(2)}) copy-start(bf16[1,576]{1,0:T(2,128)(2,1)} %fresh_ref.1) | copy-start | bytes 3460
  0.7 1.1 %copy-start.3 = (bf16[1,128,576]{1,2,0:T(8,128)(2,1)S(1)}, bf16[1,128,576]{1,2,0:T(8,128)(2,1)}, u32[]{:S(2)}) copy-start(bf16[1,128,576]{1,2,0:T(8,128)(2,1)} %param.12) | copy-start | bytes 442372
  1.7 16.0 %copy-start = (bf16[16,512,128]{2,1,0:T(8,128)(2,1)S(1)}, bf16[16,512,128]{2,1,0:T(8,128)(2,1)}, u32[]{:S(2)}) copy-start(bf16[16,512,128]{2,1,0:T(8,128)(2,1)} %uv_ref.1) | copy-start | bytes 6291460
  1.7 16.0 %copy-start.1 = (bf16[1,7168]{1,0:T(2,128)(2,1)S(1)}, bf16[1,7168]{1,0:T(2,128)(2,1)}, u32[]{:S(2)}) copy-start(bf16[1,7168]{1,0:T(2,128)(2,1)} %resid_ref.1) | copy-start | bytes 43012
  17.8 28.5 %slice-start.2 = ((s8[8257536]{0:T(1024)(128)(4,1)}), s8[4194304]{0:T(1024)(128)(4,1)S(1)}, s32[]{:S(2)}) async-start(s8[8257536]{0:T(1024)(128)(4,1)} %bitcast.16), calls=%async_computation.4 | async-start | bytes 8388608
  17.8 28.5 %slice-start.4 = ((s8[8257536]{0:T(1024)(128)(4,1)}), s8[4194304]{0:T(1024)(128)(4,1)S(1)}, s32[]{:S(2)}) async-start(s8[8257536]{0:T(1024)(128)(4,1)} %bitcast.19), calls=%async_computation.6 | async-start | bytes 8388608
  18.2 28.0 %slice-start.3 = ((s8[8257536]{0:T(1024)(128)(4,1)}), s8[4063232]{0:T(1024)(128)(4,1)S(1)}, s32[]{:S(2)}) async-start(s8[8257536]{0:T(1024)(128)(4,1)} %bitcast.16), calls=%async_computation.5 | async-start | bytes 8126464
  18.2 28.0 %slice-start.5 = ((s8[8257536]{0:T(1024)(128)(4,1)}), s8[4063232]{0:T(1024)(128)(4,1)S(1)}, s32[]{:S(2)}) async-start(s8[8257536]{0:T(1024)(128)(4,1)} %bitcast.19), calls=%async_computation.7 | async-start | bytes 8126464
  18.3 28.0 %copy-start.4 = (bf16[7168]{0:T(1024)(128)(2,1)S(1)}, bf16[7168]{0:T(1024)(128)(2,1)}, u32[]{:S(2)}) copy-start(bf16[7168]{0:T(1024)(128)(2,1)} %gain_ref.1) | copy-start | bytes 43012
  18.3 2.0 %collective-permute-start.2 = (bf16[8,2944]{1,0:T(8,128)(2,1)S(1)}, bf16[8,2944]{1,0:T(8,128)(2,1)S(1)}, u32[]{:S(2)}, u32[]{:S(2)}) collective-permute-start(bf16[8,2944]{1,0:T(8,128)(2,1)S(1)} %values.1.own_ref), channel_id=1, source_target_pairs={{0,1},{1,0},{2,3},{3,2},{4,5},{5,4},{6,7},{7,6},{8,9},{9,8},{10,11... | collective-permute-start | bytes 141320 | tf_op jit(solution)/shard_map/ppermute | solution.py:349
  18.4 8.7 %collective-permute-start.1 = (bf16[288,128]{1,0:T(8,128)(2,1)S(1)}, bf16[288,128]{1,0:T(8,128)(2,1)S(1)}, u32[]{:S(2)}, u32[]{:S(2)}) collective-permute-start(bf16[288,128]{1,0:T(8,128)(2,1)S(1)} %get-tuple-element.33.kept_ref), channel_id=1, source_target_pairs={{0,4},{2,6},{4,0},{6,2},{8,12},{10,14},{12,8},{14,10},{1,5},{3,7},... | collective-permute-start | bytes 221192 | tf_op jit(solution)/shard_map/ppermute | solution.py:409
  18.4 8.6 %collective-permute-start = (bf16[576,128]{1,0:T(8,128)(2,1)S(1)}, bf16[576,128]{1,0:T(8,128)(2,1)S(1)}, u32[]{:S(2)}, u32[]{:S(2)}) collective-permute-start(bf16[576,128]{1,0:T(8,128)(2,1)S(1)} %get-tuple-element.32.kept_ref), channel_id=1, source_target_pairs={{0,12},{2,14},{4,8},{6,10},{8,4},{10,6},{12,0},{14,2},{1,13},{3,15... | collective-permute-start | bytes 442376 | tf_op jit(solution)/shard_map/ppermute | solution.py:409
  27.1 5.0 %collective-permute-start.4 = (bf16[16,3584]{1,0:T(8,128)(2,1)S(1)}, bf16[16,3584]{1,0:T(8,128)(2,1)S(1)}, u32[]{:S(2)}, u32[]{:S(2)}) collective-permute-start(bf16[16,3584]{1,0:T(8,128)(2,1)S(1)} %get-tuple-element.38), channel_id=1, source_target_pairs={{0,2},{2,0},{4,6},{6,4},{8,10},{10,8},{12,14},{14,12},{1,3},{3,1},... | collective-permute-start | bytes 344072 | tf_op jit(solution)/shard_map/ppermute | solution.py:409
  28.1 6.3 %collective-permute-start.3 = (bf16[576,128]{1,0:T(8,128)(2,1)S(1)}, bf16[576,128]{1,0:T(8,128)(2,1)S(1)}, u32[]{:S(2)}, u32[]{:S(2)}) collective-permute-start(bf16[576,128]{1,0:T(8,128)(2,1)S(1)} %hop.4.kept_ref), channel_id=1, source_target_pairs={{0,4},{2,6},{4,0},{6,2},{8,12},{10,14},{12,8},{14,10},{1,5},{3,7},... | collective-permute-start | bytes 442376 | tf_op jit(solution)/shard_map/ppermute | solution.py:409
  32.1 5.1 %collective-permute-start.5 = (bf16[16,3584]{1,0:T(8,128)(2,1)S(1)}, bf16[16,3584]{1,0:T(8,128)(2,1)S(1)}, u32[]{:S(2)}, u32[]{:S(2)}) collective-permute-start(bf16[16,3584]{1,0:T(8,128)(2,1)S(1)} %get-tuple-element.42), channel_id=1, source_target_pairs={{0,4},{2,6},{4,0},{6,2},{8,12},{10,14},{12,8},{14,10},{1,5},{3,7},... | collective-permute-start | bytes 344072 | tf_op jit(solution)/shard_map/ppermute | solution.py:409
  35.0 8.9 %collective-permute-start.7 = (bf16[576,128]{1,0:T(8,128)(2,1)S(1)}, bf16[576,128]{1,0:T(8,128)(2,1)S(1)}, u32[]{:S(2)}, u32[]{:S(2)}) collective-permute-start(bf16[576,128]{1,0:T(8,128)(2,1)S(1)} %hop.5.near_ref), channel_id=1, source_target_pairs={{0,2},{2,0},{4,6},{6,4},{8,10},{10,8},{12,14},{14,12},{1,3},{3,1},... | collective-permute-start | bytes 442376 | tf_op jit(solution)/shard_map/ppermute | solution.py:409
  37.2 6.8 %collective-permute-start.6 = (bf16[16,3584]{1,0:T(8,128)(2,1)S(1)}, bf16[16,3584]{1,0:T(8,128)(2,1)S(1)}, u32[]{:S(2)}, u32[]{:S(2)}) collective-permute-start(bf16[16,3584]{1,0:T(8,128)(2,1)S(1)} %get-tuple-element.43), channel_id=1, source_target_pairs={{0,12},{2,14},{4,8},{6,10},{8,4},{10,6},{12,0},{14,2},{1,13},{3,15... | collective-permute-start | bytes 344072 | tf_op jit(solution)/shard_map/ppermute | solution.py:409
  39.0 4.4 %collective-permute-start.8 = (bf16[288,128]{1,0:T(8,128)(2,1)S(1)}, bf16[288,128]{1,0:T(8,128)(2,1)S(1)}, u32[]{:S(2)}, u32[]{:S(2)}) collective-permute-start(bf16[288,128]{1,0:T(8,128)(2,1)S(1)} %hop.6.kept_ref), channel_id=1, source_target_pairs={{0,2},{2,0},{4,6},{6,4},{8,10},{10,8},{12,14},{14,12},{1,3},{3,1},... | collective-permute-start | bytes 221192 | tf_op jit(solution)/shard_map/ppermute | solution.py:409
  43.3 19.9 %slice-start = ((s8[8257536]{0:T(1024)(128)(4,1)}), s8[4194304]{0:T(1024)(128)(4,1)S(1)}, s32[]{:S(2)}) async-start(s8[8257536]{0:T(1024)(128)(4,1)} %bitcast.13), calls=%async_computation.2 | async-start | bytes 8388608
  44.0 2.2 %collective-permute-start.9 = (bf16[16,3584]{1,0:T(8,128)(2,1)S(1)}, bf16[16,3584]{1,0:T(8,128)(2,1)S(1)}, u32[]{:S(2)}, u32[]{:S(2)}) collective-permute-start(bf16[16,3584]{1,0:T(8,128)(2,1)S(1)} %last_add.1.own_ref), channel_id=1, source_target_pairs={{0,1},{1,0},{2,3},{3,2},{4,5},{5,4},{6,7},{7,6},{8,9},{9,8},{10,11... | collective-permute-start | bytes 344072 | tf_op jit(solution)/shard_map/ppermute | solution.py:349
  44.1 6.9 %collective-permute-start.10 = (bf16[288,128]{1,0:T(8,128)(2,1)S(1)}, bf16[288,128]{1,0:T(8,128)(2,1)S(1)}, u32[]{:S(2)}, u32[]{:S(2)}) collective-permute-start(bf16[288,128]{1,0:T(8,128)(2,1)S(1)} %hop.7.far_ref), channel_id=1, source_target_pairs={{0,12},{2,14},{4,8},{6,10},{8,4},{10,6},{12,0},{14,2},{1,13},{3,15... | collective-permute-start | bytes 221192 | tf_op jit(solution)/shard_map/ppermute | solution.py:409
  46.3 17.0 %slice-start.1 = ((s8[8257536]{0:T(1024)(128)(4,1)}), s8[4063232]{0:T(1024)(128)(4,1)S(1)}, s32[]{:S(2)}) async-start(s8[8257536]{0:T(1024)(128)(4,1)} %bitcast.13), calls=%async_computation.3 | async-start | bytes 8126464
  61.9 1.4 %collective-permute-start.11 = (bf16[8,72,128]{2,1,0:T(8,128)(2,1)S(1)}, bf16[8,72,128]{2,1,0:T(8,128)(2,1)S(1)}, u32[]{:S(2)}, u32[]{:S(2)}) collective-permute-start(bf16[8,72,128]{2,1,0:T(8,128)(2,1)S(1)} %all_to_all.11.own_ref), channel_id=1, source_target_pairs={{0,1},{1,0},{2,3},{3,2},{4,5},{5,4},{6,7},{7,6},{8,9},{9,8},{10,11... | collective-permute-start | bytes 442376 | tf_op jit(solution)/shard_map/ppermute | solution.py:349
